TPU v7x, 256 devices: a whole 4x4x8 slice. The times are simulated.
256 devices in a mesh: dom: 16 (over z, core), orb: 16 (over y, x).
Axes of the slice: x: 4, y: 4, z: 8, core: 2. Of those that a mesh axis runs over, the one named last changes fastest.
Arguments:
- green_blocks: bfloat16 [16, 2048, 2048], P('dom', 'orb'), may hold values from -2 to 2
- couplings: bfloat16 [16, 2048, 2048], P('dom', 'orb'), may hold values from -0.125 to 0.125
- pattern: int32 [16, 32, 32], P('dom', 'orb'), may hold values 0 or 1
- sources: bfloat16 [16, 64, 2048], P('dom', None, 'orb'), may hold values from -6 to 6
- injected: bfloat16 [64, 2048], replicated, may hold values from -6 to 6
Outputs:
- states: bfloat16 [16, 64, 2048], P('dom', None, 'orb')
All inputs are finite; a program needn't handle non-finite values. No bound on the sum of `pattern` on one device may be relied on, other than what follows from the above.
Results may differ from a plain program's by a relative error of at most 0.025.
Values may be sent and summed in bfloat16 or wider, within the bound.
No kernel may reach another device: no remote copies, remote signals or barrier semaphores. Data moves between devices by JAX's collectives and lax.ppermute only.
A program may use at most 64 MiB of HBM per device.

v0:
```python
import jax
import jax.numpy as jnp
from jax import lax
from jax.sharding import PartitionSpec as P

BLOCK = 64


def passed_along(value, axis, steps):
    count = lax.axis_size(axis)
    initial, last = (max(0, -steps), min(count, count - steps))
    return lax.ppermute(value, axis, [(source, source + steps) for source in range(initial, last)])


def on_device(green_blocks, couplings, pattern, sources, injected):
    green_rows = green_blocks[0]
    block_mask = pattern[0]
    expanded = jnp.repeat(jnp.repeat(block_mask, BLOCK, axis=0), BLOCK, axis=1).astype(jnp.bfloat16)
    masked = couplings[0] * expanded
    row_count = green_rows.shape[0]
    transfer = jnp.dot(
        green_rows,
        lax.all_gather(masked, "orb", axis=0, tiled=True),
        preferred_element_type=jnp.float32,
    ).astype(jnp.bfloat16)
    source = sources[0].astype(jnp.float32)
    chain_turns = lax.axis_size("dom")
    is_first = lax.axis_index("dom") == 0
    contract = (((1,), (1,)), ((), ()))
    start_state = jnp.zeros((injected.shape[0], row_count), jnp.bfloat16)

    def advance(step, loop_state):
        incoming = loop_state[0]
        product = lax.dot_general(incoming, transfer, contract, preferred_element_type=jnp.float32)
        current = (source - product).astype(jnp.bfloat16)
        gathered = lax.all_gather(current, "orb", axis=1, tiled=True)
        passed = passed_along(gathered, "dom", 1)
        return (jnp.where(is_first, injected, passed), current)

    _, current = lax.fori_loop(0, chain_turns, advance, (injected, start_state))
    return current[None]


def solution(mesh):
    return jax.shard_map(
        on_device,
        mesh=mesh,
        in_specs=(
            P("dom", "orb", None),
            P("dom", "orb", None),
            P("dom", "orb", None),
            P("dom", None, "orb"),
            P(),
        ),
        out_specs=P("dom", None, "orb"),
        check_vma=False,
    )
```

profile of v0, /device:TPU:128, one launch (start us, length us, event | category | flops | bytes accessed | tf_op | source)
XLA Modules:
  0.0 616.4 jit_solution(552985734197300553)
XLA Ops:
  6.5 1.4 copy.7
  7.9 0.7 convert_bitcast_fusion
  9.0 0.9 bitcast_multiply_fusion
  9.9 1.0 copy.11
  10.8 0.7 bitcast_convert_fusion
  11.5 83.3 %all-gather.2.cloned.1.call-done = bf16[2048,2048]{0,1:T(8,128)(2,1)} async-done(((bf16[128,2048]{0,1:T(8,128)(2,1)}), bf16[2048,2048]{0,1:T(8,128)(2,1)}) %all-gather.2.cloned.1.call-update) | async-done | bytes 8388624 | tf_op jit(solution)/shard_map/all_gather | solution.py:23
  94.9 5.7 fusion.1
  100.9 508.7 %while.12 = (s32[]{:T(128)}, bf16[64,2048]{1,0:T(8,128)(2,1)S(1)}, bf16[64,128]{1,0:T(8,128)(2,1)}, pred[]{:T(512)}, bf16[128,2048]{1,0:T(8,128)(2,1)S(1)}, /*in...) while((s32[]{:T(128)}, bf16[64,2048]{1,0:T(8,128)(2,1)S(1)}, bf16[64,128]{1,0:T(8,128)(2,1)}, ...), condition=%wide.region_1.2_spmd, body=%wide.region_0.1_spmd.sunk | while | flops 33701888 | bytes 3014810 | solution.py:40
  100.9 0.3 fusion.11
  101.2 23.3 %all_gather.8 = bf16[64,2048]{1,0:T(8,128)(2,1)S(1)} all-gather(bf16[64,128]{1,0:T(8,128)(2,1)S(1)} %fusion.11), channel_id=1, replica_groups=mesh['dom'=16,'orb'=16] {'orb'}, dimensions={1}, use_global_device_ids=true | all-gather | bytes 278528 | tf_op jit(solution)/shard_map/while/body/eval_jaxpr/all_gather | solution.py:36
  124.5 1.9 collective-permute-start
  126.4 7.0 %collective-permute-done = bf16[64,2048]{1,0:T(8,128)(2,1)S(1)} collective-permute-done((bf16[64,2048]{1,0:T(8,128)(2,1)S(1)}, bf16[64,2048]{1,0:T(8,128)(2,1)S(1)}, u32[]{:S(2)}, u32[]{:S(2)}) %collective-permute-start) | collective-permute-done | bytes 262176 | tf_op jit(solution)/shard_map/while/body/eval_jaxpr/ppermute | solution.py:12
  133.4 0.3 fusion.11
  133.8 21.8 %all_gather.8 = bf16[64,2048]{1,0:T(8,128)(2,1)S(1)} all-gather(bf16[64,128]{1,0:T(8,128)(2,1)S(1)} %fusion.11), channel_id=1, replica_groups=mesh['dom'=16,'orb'=16] {'orb'}, dimensions={1}, use_global_device_ids=true | all-gather | bytes 278528 | tf_op jit(solution)/shard_map/while/body/eval_jaxpr/all_gather | solution.py:36
  155.6 1.9 collective-permute-start
  157.5 7.0 %collective-permute-done = bf16[64,2048]{1,0:T(8,128)(2,1)S(1)} collective-permute-done((bf16[64,2048]{1,0:T(8,128)(2,1)S(1)}, bf16[64,2048]{1,0:T(8,128)(2,1)S(1)}, u32[]{:S(2)}, u32[]{:S(2)}) %collective-permute-start) | collective-permute-done | bytes 262176 | tf_op jit(solution)/shard_map/while/body/eval_jaxpr/ppermute | solution.py:12
  164.5 0.3 fusion.11
  164.8 23.3 %all_gather.8 = bf16[64,2048]{1,0:T(8,128)(2,1)S(1)} all-gather(bf16[64,128]{1,0:T(8,128)(2,1)S(1)} %fusion.11), channel_id=1, replica_groups=mesh['dom'=16,'orb'=16] {'orb'}, dimensions={1}, use_global_device_ids=true | all-gather | bytes 278528 | tf_op jit(solution)/shard_map/while/body/eval_jaxpr/all_gather | solution.py:36
  188.1 1.9 collective-permute-start
  190.0 7.0 %collective-permute-done = bf16[64,2048]{1,0:T(8,128)(2,1)S(1)} collective-permute-done((bf16[64,2048]{1,0:T(8,128)(2,1)S(1)}, bf16[64,2048]{1,0:T(8,128)(2,1)S(1)}, u32[]{:S(2)}, u32[]{:S(2)}) %collective-permute-start) | collective-permute-done | bytes 262176 | tf_op jit(solution)/shard_map/while/body/eval_jaxpr/ppermute | solution.py:12
  197.1 0.3 fusion.11
  197.4 21.8 %all_gather.8 = bf16[64,2048]{1,0:T(8,128)(2,1)S(1)} all-gather(bf16[64,128]{1,0:T(8,128)(2,1)S(1)} %fusion.11), channel_id=1, replica_groups=mesh['dom'=16,'orb'=16] {'orb'}, dimensions={1}, use_global_device_ids=true | all-gather | bytes 278528 | tf_op jit(solution)/shard_map/while/body/eval_jaxpr/all_gather | solution.py:36
  219.1 1.9 collective-permute-start
  221.1 7.0 %collective-permute-done = bf16[64,2048]{1,0:T(8,128)(2,1)S(1)} collective-permute-done((bf16[64,2048]{1,0:T(8,128)(2,1)S(1)}, bf16[64,2048]{1,0:T(8,128)(2,1)S(1)}, u32[]{:S(2)}, u32[]{:S(2)}) %collective-permute-start) | collective-permute-done | bytes 262176 | tf_op jit(solution)/shard_map/while/body/eval_jaxpr/ppermute | solution.py:12
  228.1 0.3 fusion.11
  228.4 23.3 %all_gather.8 = bf16[64,2048]{1,0:T(8,128)(2,1)S(1)} all-gather(bf16[64,128]{1,0:T(8,128)(2,1)S(1)} %fusion.11), channel_id=1, replica_groups=mesh['dom'=16,'orb'=16] {'orb'}, dimensions={1}, use_global_device_ids=true | all-gather | bytes 278528 | tf_op jit(solution)/shard_map/while/body/eval_jaxpr/all_gather | solution.py:36
  251.7 1.9 collective-permute-start
  253.6 7.0 %collective-permute-done = bf16[64,2048]{1,0:T(8,128)(2,1)S(1)} collective-permute-done((bf16[64,2048]{1,0:T(8,128)(2,1)S(1)}, bf16[64,2048]{1,0:T(8,128)(2,1)S(1)}, u32[]{:S(2)}, u32[]{:S(2)}) %collective-permute-start) | collective-permute-done | bytes 262176 | tf_op jit(solution)/shard_map/while/body/eval_jaxpr/ppermute | solution.py:12
  260.6 0.3 fusion.11
  261.0 21.8 %all_gather.8 = bf16[64,2048]{1,0:T(8,128)(2,1)S(1)} all-gather(bf16[64,128]{1,0:T(8,128)(2,1)S(1)} %fusion.11), channel_id=1, replica_groups=mesh['dom'=16,'orb'=16] {'orb'}, dimensions={1}, use_global_device_ids=true | all-gather | bytes 278528 | tf_op jit(solution)/shard_map/while/body/eval_jaxpr/all_gather | solution.py:36
  282.7 1.9 collective-permute-start
  284.6 7.0 %collective-permute-done = bf16[64,2048]{1,0:T(8,128)(2,1)S(1)} collective-permute-done((bf16[64,2048]{1,0:T(8,128)(2,1)S(1)}, bf16[64,2048]{1,0:T(8,128)(2,1)S(1)}, u32[]{:S(2)}, u32[]{:S(2)}) %collective-permute-start) | collective-permute-done | bytes 262176 | tf_op jit(solution)/shard_map/while/body/eval_jaxpr/ppermute | solution.py:12
  291.7 0.3 fusion.11
  292.0 23.3 %all_gather.8 = bf16[64,2048]{1,0:T(8,128)(2,1)S(1)} all-gather(bf16[64,128]{1,0:T(8,128)(2,1)S(1)} %fusion.11), channel_id=1, replica_groups=mesh['dom'=16,'orb'=16] {'orb'}, dimensions={1}, use_global_device_ids=true | all-gather | bytes 278528 | tf_op jit(solution)/shard_map/while/body/eval_jaxpr/all_gather | solution.py:36
  315.3 1.9 collective-permute-start
  317.2 7.0 %collective-permute-done = bf16[64,2048]{1,0:T(8,128)(2,1)S(1)} collective-permute-done((bf16[64,2048]{1,0:T(8,128)(2,1)S(1)}, bf16[64,2048]{1,0:T(8,128)(2,1)S(1)}, u32[]{:S(2)}, u32[]{:S(2)}) %collective-permute-start) | collective-permute-done | bytes 262176 | tf_op jit(solution)/shard_map/while/body/eval_jaxpr/ppermute | solution.py:12
  324.2 0.3 fusion.11
  324.5 21.8 %all_gather.8 = bf16[64,2048]{1,0:T(8,128)(2,1)S(1)} all-gather(bf16[64,128]{1,0:T(8,128)(2,1)S(1)} %fusion.11), channel_id=1, replica_groups=mesh['dom'=16,'orb'=16] {'orb'}, dimensions={1}, use_global_device_ids=true | all-gather | bytes 278528 | tf_op jit(solution)/shard_map/while/body/eval_jaxpr/all_gather | solution.py:36
  346.3 1.9 collective-permute-start
  348.2 7.0 %collective-permute-done = bf16[64,2048]{1,0:T(8,128)(2,1)S(1)} collective-permute-done((bf16[64,2048]{1,0:T(8,128)(2,1)S(1)}, bf16[64,2048]{1,0:T(8,128)(2,1)S(1)}, u32[]{:S(2)}, u32[]{:S(2)}) %collective-permute-start) | collective-permute-done | bytes 262176 | tf_op jit(solution)/shard_map/while/body/eval_jaxpr/ppermute | solution.py:12
  355.6 23.3 %all_gather.8 = bf16[64,2048]{1,0:T(8,128)(2,1)S(1)} all-gather(bf16[64,128]{1,0:T(8,128)(2,1)S(1)} %fusion.11), channel_id=1, replica_groups=mesh['dom'=16,'orb'=16] {'orb'}, dimensions={1}, use_global_device_ids=true | all-gather | bytes 278528 | tf_op jit(solution)/shard_map/while/body/eval_jaxpr/all_gather | solution.py:36
  378.8 1.9 collective-permute-start
  380.8 7.0 %collective-permute-done = bf16[64,2048]{1,0:T(8,128)(2,1)S(1)} collective-permute-done((bf16[64,2048]{1,0:T(8,128)(2,1)S(1)}, bf16[64,2048]{1,0:T(8,128)(2,1)S(1)}, u32[]{:S(2)}, u32[]{:S(2)}) %collective-permute-start) | collective-permute-done | bytes 262176 | tf_op jit(solution)/shard_map/while/body/eval_jaxpr/ppermute | solution.py:12
  388.1 21.8 %all_gather.8 = bf16[64,2048]{1,0:T(8,128)(2,1)S(1)} all-gather(bf16[64,128]{1,0:T(8,128)(2,1)S(1)} %fusion.11), channel_id=1, replica_groups=mesh['dom'=16,'orb'=16] {'orb'}, dimensions={1}, use_global_device_ids=true | all-gather | bytes 278528 | tf_op jit(solution)/shard_map/while/body/eval_jaxpr/all_gather | solution.py:36
  409.9 1.9 collective-permute-start
  411.8 7.0 %collective-permute-done = bf16[64,2048]{1,0:T(8,128)(2,1)S(1)} collective-permute-done((bf16[64,2048]{1,0:T(8,128)(2,1)S(1)}, bf16[64,2048]{1,0:T(8,128)(2,1)S(1)}, u32[]{:S(2)}, u32[]{:S(2)}) %collective-permute-start) | collective-permute-done | bytes 262176 | tf_op jit(solution)/shard_map/while/body/eval_jaxpr/ppermute | solution.py:12
  419.2 23.3 %all_gather.8 = bf16[64,2048]{1,0:T(8,128)(2,1)S(1)} all-gather(bf16[64,128]{1,0:T(8,128)(2,1)S(1)} %fusion.11), channel_id=1, replica_groups=mesh['dom'=16,'orb'=16] {'orb'}, dimensions={1}, use_global_device_ids=true | all-gather | bytes 278528 | tf_op jit(solution)/shard_map/while/body/eval_jaxpr/all_gather | solution.py:36
  442.4 1.9 collective-permute-start
  444.3 7.0 %collective-permute-done = bf16[64,2048]{1,0:T(8,128)(2,1)S(1)} collective-permute-done((bf16[64,2048]{1,0:T(8,128)(2,1)S(1)}, bf16[64,2048]{1,0:T(8,128)(2,1)S(1)}, u32[]{:S(2)}, u32[]{:S(2)}) %collective-permute-start) | collective-permute-done | bytes 262176 | tf_op jit(solution)/shard_map/while/body/eval_jaxpr/ppermute | solution.py:12
  451.7 21.8 %all_gather.8 = bf16[64,2048]{1,0:T(8,128)(2,1)S(1)} all-gather(bf16[64,128]{1,0:T(8,128)(2,1)S(1)} %fusion.11), channel_id=1, replica_groups=mesh['dom'=16,'orb'=16] {'orb'}, dimensions={1}, use_global_device_ids=true | all-gather | bytes 278528 | tf_op jit(solution)/shard_map/while/body/eval_jaxpr/all_gather | solution.py:36
  473.5 1.9 collective-permute-start
  475.4 7.0 %collective-permute-done = bf16[64,2048]{1,0:T(8,128)(2,1)S(1)} collective-permute-done((bf16[64,2048]{1,0:T(8,128)(2,1)S(1)}, bf16[64,2048]{1,0:T(8,128)(2,1)S(1)}, u32[]{:S(2)}, u32[]{:S(2)}) %collective-permute-start) | collective-permute-done | bytes 262176 | tf_op jit(solution)/shard_map/while/body/eval_jaxpr/ppermute | solution.py:12
  482.7 23.3 %all_gather.8 = bf16[64,2048]{1,0:T(8,128)(2,1)S(1)} all-gather(bf16[64,128]{1,0:T(8,128)(2,1)S(1)} %fusion.11), channel_id=1, replica_groups=mesh['dom'=16,'orb'=16] {'orb'}, dimensions={1}, use_global_device_ids=true | all-gather | bytes 278528 | tf_op jit(solution)/shard_map/while/body/eval_jaxpr/all_gather | solution.py:36
  506.0 1.9 collective-permute-start
  507.9 7.0 %collective-permute-done = bf16[64,2048]{1,0:T(8,128)(2,1)S(1)} collective-permute-done((bf16[64,2048]{1,0:T(8,128)(2,1)S(1)}, bf16[64,2048]{1,0:T(8,128)(2,1)S(1)}, u32[]{:S(2)}, u32[]{:S(2)}) %collective-permute-start) | collective-permute-done | bytes 262176 | tf_op jit(solution)/shard_map/while/body/eval_jaxpr/ppermute | solution.py:12
  515.3 21.8 %all_gather.8 = bf16[64,2048]{1,0:T(8,128)(2,1)S(1)} all-gather(bf16[64,128]{1,0:T(8,128)(2,1)S(1)} %fusion.11), channel_id=1, replica_groups=mesh['dom'=16,'orb'=16] {'orb'}, dimensions={1}, use_global_device_ids=true | all-gather | bytes 278528 | tf_op jit(solution)/shard_map/while/body/eval_jaxpr/all_gather | solution.py:36
  537.0 1.9 collective-permute-start
  539.0 7.0 %collective-permute-done = bf16[64,2048]{1,0:T(8,128)(2,1)S(1)} collective-permute-done((bf16[64,2048]{1,0:T(8,128)(2,1)S(1)}, bf16[64,2048]{1,0:T(8,128)(2,1)S(1)}, u32[]{:S(2)}, u32[]{:S(2)}) %collective-permute-start) | collective-permute-done | bytes 262176 | tf_op jit(solution)/shard_map/while/body/eval_jaxpr/ppermute | solution.py:12
  546.3 23.3 %all_gather.8 = bf16[64,2048]{1,0:T(8,128)(2,1)S(1)} all-gather(bf16[64,128]{1,0:T(8,128)(2,1)S(1)} %fusion.11), channel_id=1, replica_groups=mesh['dom'=16,'orb'=16] {'orb'}, dimensions={1}, use_global_device_ids=true | all-gather | bytes 278528 | tf_op jit(solution)/shard_map/while/body/eval_jaxpr/all_gather | solution.py:36
  569.6 1.9 collective-permute-start
  571.5 7.0 %collective-permute-done = bf16[64,2048]{1,0:T(8,128)(2,1)S(1)} collective-permute-done((bf16[64,2048]{1,0:T(8,128)(2,1)S(1)}, bf16[64,2048]{1,0:T(8,128)(2,1)S(1)}, u32[]{:S(2)}, u32[]{:S(2)}) %collective-permute-start) | collective-permute-done | bytes 262176 | tf_op jit(solution)/shard_map/while/body/eval_jaxpr/ppermute | solution.py:12
  578.8 21.8 %all_gather.8 = bf16[64,2048]{1,0:T(8,128)(2,1)S(1)} all-gather(bf16[64,128]{1,0:T(8,128)(2,1)S(1)} %fusion.11), channel_id=1, replica_groups=mesh['dom'=16,'orb'=16] {'orb'}, dimensions={1}, use_global_device_ids=true | all-gather | bytes 278528 | tf_op jit(solution)/shard_map/while/body/eval_jaxpr/all_gather | solution.py:36
  600.6 1.9 collective-permute-start
  602.5 7.0 %collective-permute-done = bf16[64,2048]{1,0:T(8,128)(2,1)S(1)} collective-permute-done((bf16[64,2048]{1,0:T(8,128)(2,1)S(1)}, bf16[64,2048]{1,0:T(8,128)(2,1)S(1)}, u32[]{:S(2)}, u32[]{:S(2)}) %collective-permute-start) | collective-permute-done | bytes 262176 | tf_op jit(solution)/shard_map/while/body/eval_jaxpr/ppermute | solution.py:12
  (67 shorter events, 3.5 us)
Async XLA Ops:
  6.5 88.4 %copy-start = (bf16[1,128,2048]{2,1,0:T(8,128)(2,1)S(1)}, bf16[1,128,2048]{2,1,0:T(8,128)(2,1)}, u32[]{:S(2)}) copy-start(bf16[1,128,2048]{2,1,0:T(8,128)(2,1)} %param.7) | copy-start | bytes 1572868
  6.5 88.4 %all-gather.2.cloned.1.call-start = ((), (), s32[]{:S(2)}) async-start(), calls=%async_computation | async-start | bytes 8912896 | tf_op jit(solution)/shard_map/all_gather | solution.py:23
  7.9 92.9 %copy-start.1 = (bf16[64,2048]{1,0:T(8,128)(2,1)S(1)}, bf16[64,2048]{1,0:T(8,128)(2,1)}, u32[]{:S(2)}) copy-start(bf16[64,2048]{1,0:T(8,128)(2,1)} %param.11) | copy-start | bytes 786436
  101.2 32.2 %copy-start.2 = (bf16[64,128]{1,0:T(8,128)(2,1)}, bf16[64,128]{1,0:T(8,128)(2,1)S(1)}, u32[]{:S(2)}) copy-start(bf16[64,128]{1,0:T(8,128)(2,1)S(1)} %fusion.11) | copy-start | bytes 49156 | tf_op jit(solution)/shard_map/while
  124.5 8.9 %collective-permute-start = (bf16[64,2048]{1,0:T(8,128)(2,1)S(1)}, bf16[64,2048]{1,0:T(8,128)(2,1)S(1)}, u32[]{:S(2)}, u32[]{:S(2)}) collective-permute-start(bf16[64,2048]{1,0:T(8,128)(2,1)S(1)} %all_gather.8), channel_id=1, source_target_pairs={{0,16},{16,32},{32,48},{48,64},{64,80},{80,96},{96,112},{112,128},... | collective-permute-start | bytes 786440 | tf_op jit(solution)/shard_map/while/body/eval_jaxpr/ppermute | solution.py:12
  133.7 30.8 %copy-start.2 = (bf16[64,128]{1,0:T(8,128)(2,1)}, bf16[64,128]{1,0:T(8,128)(2,1)S(1)}, u32[]{:S(2)}) copy-start(bf16[64,128]{1,0:T(8,128)(2,1)S(1)} %fusion.11) | copy-start | bytes 49156 | tf_op jit(solution)/shard_map/while
  155.6 8.9 %collective-permute-start = (bf16[64,2048]{1,0:T(8,128)(2,1)S(1)}, bf16[64,2048]{1,0:T(8,128)(2,1)S(1)}, u32[]{:S(2)}, u32[]{:S(2)}) collective-permute-start(bf16[64,2048]{1,0:T(8,128)(2,1)S(1)} %all_gather.8), channel_id=1, source_target_pairs={{0,16},{16,32},{32,48},{48,64},{64,80},{80,96},{96,112},{112,128},... | collective-permute-start | bytes 786440 | tf_op jit(solution)/shard_map/while/body/eval_jaxpr/ppermute | solution.py:12
  164.8 32.2 %copy-start.2 = (bf16[64,128]{1,0:T(8,128)(2,1)}, bf16[64,128]{1,0:T(8,128)(2,1)S(1)}, u32[]{:S(2)}) copy-start(bf16[64,128]{1,0:T(8,128)(2,1)S(1)} %fusion.11) | copy-start | bytes 49156 | tf_op jit(solution)/shard_map/while
  188.1 8.9 %collective-permute-start = (bf16[64,2048]{1,0:T(8,128)(2,1)S(1)}, bf16[64,2048]{1,0:T(8,128)(2,1)S(1)}, u32[]{:S(2)}, u32[]{:S(2)}) collective-permute-start(bf16[64,2048]{1,0:T(8,128)(2,1)S(1)} %all_gather.8), channel_id=1, source_target_pairs={{0,16},{16,32},{32,48},{48,64},{64,80},{80,96},{96,112},{112,128},... | collective-permute-start | bytes 786440 | tf_op jit(solution)/shard_map/while/body/eval_jaxpr/ppermute | solution.py:12
  197.4 30.7 %copy-start.2 = (bf16[64,128]{1,0:T(8,128)(2,1)}, bf16[64,128]{1,0:T(8,128)(2,1)S(1)}, u32[]{:S(2)}) copy-start(bf16[64,128]{1,0:T(8,128)(2,1)S(1)} %fusion.11) | copy-start | bytes 49156 | tf_op jit(solution)/shard_map/while
  219.1 8.9 %collective-permute-start = (bf16[64,2048]{1,0:T(8,128)(2,1)S(1)}, bf16[64,2048]{1,0:T(8,128)(2,1)S(1)}, u32[]{:S(2)}, u32[]{:S(2)}) collective-permute-start(bf16[64,2048]{1,0:T(8,128)(2,1)S(1)} %all_gather.8), channel_id=1, source_target_pairs={{0,16},{16,32},{32,48},{48,64},{64,80},{80,96},{96,112},{112,128},... | collective-permute-start | bytes 786440 | tf_op jit(solution)/shard_map/while/body/eval_jaxpr/ppermute | solution.py:12
  228.4 32.2 %copy-start.2 = (bf16[64,128]{1,0:T(8,128)(2,1)}, bf16[64,128]{1,0:T(8,128)(2,1)S(1)}, u32[]{:S(2)}) copy-start(bf16[64,128]{1,0:T(8,128)(2,1)S(1)} %fusion.11) | copy-start | bytes 49156 | tf_op jit(solution)/shard_map/while
  251.7 8.9 %collective-permute-start = (bf16[64,2048]{1,0:T(8,128)(2,1)S(1)}, bf16[64,2048]{1,0:T(8,128)(2,1)S(1)}, u32[]{:S(2)}, u32[]{:S(2)}) collective-permute-start(bf16[64,2048]{1,0:T(8,128)(2,1)S(1)} %all_gather.8), channel_id=1, source_target_pairs={{0,16},{16,32},{32,48},{48,64},{64,80},{80,96},{96,112},{112,128},... | collective-permute-start | bytes 786440 | tf_op jit(solution)/shard_map/while/body/eval_jaxpr/ppermute | solution.py:12
  260.9 30.7 %copy-start.2 = (bf16[64,128]{1,0:T(8,128)(2,1)}, bf16[64,128]{1,0:T(8,128)(2,1)S(1)}, u32[]{:S(2)}) copy-start(bf16[64,128]{1,0:T(8,128)(2,1)S(1)} %fusion.11) | copy-start | bytes 49156 | tf_op jit(solution)/shard_map/while
  282.7 8.9 %collective-permute-start = (bf16[64,2048]{1,0:T(8,128)(2,1)S(1)}, bf16[64,2048]{1,0:T(8,128)(2,1)S(1)}, u32[]{:S(2)}, u32[]{:S(2)}) collective-permute-start(bf16[64,2048]{1,0:T(8,128)(2,1)S(1)} %all_gather.8), channel_id=1, source_target_pairs={{0,16},{16,32},{32,48},{48,64},{64,80},{80,96},{96,112},{112,128},... | collective-permute-start | bytes 786440 | tf_op jit(solution)/shard_map/while/body/eval_jaxpr/ppermute | solution.py:12
  292.0 32.2 %copy-start.2 = (bf16[64,128]{1,0:T(8,128)(2,1)}, bf16[64,128]{1,0:T(8,128)(2,1)S(1)}, u32[]{:S(2)}) copy-start(bf16[64,128]{1,0:T(8,128)(2,1)S(1)} %fusion.11) | copy-start | bytes 49156 | tf_op jit(solution)/shard_map/while
  315.3 8.9 %collective-permute-start = (bf16[64,2048]{1,0:T(8,128)(2,1)S(1)}, bf16[64,2048]{1,0:T(8,128)(2,1)S(1)}, u32[]{:S(2)}, u32[]{:S(2)}) collective-permute-start(bf16[64,2048]{1,0:T(8,128)(2,1)S(1)} %all_gather.8), channel_id=1, source_target_pairs={{0,16},{16,32},{32,48},{48,64},{64,80},{80,96},{96,112},{112,128},... | collective-permute-start | bytes 786440 | tf_op jit(solution)/shard_map/while/body/eval_jaxpr/ppermute | solution.py:12
  324.5 30.7 %copy-start.2 = (bf16[64,128]{1,0:T(8,128)(2,1)}, bf16[64,128]{1,0:T(8,128)(2,1)S(1)}, u32[]{:S(2)}) copy-start(bf16[64,128]{1,0:T(8,128)(2,1)S(1)} %fusion.11) | copy-start | bytes 49156 | tf_op jit(solution)/shard_map/while
  346.3 8.9 %collective-permute-start = (bf16[64,2048]{1,0:T(8,128)(2,1)S(1)}, bf16[64,2048]{1,0:T(8,128)(2,1)S(1)}, u32[]{:S(2)}, u32[]{:S(2)}) collective-permute-start(bf16[64,2048]{1,0:T(8,128)(2,1)S(1)} %all_gather.8), channel_id=1, source_target_pairs={{0,16},{16,32},{32,48},{48,64},{64,80},{80,96},{96,112},{112,128},... | collective-permute-start | bytes 786440 | tf_op jit(solution)/shard_map/while/body/eval_jaxpr/ppermute | solution.py:12
  355.6 32.2 %copy-start.2 = (bf16[64,128]{1,0:T(8,128)(2,1)}, bf16[64,128]{1,0:T(8,128)(2,1)S(1)}, u32[]{:S(2)}) copy-start(bf16[64,128]{1,0:T(8,128)(2,1)S(1)} %fusion.11) | copy-start | bytes 49156 | tf_op jit(solution)/shard_map/while
  378.8 8.9 %collective-permute-start = (bf16[64,2048]{1,0:T(8,128)(2,1)S(1)}, bf16[64,2048]{1,0:T(8,128)(2,1)S(1)}, u32[]{:S(2)}, u32[]{:S(2)}) collective-permute-start(bf16[64,2048]{1,0:T(8,128)(2,1)S(1)} %all_gather.8), channel_id=1, source_target_pairs={{0,16},{16,32},{32,48},{48,64},{64,80},{80,96},{96,112},{112,128},... | collective-permute-start | bytes 786440 | tf_op jit(solution)/shard_map/while/body/eval_jaxpr/ppermute | solution.py:12
  388.1 30.7 %copy-start.2 = (bf16[64,128]{1,0:T(8,128)(2,1)}, bf16[64,128]{1,0:T(8,128)(2,1)S(1)}, u32[]{:S(2)}) copy-start(bf16[64,128]{1,0:T(8,128)(2,1)S(1)} %fusion.11) | copy-start | bytes 49156 | tf_op jit(solution)/shard_map/while
  409.9 8.9 %collective-permute-start = (bf16[64,2048]{1,0:T(8,128)(2,1)S(1)}, bf16[64,2048]{1,0:T(8,128)(2,1)S(1)}, u32[]{:S(2)}, u32[]{:S(2)}) collective-permute-start(bf16[64,2048]{1,0:T(8,128)(2,1)S(1)} %all_gather.8), channel_id=1, source_target_pairs={{0,16},{16,32},{32,48},{48,64},{64,80},{80,96},{96,112},{112,128},... | collective-permute-start | bytes 786440 | tf_op jit(solution)/shard_map/while/body/eval_jaxpr/ppermute | solution.py:12
  419.1 32.2 %copy-start.2 = (bf16[64,128]{1,0:T(8,128)(2,1)}, bf16[64,128]{1,0:T(8,128)(2,1)S(1)}, u32[]{:S(2)}) copy-start(bf16[64,128]{1,0:T(8,128)(2,1)S(1)} %fusion.11) | copy-start | bytes 49156 | tf_op jit(solution)/shard_map/while
  442.4 8.9 %collective-permute-start = (bf16[64,2048]{1,0:T(8,128)(2,1)S(1)}, bf16[64,2048]{1,0:T(8,128)(2,1)S(1)}, u32[]{:S(2)}, u32[]{:S(2)}) collective-permute-start(bf16[64,2048]{1,0:T(8,128)(2,1)S(1)} %all_gather.8), channel_id=1, source_target_pairs={{0,16},{16,32},{32,48},{48,64},{64,80},{80,96},{96,112},{112,128},... | collective-permute-start | bytes 786440 | tf_op jit(solution)/shard_map/while/body/eval_jaxpr/ppermute | solution.py:12
  451.7 30.7 %copy-start.2 = (bf16[64,128]{1,0:T(8,128)(2,1)}, bf16[64,128]{1,0:T(8,128)(2,1)S(1)}, u32[]{:S(2)}) copy-start(bf16[64,128]{1,0:T(8,128)(2,1)S(1)} %fusion.11) | copy-start | bytes 49156 | tf_op jit(solution)/shard_map/while
  473.5 8.9 %collective-permute-start = (bf16[64,2048]{1,0:T(8,128)(2,1)S(1)}, bf16[64,2048]{1,0:T(8,128)(2,1)S(1)}, u32[]{:S(2)}, u32[]{:S(2)}) collective-permute-start(bf16[64,2048]{1,0:T(8,128)(2,1)S(1)} %all_gather.8), channel_id=1, source_target_pairs={{0,16},{16,32},{32,48},{48,64},{64,80},{80,96},{96,112},{112,128},... | collective-permute-start | bytes 786440 | tf_op jit(solution)/shard_map/while/body/eval_jaxpr/ppermute | solution.py:12
  482.7 32.2 %copy-start.2 = (bf16[64,128]{1,0:T(8,128)(2,1)}, bf16[64,128]{1,0:T(8,128)(2,1)S(1)}, u32[]{:S(2)}) copy-start(bf16[64,128]{1,0:T(8,128)(2,1)S(1)} %fusion.11) | copy-start | bytes 49156 | tf_op jit(solution)/shard_map/while
  506.0 8.9 %collective-permute-start = (bf16[64,2048]{1,0:T(8,128)(2,1)S(1)}, bf16[64,2048]{1,0:T(8,128)(2,1)S(1)}, u32[]{:S(2)}, u32[]{:S(2)}) collective-permute-start(bf16[64,2048]{1,0:T(8,128)(2,1)S(1)} %all_gather.8), channel_id=1, source_target_pairs={{0,16},{16,32},{32,48},{48,64},{64,80},{80,96},{96,112},{112,128},... | collective-permute-start | bytes 786440 | tf_op jit(solution)/shard_map/while/body/eval_jaxpr/ppermute | solution.py:12
  515.3 30.7 %copy-start.2 = (bf16[64,128]{1,0:T(8,128)(2,1)}, bf16[64,128]{1,0:T(8,128)(2,1)S(1)}, u32[]{:S(2)}) copy-start(bf16[64,128]{1,0:T(8,128)(2,1)S(1)} %fusion.11) | copy-start | bytes 49156 | tf_op jit(solution)/shard_map/while
  537.0 8.9 %collective-permute-start = (bf16[64,2048]{1,0:T(8,128)(2,1)S(1)}, bf16[64,2048]{1,0:T(8,128)(2,1)S(1)}, u32[]{:S(2)}, u32[]{:S(2)}) collective-permute-start(bf16[64,2048]{1,0:T(8,128)(2,1)S(1)} %all_gather.8), channel_id=1, source_target_pairs={{0,16},{16,32},{32,48},{48,64},{64,80},{80,96},{96,112},{112,128},... | collective-permute-start | bytes 786440 | tf_op jit(solution)/shard_map/while/body/eval_jaxpr/ppermute | solution.py:12
  546.3 32.2 %copy-start.2 = (bf16[64,128]{1,0:T(8,128)(2,1)}, bf16[64,128]{1,0:T(8,128)(2,1)S(1)}, u32[]{:S(2)}) copy-start(bf16[64,128]{1,0:T(8,128)(2,1)S(1)} %fusion.11) | copy-start | bytes 49156 | tf_op jit(solution)/shard_map/while
  569.6 8.9 %collective-permute-start = (bf16[64,2048]{1,0:T(8,128)(2,1)S(1)}, bf16[64,2048]{1,0:T(8,128)(2,1)S(1)}, u32[]{:S(2)}, u32[]{:S(2)}) collective-permute-start(bf16[64,2048]{1,0:T(8,128)(2,1)S(1)} %all_gather.8), channel_id=1, source_target_pairs={{0,16},{16,32},{32,48},{48,64},{64,80},{80,96},{96,112},{112,128},... | collective-permute-start | bytes 786440 | tf_op jit(solution)/shard_map/while/body/eval_jaxpr/ppermute | solution.py:12
  578.8 30.7 %copy-start.2 = (bf16[64,128]{1,0:T(8,128)(2,1)}, bf16[64,128]{1,0:T(8,128)(2,1)S(1)}, u32[]{:S(2)}) copy-start(bf16[64,128]{1,0:T(8,128)(2,1)S(1)} %fusion.11) | copy-start | bytes 49156 | tf_op jit(solution)/shard_map/while
  600.6 8.9 %collective-permute-start = (bf16[64,2048]{1,0:T(8,128)(2,1)S(1)}, bf16[64,2048]{1,0:T(8,128)(2,1)S(1)}, u32[]{:S(2)}, u32[]{:S(2)}) collective-permute-start(bf16[64,2048]{1,0:T(8,128)(2,1)S(1)} %all_gather.8), channel_id=1, source_target_pairs={{0,16},{16,32},{32,48},{48,64},{64,80},{80,96},{96,112},{112,128},... | collective-permute-start | bytes 786440 | tf_op jit(solution)/shard_map/while/body/eval_jaxpr/ppermute | solution.py:12
Sparse Core Ops, SparseCore 0:
  10.0 84.8 all-gather.1
where the time goes:
time: 617 us; the launch traced here: 616 us
  blocking collectives  360 us (58%)
  waiting for transfers between devices  195 us (32%)
  starting transfers between devices  30.6 us (5%)
  between operations  13.5 us (2%)
  matrix products  10.5 us (2%)
    all_gather x16, blocking collectives, advance(): gathered = lax.all_gather(current, 'orb', axis=1, tiled=True)  360 us
    ppermute x16, waiting for transfers between devices, passed_along(): lax.ppermute(value, axis, [(source, source + steps) for source in range(i...  112 us
    all_gather x1, waiting for transfers between devices, on_device(): lax.all_gather(masked, 'orb', axis=0, tiled=True)  83.3 us
    ppermute x16, starting transfers between devices, passed_along(): lax.ppermute(value, axis, [(source, source + steps) for source in range(i...  30.6 us
  transfers between devices with their start and end apart: 17, of which 17 were waited for; matrix products, arithmetic and copies ran while one was open for 0% of the time, Pallas kernels for 0%

commit v1 on v0

v1 whole, which is shorter than its diff:
```python
import functools

import jax
import jax.numpy as jnp
from jax import lax
from jax.experimental import pallas as pl
from jax.experimental.pallas import tpu as pltpu
from jax.sharding import PartitionSpec as P

BLOCK = 64
SIDE = 4
CORES = 2
OFFSETS = (0, -1, 1, 2)
WHOLE = pl.BlockSpec(memory_space=pltpu.VMEM)
SCALARS = pl.BlockSpec(memory_space=pltpu.SMEM)


def near(value):
    return pltpu.with_memory_space_constraint(value, pltpu.VMEM)


def bf16(*shape):
    return jax.ShapeDtypeStruct(shape, jnp.bfloat16)


def sent(value, planes, target):
    pairs = []
    for z in range(planes):
        for k in range(CORES):
            for y in range(SIDE):
                for x in range(SIDE):
                    to = target(z, k, y, x)
                    if to is not None:
                        number = lambda z, k, y, x: ((z * CORES + k) * SIDE + y % SIDE) * SIDE + x % SIDE
                        pairs.append((number(z, k, y, x), number(*to)))
    return lax.ppermute(value, ("dom", "orb"), pairs)


def ring(low, high, move):
    low_before, high_after = move(low, 1), move(high, -1)
    high_before, low_after = move(high, 1), move(low, -1)
    low_far, high_far = move(low_before, 1), move(high_after, -1)
    return [(low, high), (low_before, high_before), (low_after, high_after), (low_far, high_far)]


def mask_kernel(info, coupling, pattern, *refs):
    pieces, (masked, done) = refs[:SIDE], refs[SIDE:]
    rows, order = coupling.shape
    fetch = pltpu.make_async_copy(coupling, masked, done)
    fetch.start()
    blocks = order // BLOCK
    column_block = lax.broadcasted_iota(jnp.int32, (blocks, order), 1) // BLOCK
    spread = (column_block == lax.broadcasted_iota(jnp.int32, (blocks, order), 0)).astype(jnp.bfloat16)
    present = jnp.dot(pattern[...].astype(jnp.bfloat16), spread, preferred_element_type=jnp.float32)
    fetch.wait()
    for at in range(rows // BLOCK):
        part = slice(at * BLOCK, (at + 1) * BLOCK)
        masked[part, :] = masked[part, :] * present[at : at + 1, :].astype(jnp.bfloat16)
    wide = order // SIDE
    for offset in range(SIDE):
        turn = lax.rem(info[2] + offset, SIDE)
        pieces[offset][...] = masked[:, pl.ds(pl.multiple_of(turn * wide, wide), wide)]


def masked_pieces(info, coupling, pattern):
    rows, order = coupling.shape
    return pl.pallas_call(
        mask_kernel,
        out_shape=[pltpu.VMEM((rows, order // SIDE), jnp.bfloat16)] * SIDE,
        in_specs=[SCALARS, pl.BlockSpec(memory_space=pltpu.HBM), WHOLE],
        out_specs=[WHOLE] * SIDE,
        scratch_shapes=[pltpu.VMEM((rows, order), jnp.bfloat16), pltpu.SemaphoreType.DMA],
        compiler_params=pltpu.CompilerParams(vmem_limit_bytes=4 << 20),
    )(info, coupling, pattern)


def halves_kernel(green, after, low, high, done):
    half = low.shape[0]
    copies = [
        pltpu.make_async_copy(green.at[pl.ds(at * half, half)], out, done.at[at]) for at, out in enumerate((low, high))
    ]
    for copy in copies:
        copy.start()
    for copy in copies:
        copy.wait()


def halves(green, after):
    rows, order = green.shape
    return pl.pallas_call(
        halves_kernel,
        out_shape=[pltpu.VMEM((rows // 2, order), jnp.bfloat16)] * 2,
        in_specs=[pl.BlockSpec(memory_space=pltpu.HBM), pl.BlockSpec(memory_space=pl.ANY)],
        out_specs=[WHOLE] * 2,
        scratch_shapes=[pltpu.SemaphoreType.DMA((2,))],
        compiler_params=pltpu.CompilerParams(vmem_limit_bytes=2 << 20),
    )(green, after)


def tile_kernel(info, *refs):
    count = 2 * SIDE
    columns, greens = refs[:count], refs[count : 2 * count]
    out_low, out_high, all_columns, all_greens = refs[2 * count :]
    core, a, b = info[0], info[1], info[2]
    rows = columns[0].shape[0] // 2
    for at, offset in enumerate(OFFSETS):
        row_turn = lax.rem(a + (offset + SIDE), SIDE)
        green_turn = lax.rem(b + (offset + SIDE), SIDE)
        for half in range(2):
            for inner in range(2):
                turn = lax.rem(b + (SIDE - 2 * half - inner), SIDE)
                block = jnp.where(core == 0, SIDE * row_turn + turn, SIDE * turn + row_turn)
                place = pl.ds(pl.multiple_of(block * rows, rows), rows)
                all_columns[place, :] = columns[2 * at + half][inner * rows : (inner + 1) * rows, :]
            part = greens[2 * at + half]
            size = part.shape[0]
            start = pl.multiple_of((2 * green_turn + half) * size, size)
            all_greens[pl.ds(start, size), :] = part[...]
    tile = jnp.dot(all_greens[...], all_columns[...], preferred_element_type=jnp.float32)
    middle = tile.shape[1] // 2
    out_low[...] = tile[:, :middle].T.astype(jnp.bfloat16)
    out_high[...] = tile[:, middle:].T.astype(jnp.bfloat16)


def tiled(info, columns, greens):
    columns = [half for pair in columns for half in pair]
    greens = [half for pair in greens for half in pair]
    wide = columns[0].shape[1]
    order = greens[0].shape[1]
    return pl.pallas_call(
        tile_kernel,
        out_shape=[bf16(wide // 2, wide)] * 2,
        in_specs=[SCALARS] + [WHOLE] * 16,
        out_specs=[WHOLE] * 2,
        scratch_shapes=[pltpu.VMEM((order, wide), jnp.bfloat16), pltpu.VMEM((wide, order), jnp.bfloat16)],
        compiler_params=pltpu.CompilerParams(vmem_limit_bytes=12 << 20),
    )(info, *map(near, columns + greens))


def arrange_kernel(info, *refs):
    own, other, (even, odd) = refs[:8], refs[8:16], refs[16:]
    core, x = info[0], info[3]
    half, wide = own[0].shape
    block = wide // SIDE

    def arrange(from_even, from_odd):
        for at, offset in enumerate(OFFSETS):
            turn = lax.rem(x + (offset + SIDE), SIDE)
            for side in range(2):
                even[pl.ds(pl.multiple_of(turn * wide + side * half, half), half), :] = from_even[2 * at + side][...]
                for row in range(SIDE):
                    place = pl.ds(pl.multiple_of((SIDE * row + turn) * block, block), block)
                    piece = from_odd[2 * at + side][:, row * block : (row + 1) * block]
                    odd[side * half : (side + 1) * half, place] = piece

    pl.when(core == 0)(lambda: arrange(own, other))
    pl.when(core != 0)(lambda: arrange(other, own))


def arranged(info, own, other):
    wide = own[0].shape[1]
    order = SIDE * wide
    return pl.pallas_call(
        arrange_kernel,
        out_shape=[pltpu.VMEM((order, wide), jnp.bfloat16), pltpu.VMEM((wide, order), jnp.bfloat16)],
        in_specs=[SCALARS] + [WHOLE] * 16,
        out_specs=[WHOLE] * 2,
        compiler_params=pltpu.CompilerParams(vmem_limit_bytes=4 << 20),
    )(info, *map(near, own), *map(near, other))


def plane_kernel(at, info, state, *refs):
    arrived, refs = refs[:SIDE], refs[SIDE:]
    even_source, odd_source, even, odd, odd_part, even_state, kept = refs
    plane, y = info[5], info[4]
    wide = even_state.shape[1]
    total = arrived[0][...].astype(jnp.float32)
    for piece in arrived[1:]:
        total += piece[...].astype(jnp.float32)
    total = jnp.where(plane == at, total, 0.0) + state[...].astype(jnp.float32)
    total = total.astype(jnp.bfloat16)
    kept[...] = total
    product = jnp.dot(total, even[...], preferred_element_type=jnp.float32)
    current = (even_source[...].astype(jnp.float32) - product).astype(jnp.bfloat16)
    even_state[...] = current
    product = jnp.dot(current, odd[...], preferred_element_type=jnp.float32)
    odd_part[...] = (odd_source[...].astype(jnp.float32) - product).astype(jnp.bfloat16)


def through_plane(at, info, state, arrived, sources, even, odd):
    modes, order = state.shape
    wide = even.shape[1]
    return pl.pallas_call(
        functools.partial(plane_kernel, at),
        out_shape=[pltpu.VMEM((modes, columns), jnp.bfloat16) for columns in (order, wide, order)],
        in_specs=[SCALARS] + [WHOLE] * 9,
        out_specs=[WHOLE] * 3,
        compiler_params=pltpu.CompilerParams(vmem_limit_bytes=4 << 20),
    )(info, *map(near, (state, *arrived, *sources, even, odd)))


def on_device(green_blocks, couplings, pattern, sources, injected):
    orb, dom = lax.axis_index("orb"), lax.axis_index("dom")
    planes = lax.axis_size("dom") // CORES
    y, x = orb // SIDE, orb % SIDE
    plane, core = dom // CORES, dom % CORES
    first = core == 0
    a, b = jnp.where(first, y, x), jnp.where(first, x, y)
    info = jnp.stack([core, a, b, x, y, plane]).astype(jnp.int32)
    send = functools.partial(sent, planes=planes)
    along_x = lambda value, step: send(value, target=lambda z, k, y, x: (z, k, y, x + step))
    along_b = lambda value, step: send(value, target=lambda z, k, y, x: (z, k, y + k * step, x + (1 - k) * step))
    along_a = lambda value, step: send(value, target=lambda z, k, y, x: (z, k, y + (1 - k) * step, x + k * step))
    to_other_core = lambda value: send(value, target=lambda z, k, y, x: (z, 1 - k, y, x))

    pieces = masked_pieces(info, couplings[0], pattern[0])
    green_low, green_high = halves(green_blocks[0], pieces[0])
    pieces = [pieces[0]] + [along_b(pieces[offset], offset) for offset in range(1, SIDE)]
    greens = ring(green_low, green_high, along_b)
    columns = ring(jnp.concatenate(pieces[:2]), jnp.concatenate(pieces[2:]), along_a)
    tile_low, tile_high = tiled(info, columns, greens)
    own = [half for pair in ring(tile_low, tile_high, along_x) for half in pair]
    other = [to_other_core(half) for half in own]
    even, odd = arranged(info, own, other)

    order = injected.shape[1]
    wide = order // SIDE
    modes = injected.shape[0] // (SIDE * CORES)
    by_x = sources[0].reshape(SIDE, CORES * modes, -1)
    source = jnp.zeros((CORES * modes, wide), jnp.bfloat16)
    for step in range(SIDE):
        piece = lax.dynamic_index_in_dim(by_x, (x + step) % SIDE, 0, keepdims=False)
        piece = along_x(piece, step) if step else piece
        source = lax.dynamic_update_slice(source, piece, (0, (x - step) % SIDE * (wide // SIDE)))
    mine = jnp.where(first, source[:modes], source[modes:])
    theirs = to_other_core(jnp.where(first, source[modes:], source[:modes]))
    even_source, odd_source = jnp.where(first, mine, theirs), jnp.where(first, theirs, mine)
    odd_source = lax.dynamic_update_slice(jnp.zeros((modes, order), jnp.bfloat16), odd_source, (0, y * wide))

    start = lax.dynamic_slice_in_dim(injected, (CORES * x + core) * modes, modes, 0)
    state = jnp.where(plane == 0, start, jnp.zeros_like(start))
    arrived = [jnp.zeros_like(start)] * SIDE
    onward = lambda z, at: z % 3 == at % 3 and z + 1 < planes
    for at in range(planes):
        odd_part, even_state, state = through_plane(
            at, info, state, arrived, (even_source, odd_source), even, odd
        )
        if at + 1 < planes:
            arrived = [
                send(odd_part, target=lambda z, k, y, x: (z + 1, k, y + turn, x) if onward(z, at) else None)
                for turn in range(SIDE)
            ]

    even_part = lax.dynamic_update_slice(jnp.zeros_like(odd_part), even_state, (0, y * wide))
    mine = jnp.where(first, even_part, odd_part)
    theirs = to_other_core(jnp.where(first, odd_part, even_part))
    both = jnp.concatenate([jnp.where(first, mine, theirs), jnp.where(first, theirs, mine)])
    both = both.reshape(CORES * modes, SIDE * SIDE, -1).transpose(1, 0, 2)
    parts = lax.all_to_all(both, "orb", 0, 0, tiled=True)
    parts = parts.reshape((SIDE, SIDE) + parts.shape[1:]).astype(jnp.float32)
    return parts.sum(0).reshape(1, injected.shape[0], -1).astype(jnp.bfloat16)


def solution(mesh):
    return jax.shard_map(
        on_device,
        mesh=mesh,
        in_specs=(
            P("dom", "orb", None),
            P("dom", "orb", None),
            P("dom", "orb", None),
            P("dom", None, "orb"),
            P(),
        ),
        out_specs=P("dom", None, "orb"),
        check_vma=False,
    )
```

time: 617 us -> 164 us (0.27)
  the two profiles are of different devices: /device:TPU:128 before, /device:TPU:224 now
where the time goes in v1:
time: 164 us; the launch traced here: 163 us
  waiting for transfers between devices  64.1 us (39%)
  starting transfers between devices  60.2 us (37%)
  Pallas kernels  18.1 us (11%)
  blocking collectives  12.8 us (8%)
  local copies, waits for them, and re-layouts  6.01 us (4%)
    ppermute x62, waiting for transfers between devices, sent(): return lax.ppermute(value, ('dom', 'orb'), pairs)  64.1 us
    ppermute x62, starting transfers between devices, sent(): return lax.ppermute(value, ('dom', 'orb'), pairs)  60.2 us
    all_to_all x1, blocking collectives, on_device(): parts = lax.all_to_all(both, 'orb', 0, 0, tiled=True)  12.8 us
    pallas_call x8, Pallas kernels, through_plane(): pl.pallas_call(functools.partial(plane_kernel, at), out_shape=[pltpu.VMEM...  12 us
    unnamed x12, local copies, waits for them, and re-layouts  4.44 us
    pallas_call x1, Pallas kernels, tiled(): pl.pallas_call(tile_kernel, out_shape=[bf16(wide // 2, wide)] * 2, in_spe...  3.36 us
  transfers between devices with their start and end apart: 62, of which 26 were waited for; matrix products, arithmetic and copies ran while one was open for 1% of the time, Pallas kernels for 2%

profile of v1, /device:TPU:224, one launch (start us, length us, event | category | flops | bytes accessed | tf_op | source)
XLA Modules:
  0.0 163.3 jit_solution(18047788220510997683)
XLA Ops:
  0.1 1.0 copy-done.1
  1.8 0.8 shard_map.55
  2.7 1.0 copy-done
  3.8 2.8 %collective-permute-start.16 = (bf16[64,2048]{1,0:T(8,128)(2,1)S(1)}, bf16[64,2048]{1,0:T(8,128)(2,1)S(1)}, u32[]{:S(2)}, u32[]{:S(2)}) collective-permute-start(bf16[64,2048]{1,0:T(8,128)(2,1)S(1)} %get-tuple-element.36.refs_9_), channel_id=1, source_target_pairs={{0,3},{1,0},{2,1},{3,2},{4,7},{5,4},{6,5},{7,6},{8,11},{9,8},{10,9... | collective-permute-start | bytes 786440 | tf_op jit(solution)/shard_map/ppermute | solution.py:36
  6.6 2.3 %collective-permute-start.5 = (bf16[128,512]{1,0:T(8,128)(2,1)S(1)}, bf16[128,512]{1,0:T(8,128)(2,1)S(1)}, u32[]{:S(2)}, u32[]{:S(2)}) collective-permute-start(bf16[128,512]{1,0:T(8,128)(2,1)S(1)} %get-tuple-element.33), channel_id=1, source_target_pairs={{0,2},{1,3},{2,0},{3,1},{4,6},{5,7},{6,4},{7,5},{8,10},{9,11},{10,... | collective-permute-start | bytes 393224 | tf_op jit(solution)/shard_map/ppermute | solution.py:36
  8.9 1.1 collective-permute-start.6
  10.0 0.9 collective-permute-start.4
  11.0 0.7 dynamic-slice_bitcast_fusion
  11.7 3.0 %collective-permute-done.5 = bf16[128,512]{1,0:T(8,128)(2,1)S(1)} collective-permute-done((bf16[128,512]{1,0:T(8,128)(2,1)S(1)}, bf16[128,512]{1,0:T(8,128)(2,1)S(1)}, u32[]{:S(2)}, u32[]{:S(2)}) %collective-permute-start.5) | collective-permute-done | bytes 131104 | tf_op jit(solution)/shard_map/ppermute | solution.py:36
  15.1 0.9 collective-permute-start
  15.9 1.0 collective-permute-done.4
  17.0 2.7 %collective-permute-start.1 = (bf16[16,128]{1,0:T(8,128)(2,1)S(1)}, bf16[16,128]{1,0:T(8,128)(2,1)S(1)}, u32[]{:S(2)}, u32[]{:S(2)}) collective-permute-start(bf16[16,128]{1,0:T(8,128)(2,1)S(1)} %get-tuple-element.62), channel_id=1, source_target_pairs={{0,2},{1,3},{2,0},{3,1},{4,6},{5,7},{6,4},{7,5},{8,10},{9,11},{10,... | collective-permute-start | bytes 12296 | tf_op jit(solution)/shard_map/ppermute | solution.py:36
  19.7 2.8 %collective-permute-done = bf16[16,128]{1,0:T(8,128)(2,1)S(1)} collective-permute-done((bf16[16,128]{1,0:T(8,128)(2,1)S(1)}, bf16[16,128]{1,0:T(8,128)(2,1)S(1)}, u32[]{:S(2)}, u32[]{:S(2)}) %collective-permute-start) | collective-permute-done | bytes 4128 | tf_op jit(solution)/shard_map/ppermute | solution.py:36
  22.9 3.0 %collective-permute-start.10 = (bf16[256,512]{1,0:T(8,128)(2,1)S(1)}, bf16[256,512]{1,0:T(8,128)(2,1)S(1)}, u32[]{:S(2)}, u32[]{:S(2)}) collective-permute-start(bf16[256,512]{1,0:T(8,128)(2,1)S(1)} %constant_dynamic-update-slice_fusion.2.refs_1_), channel_id=1, source_target_pairs={{0,12},{1,13},{2,14},{3,15},{4,0},{5,1},{6,2},{7,3},{8,4},{9,5},{1... | collective-permute-start | bytes 786440 | tf_op jit(solution)/shard_map/ppermute | solution.py:36
  26.4 2.7 %collective-permute-start.9 = (bf16[256,512]{1,0:T(8,128)(2,1)S(1)}, bf16[256,512]{1,0:T(8,128)(2,1)S(1)}, u32[]{:S(2)}, u32[]{:S(2)}) collective-permute-start(bf16[256,512]{1,0:T(8,128)(2,1)S(1)} %constant_dynamic-update-slice_fusion.refs_0_), channel_id=1, source_target_pairs={{0,12},{1,13},{2,14},{3,15},{4,0},{5,1},{6,2},{7,3},{8,4},{9,5},{1... | collective-permute-start | bytes 786440 | tf_op jit(solution)/shard_map/ppermute | solution.py:36
  29.2 2.1 %collective-permute-done.15.refs_12_ = bf16[64,2048]{1,0:T(8,128)(2,1)S(1)} collective-permute-done((bf16[64,2048]{1,0:T(8,128)(2,1)S(1)}, bf16[64,2048]{1,0:T(8,128)(2,1)S(1)}, u32[]{:S(2)}, u32[]{:S(2)}) %collective-permute-start.15) | collective-permute-done | bytes 262176 | tf_op jit(solution)/shard_map/ppermute | solution.py:36
  31.5 3.0 %collective-permute-start.18 = (bf16[64,2048]{1,0:T(8,128)(2,1)S(1)}, bf16[64,2048]{1,0:T(8,128)(2,1)}, u32[]{:S(2)}, u32[]{:S(2)}) collective-permute-start(bf16[64,2048]{1,0:T(8,128)(2,1)S(1)} %collective-permute-done.16.refs_13_), channel_id=1, source_target_pairs={{0,3},{1,0},{2,1},{3,2},{4,7},{5,4},{6,5},{7,6},{8,11},{9,8},{10,9... | collective-permute-start | bytes 786440 | tf_op jit(solution)/shard_map/ppermute | solution.py:36
  34.5 1.8 %collective-permute-start.12 = (bf16[256,512]{1,0:T(8,128)(2,1)S(1)}, bf16[256,512]{1,0:T(8,128)(2,1)}, u32[]{:S(2)}, u32[]{:S(2)}) collective-permute-start(bf16[256,512]{1,0:T(8,128)(2,1)S(1)} %collective-permute-done.10.refs_5_), channel_id=1, source_target_pairs={{0,12},{1,13},{2,14},{3,15},{4,0},{5,1},{6,2},{7,3},{8,4},{9,5},{1... | collective-permute-start | bytes 786440 | tf_op jit(solution)/shard_map/ppermute | solution.py:36
  36.3 0.8 collective-permute-done.7.refs_2_
  37.8 1.7 %collective-permute-start.2 = (bf16[16,128]{1,0:T(8,128)(2,1)S(1)}, bf16[16,128]{1,0:T(8,128)(2,1)S(1)}, u32[]{:S(2)}, u32[]{:S(2)}) collective-permute-start(bf16[16,128]{1,0:T(8,128)(2,1)S(1)} %get-tuple-element.61), channel_id=1, source_target_pairs={{0,3},{1,0},{2,1},{3,2},{4,7},{5,4},{6,5},{7,6},{8,11},{9,8},{10,9... | collective-permute-start | bytes 12296 | tf_op jit(solution)/shard_map/ppermute | solution.py:36
  39.5 1.5 collective-permute-done.17.refs_14_
  41.8 3.0 %collective-permute-done.11.refs_6_ = bf16[256,512]{1,0:T(8,128)(2,1)} collective-permute-done((bf16[256,512]{1,0:T(8,128)(2,1)S(1)}, bf16[256,512]{1,0:T(8,128)(2,1)}, u32[]{:S(2)}, u32[]{:S(2)}) %collective-permute-start.11) | collective-permute-done | bytes 262176 | tf_op jit(solution)/shard_map/ppermute | solution.py:36
  44.8 0.9 copy-done.3
  45.7 3.4 %shard_map.57 = (bf16[256,512]{1,0:T(8,128)(2,1)S(1)}, bf16[256,512]{1,0:T(8,128)(2,1)}) custom-call(s32[6]{0:T(128)S(1)} %stack.27.info, bf16[256,512]{1,0:T(8,128)(2,1)S(1)} %constant_dynamic-update-slice_fusion.refs_0_, bf16[256,512]{1,0:T(8,128)(2,1)S(1)} %constant_dynamic-update-slice_fusion.2.refs_1_, ...), custom_call_target="tpu_custom_call" | custom-call | tf_op jit(solution)/shard_map/pallas_call | solution.py:130
  49.1 1.7 %collective-permute-start.22 = (bf16[256,512]{1,0:T(8,128)(2,1)}, bf16[256,512]{1,0:T(8,128)(2,1)S(1)}, u32[]{:S(2)}, u32[]{:S(2)}) collective-permute-start(bf16[256,512]{1,0:T(8,128)(2,1)} %get-tuple-element.38.refs_1_), channel_id=1, source_target_pairs={{0,3},{1,0},{2,1},{3,2},{4,7},{5,4},{6,5},{7,6},{8,11},{9,8},{10,9... | collective-permute-start | bytes 786440 | tf_op jit(solution)/shard_map/ppermute | solution.py:36
  51.1 0.8 collective-permute-start.19
  51.9 2.5 %collective-permute-start.21 = (bf16[256,512]{1,0:T(8,128)(2,1)S(1)}, bf16[256,512]{1,0:T(8,128)(2,1)S(1)}, u32[]{:S(2)}, u32[]{:S(2)}) collective-permute-start(bf16[256,512]{1,0:T(8,128)(2,1)S(1)} %get-tuple-element.37.refs_0_), channel_id=1, source_target_pairs={{0,3},{1,0},{2,1},{3,2},{4,7},{5,4},{6,5},{7,6},{8,11},{9,8},{10,9... | collective-permute-start | bytes 786440 | tf_op jit(solution)/shard_map/ppermute | solution.py:36
  54.5 1.2 collective-permute-done.3
  55.8 5.6 %collective-permute-done.19.refs_2_ = bf16[256,512]{1,0:T(8,128)(2,1)S(1)} collective-permute-done((bf16[256,512]{1,0:T(8,128)(2,1)S(1)}, bf16[256,512]{1,0:T(8,128)(2,1)S(1)}, u32[]{:S(2)}, u32[]{:S(2)}) %collective-permute-start.19) | collective-permute-done | bytes 262176 | tf_op jit(solution)/shard_map/ppermute | solution.py:36
  61.4 3.2 %collective-permute-start.24 = (bf16[256,512]{1,0:T(8,128)(2,1)S(1)}, bf16[256,512]{1,0:T(8,128)(2,1)S(1)}, u32[]{:S(2)}, u32[]{:S(2)}) collective-permute-start(bf16[256,512]{1,0:T(8,128)(2,1)S(1)} %collective-permute-done.22.refs_5_), channel_id=1, source_target_pairs={{0,3},{1,0},{2,1},{3,2},{4,7},{5,4},{6,5},{7,6},{8,11},{9,8},{10,9... | collective-permute-start | bytes 786440 | tf_op jit(solution)/shard_map/ppermute | solution.py:36
  65.2 6.1 %collective-permute-done.23.refs_6_ = bf16[256,512]{1,0:T(8,128)(2,1)S(1)} collective-permute-done((bf16[256,512]{1,0:T(8,128)(2,1)S(1)}, bf16[256,512]{1,0:T(8,128)(2,1)S(1)}, u32[]{:S(2)}, u32[]{:S(2)}) %collective-permute-start.23) | collective-permute-done | bytes 262176 | tf_op jit(solution)/shard_map/ppermute | solution.py:36
  72.1 0.8 dynamic-slice_select_fusion.state
  73.7 1.9 %shard_map.58 = (bf16[2048,512]{1,0:T(8,128)(2,1)S(1)}, bf16[512,2048]{1,0:T(8,128)(2,1)S(1)}) custom-call(s32[6]{0:T(128)S(1)} %stack.27.info, bf16[256,512]{1,0:T(8,128)(2,1)S(1)} %get-tuple-element.37.refs_0_, bf16[256,512]{1,0:T(8,128)(2,1)} %get-tuple-element.38.refs_1_, bf16[256,512]{1,0:T(8,128)(2,1)S(1)} %collective-permute-done.19.refs_2_, ...), custom_call_target="tpu_custom_call" | custom-call | tf_op jit(solution)/shard_map/pallas_call | solution.py:163
  75.6 1.5 shard_map.59
  77.1 1.3 collective-permute-start.33
  78.4 1.3 collective-permute-start.34
  79.7 1.3 collective-permute-start.35
  81.0 1.3 collective-permute-start.36
  82.9 3.4 %collective-permute-done.34.refs_1_ = bf16[8,2048]{1,0:T(8,128)(2,1)S(1)} collective-permute-done((bf16[8,2048]{1,0:T(8,128)(2,1)S(1)}, bf16[8,2048]{1,0:T(8,128)(2,1)S(1)}, u32[]{:S(2)}, u32[]{:S(2)}) %collective-permute-start.34) | collective-permute-done | bytes 32800 | tf_op jit(solution)/shard_map/ppermute | solution.py:36
  86.3 1.6 collective-permute-done.35.refs_2_
  87.9 1.5 shard_map.60
  92.2 1.5 shard_map.61
  96.4 1.5 shard_map.62
  97.9 1.3 collective-permute-start.45
  99.2 1.3 collective-permute-start.46
  100.5 1.3 collective-permute-start.47
  101.8 1.3 collective-permute-start.48
  103.1 12.3 %collective-permute-done.45.refs_0_ = bf16[8,2048]{1,0:T(8,128)(2,1)S(1)} collective-permute-done((bf16[8,2048]{1,0:T(8,128)(2,1)S(1)}, bf16[8,2048]{1,0:T(8,128)(2,1)S(1)}, u32[]{:S(2)}, u32[]{:S(2)}) %collective-permute-start.45) | collective-permute-done | bytes 32800 | tf_op jit(solution)/shard_map/ppermute | solution.py:36
  115.4 2.7 %collective-permute-done.46.refs_1_ = bf16[8,2048]{1,0:T(8,128)(2,1)S(1)} collective-permute-done((bf16[8,2048]{1,0:T(8,128)(2,1)S(1)}, bf16[8,2048]{1,0:T(8,128)(2,1)S(1)}, u32[]{:S(2)}, u32[]{:S(2)}) %collective-permute-start.46) | collective-permute-done | bytes 32800 | tf_op jit(solution)/shard_map/ppermute | solution.py:36
  118.1 1.5 collective-permute-done.47.refs_2_
  119.6 1.5 shard_map.63
  123.8 1.5 shard_map.64
  128.1 1.5 shard_map.65
  129.6 1.3 collective-permute-start.57
  130.9 1.3 collective-permute-start.58
  132.2 1.3 collective-permute-start.59
  133.5 1.3 collective-permute-start.60
  134.8 7.8 %collective-permute-done.57.refs_0_ = bf16[8,2048]{1,0:T(8,128)(2,1)S(1)} collective-permute-done((bf16[8,2048]{1,0:T(8,128)(2,1)S(1)}, bf16[8,2048]{1,0:T(8,128)(2,1)S(1)}, u32[]{:S(2)}, u32[]{:S(2)}) %collective-permute-start.57) | collective-permute-done | bytes 32800 | tf_op jit(solution)/shard_map/ppermute | solution.py:36
  142.6 2.2 %collective-permute-done.58.refs_1_ = bf16[8,2048]{1,0:T(8,128)(2,1)S(1)} collective-permute-done((bf16[8,2048]{1,0:T(8,128)(2,1)S(1)}, bf16[8,2048]{1,0:T(8,128)(2,1)S(1)}, u32[]{:S(2)}, u32[]{:S(2)}) %collective-permute-start.58) | collective-permute-done | bytes 32800 | tf_op jit(solution)/shard_map/ppermute | solution.py:36
  144.8 1.4 collective-permute-done.59.refs_2_
  146.2 1.0 collective-permute-done.60.refs_3_
  147.2 1.3 shard_map.66
  148.6 1.2 collective-permute-done.61
  149.8 12.8 %all_to_all.5 = bf16[16,16,128]{2,1,0:T(8,128)(2,1)S(1)} all-to-all(bf16[16,16,128]{2,1,0:T(8,128)(2,1)S(1)} %bitcast_bitcast_fusion), channel_id=1, replica_groups=mesh['dom'=16,'orb'=16] {'orb'}, dimensions={0} | all-to-all | bytes 131072 | tf_op jit(solution)/shard_map/all_to_all | solution.py:259
  (104 shorter events, 18.8 us)
Async XLA Ops:
  0.1 1.0 copy-start.1
  2.6 1.0 copy-start
  3.8 22.1 %collective-permute-start.16 = (bf16[64,2048]{1,0:T(8,128)(2,1)S(1)}, bf16[64,2048]{1,0:T(8,128)(2,1)S(1)}, u32[]{:S(2)}, u32[]{:S(2)}) collective-permute-start(bf16[64,2048]{1,0:T(8,128)(2,1)S(1)} %get-tuple-element.36.refs_9_), channel_id=1, source_target_pairs={{0,3},{1,0},{2,1},{3,2},{4,7},{5,4},{6,5},{7,6},{8,11},{9,8},{10,9... | collective-permute-start | bytes 786440 | tf_op jit(solution)/shard_map/ppermute | solution.py:36
  6.6 19.9 %collective-permute-start.14 = (bf16[64,2048]{1,0:T(8,128)(2,1)S(1)}, bf16[64,2048]{1,0:T(8,128)(2,1)S(1)}, u32[]{:S(2)}, u32[]{:S(2)}) collective-permute-start(bf16[64,2048]{1,0:T(8,128)(2,1)S(1)} %get-tuple-element.36.refs_9_), channel_id=1, source_target_pairs={{0,1},{1,2},{2,3},{3,0},{4,5},{5,6},{6,7},{7,4},{8,9},{9,10},{10,1... | collective-permute-start | bytes 786440 | tf_op jit(solution)/shard_map/ppermute | solution.py:36
  6.6 8.1 %collective-permute-start.5 = (bf16[128,512]{1,0:T(8,128)(2,1)S(1)}, bf16[128,512]{1,0:T(8,128)(2,1)S(1)}, u32[]{:S(2)}, u32[]{:S(2)}) collective-permute-start(bf16[128,512]{1,0:T(8,128)(2,1)S(1)} %get-tuple-element.33), channel_id=1, source_target_pairs={{0,2},{1,3},{2,0},{3,1},{4,6},{5,7},{6,4},{7,5},{8,10},{9,11},{10,... | collective-permute-start | bytes 393224 | tf_op jit(solution)/shard_map/ppermute | solution.py:36
  8.9 6.2 %collective-permute-start.6 = (bf16[128,512]{1,0:T(8,128)(2,1)S(1)}, bf16[128,512]{1,0:T(8,128)(2,1)S(1)}, u32[]{:S(2)}, u32[]{:S(2)}) collective-permute-start(bf16[128,512]{1,0:T(8,128)(2,1)S(1)} %get-tuple-element.34), channel_id=1, source_target_pairs={{0,3},{1,0},{2,1},{3,2},{4,7},{5,4},{6,5},{7,6},{8,11},{9,8},{10,9... | collective-permute-start | bytes 393224 | tf_op jit(solution)/shard_map/ppermute | solution.py:36
  10.0 7.0 %collective-permute-start.4 = (bf16[128,512]{1,0:T(8,128)(2,1)S(1)}, bf16[128,512]{1,0:T(8,128)(2,1)S(1)}, u32[]{:S(2)}, u32[]{:S(2)}) collective-permute-start(bf16[128,512]{1,0:T(8,128)(2,1)S(1)} %get-tuple-element.32), channel_id=1, source_target_pairs={{0,1},{1,2},{2,3},{3,0},{4,5},{5,6},{6,7},{7,4},{8,9},{9,10},{10,1... | collective-permute-start | bytes 393224 | tf_op jit(solution)/shard_map/ppermute | solution.py:36
  14.7 11.1 %collective-permute-start.13 = (bf16[64,2048]{1,0:T(8,128)(2,1)S(1)}, bf16[64,2048]{1,0:T(8,128)(2,1)S(1)}, u32[]{:S(2)}, u32[]{:S(2)}) collective-permute-start(bf16[64,2048]{1,0:T(8,128)(2,1)S(1)} %get-tuple-element.35.refs_8_), channel_id=1, source_target_pairs={{0,1},{1,2},{2,3},{3,0},{4,5},{5,6},{6,7},{7,4},{8,9},{9,10},{10,1... | collective-permute-start | bytes 786440 | tf_op jit(solution)/shard_map/ppermute | solution.py:36
  15.1 7.4 %collective-permute-start = (bf16[16,128]{1,0:T(8,128)(2,1)S(1)}, bf16[16,128]{1,0:T(8,128)(2,1)S(1)}, u32[]{:S(2)}, u32[]{:S(2)}) collective-permute-start(bf16[16,128]{1,0:T(8,128)(2,1)S(1)} %get-tuple-element.63), channel_id=1, source_target_pairs={{0,1},{1,2},{2,3},{3,0},{4,5},{5,6},{6,7},{7,4},{8,9},{9,10},{10,1... | collective-permute-start | bytes 12296 | tf_op jit(solution)/shard_map/ppermute | solution.py:36
  17.0 5.9 %collective-permute-start.1 = (bf16[16,128]{1,0:T(8,128)(2,1)S(1)}, bf16[16,128]{1,0:T(8,128)(2,1)S(1)}, u32[]{:S(2)}, u32[]{:S(2)}) collective-permute-start(bf16[16,128]{1,0:T(8,128)(2,1)S(1)} %get-tuple-element.62), channel_id=1, source_target_pairs={{0,2},{1,3},{2,0},{3,1},{4,6},{5,7},{6,4},{7,5},{8,10},{9,11},{10,... | collective-permute-start | bytes 12296 | tf_op jit(solution)/shard_map/ppermute | solution.py:36
  22.5 8.8 %collective-permute-start.15 = (bf16[64,2048]{1,0:T(8,128)(2,1)S(1)}, bf16[64,2048]{1,0:T(8,128)(2,1)S(1)}, u32[]{:S(2)}, u32[]{:S(2)}) collective-permute-start(bf16[64,2048]{1,0:T(8,128)(2,1)S(1)} %get-tuple-element.35.refs_8_), channel_id=1, source_target_pairs={{0,3},{1,0},{2,1},{3,2},{4,7},{5,4},{6,5},{7,6},{8,11},{9,8},{10,9... | collective-permute-start | bytes 786440 | tf_op jit(solution)/shard_map/ppermute | solution.py:36
  22.9 8.7 %collective-permute-start.10 = (bf16[256,512]{1,0:T(8,128)(2,1)S(1)}, bf16[256,512]{1,0:T(8,128)(2,1)S(1)}, u32[]{:S(2)}, u32[]{:S(2)}) collective-permute-start(bf16[256,512]{1,0:T(8,128)(2,1)S(1)} %constant_dynamic-update-slice_fusion.2.refs_1_), channel_id=1, source_target_pairs={{0,12},{1,13},{2,14},{3,15},{4,0},{5,1},{6,2},{7,3},{8,4},{9,5},{1... | collective-permute-start | bytes 786440 | tf_op jit(solution)/shard_map/ppermute | solution.py:36
  25.8 8.7 %collective-permute-start.8 = (bf16[256,512]{1,0:T(8,128)(2,1)S(1)}, bf16[256,512]{1,0:T(8,128)(2,1)S(1)}, u32[]{:S(2)}, u32[]{:S(2)}) collective-permute-start(bf16[256,512]{1,0:T(8,128)(2,1)S(1)} %constant_dynamic-update-slice_fusion.2.refs_1_), channel_id=1, source_target_pairs={{0,4},{1,5},{2,6},{3,7},{4,8},{5,9},{6,10},{7,11},{8,12},{9,13},{1... | collective-permute-start | bytes 786440 | tf_op jit(solution)/shard_map/ppermute | solution.py:36
  25.9 11.2 %collective-permute-start.7 = (bf16[256,512]{1,0:T(8,128)(2,1)S(1)}, bf16[256,512]{1,0:T(8,128)(2,1)S(1)}, u32[]{:S(2)}, u32[]{:S(2)}) collective-permute-start(bf16[256,512]{1,0:T(8,128)(2,1)S(1)} %constant_dynamic-update-slice_fusion.refs_0_), channel_id=1, source_target_pairs={{0,4},{1,5},{2,6},{3,7},{4,8},{5,9},{6,10},{7,11},{8,12},{9,13},{1... | collective-permute-start | bytes 786440 | tf_op jit(solution)/shard_map/ppermute | solution.py:36
  26.4 11.4 %collective-permute-start.9 = (bf16[256,512]{1,0:T(8,128)(2,1)S(1)}, bf16[256,512]{1,0:T(8,128)(2,1)S(1)}, u32[]{:S(2)}, u32[]{:S(2)}) collective-permute-start(bf16[256,512]{1,0:T(8,128)(2,1)S(1)} %constant_dynamic-update-slice_fusion.refs_0_), channel_id=1, source_target_pairs={{0,12},{1,13},{2,14},{3,15},{4,0},{5,1},{6,2},{7,3},{8,4},{9,5},{1... | collective-permute-start | bytes 786440 | tf_op jit(solution)/shard_map/ppermute | solution.py:36
  31.2 9.8 %collective-permute-start.17 = (bf16[64,2048]{1,0:T(8,128)(2,1)S(1)}, bf16[64,2048]{1,0:T(8,128)(2,1)S(1)}, u32[]{:S(2)}, u32[]{:S(2)}) collective-permute-start(bf16[64,2048]{1,0:T(8,128)(2,1)S(1)} %collective-permute-done.13.refs_10_), channel_id=1, source_target_pairs={{0,1},{1,2},{2,3},{3,0},{4,5},{5,6},{6,7},{7,4},{8,9},{9,10},{10,1... | collective-permute-start | bytes 786440 | tf_op jit(solution)/shard_map/ppermute | solution.py:36
  31.5 10.2 %collective-permute-start.18 = (bf16[64,2048]{1,0:T(8,128)(2,1)S(1)}, bf16[64,2048]{1,0:T(8,128)(2,1)}, u32[]{:S(2)}, u32[]{:S(2)}) collective-permute-start(bf16[64,2048]{1,0:T(8,128)(2,1)S(1)} %collective-permute-done.16.refs_13_), channel_id=1, source_target_pairs={{0,3},{1,0},{2,1},{3,2},{4,7},{5,4},{6,5},{7,6},{8,11},{9,8},{10,9... | collective-permute-start | bytes 786440 | tf_op jit(solution)/shard_map/ppermute | solution.py:36
  34.5 7.3 %collective-permute-start.12 = (bf16[256,512]{1,0:T(8,128)(2,1)S(1)}, bf16[256,512]{1,0:T(8,128)(2,1)}, u32[]{:S(2)}, u32[]{:S(2)}) collective-permute-start(bf16[256,512]{1,0:T(8,128)(2,1)S(1)} %collective-permute-done.10.refs_5_), channel_id=1, source_target_pairs={{0,12},{1,13},{2,14},{3,15},{4,0},{5,1},{6,2},{7,3},{8,4},{9,5},{1... | collective-permute-start | bytes 786440 | tf_op jit(solution)/shard_map/ppermute | solution.py:36
  37.1 7.7 %collective-permute-start.11 = (bf16[256,512]{1,0:T(8,128)(2,1)S(1)}, bf16[256,512]{1,0:T(8,128)(2,1)}, u32[]{:S(2)}, u32[]{:S(2)}) collective-permute-start(bf16[256,512]{1,0:T(8,128)(2,1)S(1)} %collective-permute-done.7.refs_2_), channel_id=1, source_target_pairs={{0,4},{1,5},{2,6},{3,7},{4,8},{5,9},{6,10},{7,11},{8,12},{9,13},{1... | collective-permute-start | bytes 786440 | tf_op jit(solution)/shard_map/ppermute | solution.py:36
  37.8 16.6 %collective-permute-start.2 = (bf16[16,128]{1,0:T(8,128)(2,1)S(1)}, bf16[16,128]{1,0:T(8,128)(2,1)S(1)}, u32[]{:S(2)}, u32[]{:S(2)}) collective-permute-start(bf16[16,128]{1,0:T(8,128)(2,1)S(1)} %get-tuple-element.61), channel_id=1, source_target_pairs={{0,3},{1,0},{2,1},{3,2},{4,7},{5,4},{6,5},{7,6},{8,11},{9,8},{10,9... | collective-permute-start | bytes 12296 | tf_op jit(solution)/shard_map/ppermute | solution.py:36
  49.1 12.3 %collective-permute-start.22 = (bf16[256,512]{1,0:T(8,128)(2,1)}, bf16[256,512]{1,0:T(8,128)(2,1)S(1)}, u32[]{:S(2)}, u32[]{:S(2)}) collective-permute-start(bf16[256,512]{1,0:T(8,128)(2,1)} %get-tuple-element.38.refs_1_), channel_id=1, source_target_pairs={{0,3},{1,0},{2,1},{3,2},{4,7},{5,4},{6,5},{7,6},{8,11},{9,8},{10,9... | collective-permute-start | bytes 786440 | tf_op jit(solution)/shard_map/ppermute | solution.py:36
  50.8 10.6 %collective-permute-start.20 = (bf16[256,512]{1,0:T(8,128)(2,1)}, bf16[256,512]{1,0:T(8,128)(2,1)S(1)}, u32[]{:S(2)}, u32[]{:S(2)}) collective-permute-start(bf16[256,512]{1,0:T(8,128)(2,1)} %get-tuple-element.38.refs_1_), channel_id=1, source_target_pairs={{0,1},{1,2},{2,3},{3,0},{4,5},{5,6},{6,7},{7,4},{8,9},{9,10},{10,1... | collective-permute-start | bytes 786440 | tf_op jit(solution)/shard_map/ppermute | solution.py:36
  51.1 10.2 %collective-permute-start.19 = (bf16[256,512]{1,0:T(8,128)(2,1)S(1)}, bf16[256,512]{1,0:T(8,128)(2,1)S(1)}, u32[]{:S(2)}, u32[]{:S(2)}) collective-permute-start(bf16[256,512]{1,0:T(8,128)(2,1)S(1)} %get-tuple-element.37.refs_0_), channel_id=1, source_target_pairs={{0,1},{1,2},{2,3},{3,0},{4,5},{5,6},{6,7},{7,4},{8,9},{9,10},{10,1... | collective-permute-start | bytes 786440 | tf_op jit(solution)/shard_map/ppermute | solution.py:36
  51.9 12.7 %collective-permute-start.21 = (bf16[256,512]{1,0:T(8,128)(2,1)S(1)}, bf16[256,512]{1,0:T(8,128)(2,1)S(1)}, u32[]{:S(2)}, u32[]{:S(2)}) collective-permute-start(bf16[256,512]{1,0:T(8,128)(2,1)S(1)} %get-tuple-element.37.refs_0_), channel_id=1, source_target_pairs={{0,3},{1,0},{2,1},{3,2},{4,7},{5,4},{6,5},{7,6},{8,11},{9,8},{10,9... | collective-permute-start | bytes 786440 | tf_op jit(solution)/shard_map/ppermute | solution.py:36
  54.4 1.3 collective-permute-start.3
  55.6 9.0 %collective-permute-start.25 = (bf16[256,512]{1,0:T(8,128)(2,1)S(1)}, bf16[256,512]{1,0:T(8,128)(2,1)S(1)}, u32[]{:S(2)}, u32[]{:S(2)}) collective-permute-start(bf16[256,512]{1,0:T(8,128)(2,1)S(1)} %get-tuple-element.37.refs_0_), channel_id=1, source_target_pairs={{0,16},{1,17},{2,18},{3,19},{4,20},{5,21},{6,22},{7,23},{8,24},{9,... | collective-permute-start | bytes 786440 | tf_op jit(solution)/shard_map/ppermute | solution.py:36
  61.4 3.8 %collective-permute-start.26 = (bf16[256,512]{1,0:T(8,128)(2,1)}, bf16[256,512]{1,0:T(8,128)(2,1)S(1)}, u32[]{:S(2)}, u32[]{:S(2)}) collective-permute-start(bf16[256,512]{1,0:T(8,128)(2,1)} %get-tuple-element.38.refs_1_), channel_id=1, source_target_pairs={{0,16},{1,17},{2,18},{3,19},{4,20},{5,21},{6,22},{7,23},{8,24},{9,... | collective-permute-start | bytes 786440 | tf_op jit(solution)/shard_map/ppermute | solution.py:36
  61.4 9.9 %collective-permute-start.23 = (bf16[256,512]{1,0:T(8,128)(2,1)S(1)}, bf16[256,512]{1,0:T(8,128)(2,1)S(1)}, u32[]{:S(2)}, u32[]{:S(2)}) collective-permute-start(bf16[256,512]{1,0:T(8,128)(2,1)S(1)} %collective-permute-done.19.refs_2_), channel_id=1, source_target_pairs={{0,1},{1,2},{2,3},{3,0},{4,5},{5,6},{6,7},{7,4},{8,9},{9,10},{10,1... | collective-permute-start | bytes 786440 | tf_op jit(solution)/shard_map/ppermute | solution.py:36
  61.4 9.9 %collective-permute-start.24 = (bf16[256,512]{1,0:T(8,128)(2,1)S(1)}, bf16[256,512]{1,0:T(8,128)(2,1)S(1)}, u32[]{:S(2)}, u32[]{:S(2)}) collective-permute-start(bf16[256,512]{1,0:T(8,128)(2,1)S(1)} %collective-permute-done.22.refs_5_), channel_id=1, source_target_pairs={{0,3},{1,0},{2,1},{3,2},{4,7},{5,4},{6,5},{7,6},{8,11},{9,8},{10,9... | collective-permute-start | bytes 786440 | tf_op jit(solution)/shard_map/ppermute | solution.py:36
  64.6 7.2 %collective-permute-start.27 = (bf16[256,512]{1,0:T(8,128)(2,1)S(1)}, bf16[256,512]{1,0:T(8,128)(2,1)S(1)}, u32[]{:S(2)}, u32[]{:S(2)}) collective-permute-start(bf16[256,512]{1,0:T(8,128)(2,1)S(1)} %collective-permute-done.19.refs_2_), channel_id=1, source_target_pairs={{0,16},{1,17},{2,18},{3,19},{4,20},{5,21},{6,22},{7,23},{8,24},{9,... | collective-permute-start | bytes 786440 | tf_op jit(solution)/shard_map/ppermute | solution.py:36
  64.6 8.5 %collective-permute-start.30 = (bf16[256,512]{1,0:T(8,128)(2,1)S(1)}, bf16[256,512]{1,0:T(8,128)(2,1)S(1)}, u32[]{:S(2)}, u32[]{:S(2)}) collective-permute-start(bf16[256,512]{1,0:T(8,128)(2,1)S(1)} %collective-permute-done.22.refs_5_), channel_id=1, source_target_pairs={{0,16},{1,17},{2,18},{3,19},{4,20},{5,21},{6,22},{7,23},{8,24},{9,... | collective-permute-start | bytes 786440 | tf_op jit(solution)/shard_map/ppermute | solution.py:36
  65.1 7.8 %collective-permute-start.28 = (bf16[256,512]{1,0:T(8,128)(2,1)S(1)}, bf16[256,512]{1,0:T(8,128)(2,1)S(1)}, u32[]{:S(2)}, u32[]{:S(2)}) collective-permute-start(bf16[256,512]{1,0:T(8,128)(2,1)S(1)} %collective-permute-done.20.refs_3_), channel_id=1, source_target_pairs={{0,16},{1,17},{2,18},{3,19},{4,20},{5,21},{6,22},{7,23},{8,24},{9,... | collective-permute-start | bytes 786440 | tf_op jit(solution)/shard_map/ppermute | solution.py:36
  71.3 1.8 %collective-permute-start.29 = (bf16[256,512]{1,0:T(8,128)(2,1)S(1)}, bf16[256,512]{1,0:T(8,128)(2,1)S(1)}, u32[]{:S(2)}, u32[]{:S(2)}) collective-permute-start(bf16[256,512]{1,0:T(8,128)(2,1)S(1)} %collective-permute-done.21.refs_4_), channel_id=1, source_target_pairs={{0,16},{1,17},{2,18},{3,19},{4,20},{5,21},{6,22},{7,23},{8,24},{9,... | collective-permute-start | bytes 786440 | tf_op jit(solution)/shard_map/ppermute | solution.py:36
  71.3 2.0 %collective-permute-start.31 = (bf16[256,512]{1,0:T(8,128)(2,1)S(1)}, bf16[256,512]{1,0:T(8,128)(2,1)}, u32[]{:S(2)}, u32[]{:S(2)}) collective-permute-start(bf16[256,512]{1,0:T(8,128)(2,1)S(1)} %collective-permute-done.23.refs_6_), channel_id=1, source_target_pairs={{0,16},{1,17},{2,18},{3,19},{4,20},{5,21},{6,22},{7,23},{8,24},{9,... | collective-permute-start | bytes 786440 | tf_op jit(solution)/shard_map/ppermute | solution.py:36
  71.8 1.9 %collective-permute-start.32 = (bf16[256,512]{1,0:T(8,128)(2,1)S(1)}, bf16[256,512]{1,0:T(8,128)(2,1)}, u32[]{:S(2)}, u32[]{:S(2)}) collective-permute-start(bf16[256,512]{1,0:T(8,128)(2,1)S(1)} %collective-permute-done.24.refs_7_), channel_id=1, source_target_pairs={{0,16},{1,17},{2,18},{3,19},{4,20},{5,21},{6,22},{7,23},{8,24},{9,... | collective-permute-start | bytes 786440 | tf_op jit(solution)/shard_map/ppermute | solution.py:36
  77.1 5.8 %collective-permute-start.33 = (bf16[8,2048]{1,0:T(8,128)(2,1)S(1)}, bf16[8,2048]{1,0:T(8,128)(2,1)S(1)}, u32[]{:S(2)}, u32[]{:S(2)}) collective-permute-start(bf16[8,2048]{1,0:T(8,128)(2,1)S(1)} %get-tuple-element.42), channel_id=1, source_target_pairs={{0,32},{1,33},{2,34},{3,35},{4,36},{5,37},{6,38},{7,39},{8,40},{9,... | collective-permute-start | bytes 98312 | tf_op jit(solution)/shard_map/ppermute | solution.py:36
  78.4 7.9 %collective-permute-start.34 = (bf16[8,2048]{1,0:T(8,128)(2,1)S(1)}, bf16[8,2048]{1,0:T(8,128)(2,1)S(1)}, u32[]{:S(2)}, u32[]{:S(2)}) collective-permute-start(bf16[8,2048]{1,0:T(8,128)(2,1)S(1)} %get-tuple-element.42), channel_id=1, source_target_pairs={{0,36},{1,37},{2,38},{3,39},{4,40},{5,41},{6,42},{7,43},{8,44},{9,... | collective-permute-start | bytes 98312 | tf_op jit(solution)/shard_map/ppermute | solution.py:36
  79.7 8.2 %collective-permute-start.35 = (bf16[8,2048]{1,0:T(8,128)(2,1)S(1)}, bf16[8,2048]{1,0:T(8,128)(2,1)S(1)}, u32[]{:S(2)}, u32[]{:S(2)}) collective-permute-start(bf16[8,2048]{1,0:T(8,128)(2,1)S(1)} %get-tuple-element.42), channel_id=1, source_target_pairs={{0,40},{1,41},{2,42},{3,43},{4,44},{5,45},{6,46},{7,47},{8,32},{9,... | collective-permute-start | bytes 98312 | tf_op jit(solution)/shard_map/ppermute | solution.py:36
  81.0 6.9 %collective-permute-start.36 = (bf16[8,2048]{1,0:T(8,128)(2,1)S(1)}, bf16[8,2048]{1,0:T(8,128)(2,1)S(1)}, u32[]{:S(2)}, u32[]{:S(2)}) collective-permute-start(bf16[8,2048]{1,0:T(8,128)(2,1)S(1)} %get-tuple-element.42), channel_id=1, source_target_pairs={{0,44},{1,45},{2,46},{3,47},{4,32},{5,33},{6,34},{7,35},{8,36},{9,... | collective-permute-start | bytes 98312 | tf_op jit(solution)/shard_map/ppermute | solution.py:36
  89.4 2.7 %collective-permute-start.37 = (bf16[8,2048]{1,0:T(8,128)(2,1)S(1)}, bf16[8,2048]{1,0:T(8,128)(2,1)S(1)}, u32[]{:S(2)}, u32[]{:S(2)}) collective-permute-start(bf16[8,2048]{1,0:T(8,128)(2,1)S(1)} %get-tuple-element.44), channel_id=1, source_target_pairs={{32,64},{33,65},{34,66},{35,67},{36,68},{37,69},{38,70},{39,71},{4... | collective-permute-start | bytes 98312 | tf_op jit(solution)/shard_map/ppermute | solution.py:36
  90.1 2.0 %collective-permute-start.38 = (bf16[8,2048]{1,0:T(8,128)(2,1)S(1)}, bf16[8,2048]{1,0:T(8,128)(2,1)S(1)}, u32[]{:S(2)}, u32[]{:S(2)}) collective-permute-start(bf16[8,2048]{1,0:T(8,128)(2,1)S(1)} %get-tuple-element.44), channel_id=1, source_target_pairs={{32,68},{33,69},{34,70},{35,71},{36,72},{37,73},{38,74},{39,75},{4... | collective-permute-start | bytes 98312 | tf_op jit(solution)/shard_map/ppermute | solution.py:36
  90.8 1.4 collective-permute-start.39
  91.4 0.7 collective-permute-start.40
  93.7 2.7 %collective-permute-start.41 = (bf16[8,2048]{1,0:T(8,128)(2,1)S(1)}, bf16[8,2048]{1,0:T(8,128)(2,1)S(1)}, u32[]{:S(2)}, u32[]{:S(2)}) collective-permute-start(bf16[8,2048]{1,0:T(8,128)(2,1)S(1)} %get-tuple-element.46), channel_id=1, source_target_pairs={{64,96},{65,97},{66,98},{67,99},{68,100},{69,101},{70,102},{71,103... | collective-permute-start | bytes 98312 | tf_op jit(solution)/shard_map/ppermute | solution.py:36
  94.3 2.0 %collective-permute-start.42 = (bf16[8,2048]{1,0:T(8,128)(2,1)S(1)}, bf16[8,2048]{1,0:T(8,128)(2,1)S(1)}, u32[]{:S(2)}, u32[]{:S(2)}) collective-permute-start(bf16[8,2048]{1,0:T(8,128)(2,1)S(1)} %get-tuple-element.46), channel_id=1, source_target_pairs={{64,100},{65,101},{66,102},{67,103},{68,104},{69,105},{70,106},{71... | collective-permute-start | bytes 98312 | tf_op jit(solution)/shard_map/ppermute | solution.py:36
  95.0 1.4 collective-permute-start.43
  95.7 0.7 collective-permute-start.44
  97.9 17.5 %collective-permute-start.45 = (bf16[8,2048]{1,0:T(8,128)(2,1)S(1)}, bf16[8,2048]{1,0:T(8,128)(2,1)S(1)}, u32[]{:S(2)}, u32[]{:S(2)}) collective-permute-start(bf16[8,2048]{1,0:T(8,128)(2,1)S(1)} %get-tuple-element.48), channel_id=1, source_target_pairs={{0,32},{1,33},{2,34},{3,35},{4,36},{5,37},{6,38},{7,39},{8,40},{9,... | collective-permute-start | bytes 98312 | tf_op jit(solution)/shard_map/ppermute | solution.py:36
  99.2 18.9 %collective-permute-start.46 = (bf16[8,2048]{1,0:T(8,128)(2,1)S(1)}, bf16[8,2048]{1,0:T(8,128)(2,1)S(1)}, u32[]{:S(2)}, u32[]{:S(2)}) collective-permute-start(bf16[8,2048]{1,0:T(8,128)(2,1)S(1)} %get-tuple-element.48), channel_id=1, source_target_pairs={{0,36},{1,37},{2,38},{3,39},{4,40},{5,41},{6,42},{7,43},{8,44},{9,... | collective-permute-start | bytes 98312 | tf_op jit(solution)/shard_map/ppermute | solution.py:36
  100.5 19.1 %collective-permute-start.47 = (bf16[8,2048]{1,0:T(8,128)(2,1)S(1)}, bf16[8,2048]{1,0:T(8,128)(2,1)S(1)}, u32[]{:S(2)}, u32[]{:S(2)}) collective-permute-start(bf16[8,2048]{1,0:T(8,128)(2,1)S(1)} %get-tuple-element.48), channel_id=1, source_target_pairs={{0,40},{1,41},{2,42},{3,43},{4,44},{5,45},{6,46},{7,47},{8,32},{9,... | collective-permute-start | bytes 98312 | tf_op jit(solution)/shard_map/ppermute | solution.py:36
  101.8 17.8 %collective-permute-start.48 = (bf16[8,2048]{1,0:T(8,128)(2,1)S(1)}, bf16[8,2048]{1,0:T(8,128)(2,1)S(1)}, u32[]{:S(2)}, u32[]{:S(2)}) collective-permute-start(bf16[8,2048]{1,0:T(8,128)(2,1)S(1)} %get-tuple-element.48), channel_id=1, source_target_pairs={{0,44},{1,45},{2,46},{3,47},{4,32},{5,33},{6,34},{7,35},{8,36},{9,... | collective-permute-start | bytes 98312 | tf_op jit(solution)/shard_map/ppermute | solution.py:36
  121.1 2.7 %collective-permute-start.49 = (bf16[8,2048]{1,0:T(8,128)(2,1)S(1)}, bf16[8,2048]{1,0:T(8,128)(2,1)S(1)}, u32[]{:S(2)}, u32[]{:S(2)}) collective-permute-start(bf16[8,2048]{1,0:T(8,128)(2,1)S(1)} %get-tuple-element.50), channel_id=1, source_target_pairs={{32,64},{33,65},{34,66},{35,67},{36,68},{37,69},{38,70},{39,71},{4... | collective-permute-start | bytes 98312 | tf_op jit(solution)/shard_map/ppermute | solution.py:36
  121.8 2.0 %collective-permute-start.50 = (bf16[8,2048]{1,0:T(8,128)(2,1)S(1)}, bf16[8,2048]{1,0:T(8,128)(2,1)S(1)}, u32[]{:S(2)}, u32[]{:S(2)}) collective-permute-start(bf16[8,2048]{1,0:T(8,128)(2,1)S(1)} %get-tuple-element.50), channel_id=1, source_target_pairs={{32,68},{33,69},{34,70},{35,71},{36,72},{37,73},{38,74},{39,75},{4... | collective-permute-start | bytes 98312 | tf_op jit(solution)/shard_map/ppermute | solution.py:36
  122.5 1.4 collective-permute-start.51
  123.1 0.7 collective-permute-start.52
  125.4 2.7 %collective-permute-start.53 = (bf16[8,2048]{1,0:T(8,128)(2,1)S(1)}, bf16[8,2048]{1,0:T(8,128)(2,1)S(1)}, u32[]{:S(2)}, u32[]{:S(2)}) collective-permute-start(bf16[8,2048]{1,0:T(8,128)(2,1)S(1)} %get-tuple-element.52), channel_id=1, source_target_pairs={{64,96},{65,97},{66,98},{67,99},{68,100},{69,101},{70,102},{71,103... | collective-permute-start | bytes 98312 | tf_op jit(solution)/shard_map/ppermute | solution.py:36
  126.0 2.0 %collective-permute-start.54 = (bf16[8,2048]{1,0:T(8,128)(2,1)S(1)}, bf16[8,2048]{1,0:T(8,128)(2,1)S(1)}, u32[]{:S(2)}, u32[]{:S(2)}) collective-permute-start(bf16[8,2048]{1,0:T(8,128)(2,1)S(1)} %get-tuple-element.52), channel_id=1, source_target_pairs={{64,100},{65,101},{66,102},{67,103},{68,104},{69,105},{70,106},{71... | collective-permute-start | bytes 98312 | tf_op jit(solution)/shard_map/ppermute | solution.py:36
  126.7 1.4 collective-permute-start.55
  127.4 0.7 collective-permute-start.56
  129.6 13.0 %collective-permute-start.57 = (bf16[8,2048]{1,0:T(8,128)(2,1)S(1)}, bf16[8,2048]{1,0:T(8,128)(2,1)S(1)}, u32[]{:S(2)}, u32[]{:S(2)}) collective-permute-start(bf16[8,2048]{1,0:T(8,128)(2,1)S(1)} %get-tuple-element.54), channel_id=1, source_target_pairs={{0,32},{1,33},{2,34},{3,35},{4,36},{5,37},{6,38},{7,39},{8,40},{9,... | collective-permute-start | bytes 98312 | tf_op jit(solution)/shard_map/ppermute | solution.py:36
  130.9 13.9 %collective-permute-start.58 = (bf16[8,2048]{1,0:T(8,128)(2,1)S(1)}, bf16[8,2048]{1,0:T(8,128)(2,1)S(1)}, u32[]{:S(2)}, u32[]{:S(2)}) collective-permute-start(bf16[8,2048]{1,0:T(8,128)(2,1)S(1)} %get-tuple-element.54), channel_id=1, source_target_pairs={{0,36},{1,37},{2,38},{3,39},{4,40},{5,41},{6,42},{7,43},{8,44},{9,... | collective-permute-start | bytes 98312 | tf_op jit(solution)/shard_map/ppermute | solution.py:36
  132.2 14.0 %collective-permute-start.59 = (bf16[8,2048]{1,0:T(8,128)(2,1)S(1)}, bf16[8,2048]{1,0:T(8,128)(2,1)S(1)}, u32[]{:S(2)}, u32[]{:S(2)}) collective-permute-start(bf16[8,2048]{1,0:T(8,128)(2,1)S(1)} %get-tuple-element.54), channel_id=1, source_target_pairs={{0,40},{1,41},{2,42},{3,43},{4,44},{5,45},{6,46},{7,47},{8,32},{9,... | collective-permute-start | bytes 98312 | tf_op jit(solution)/shard_map/ppermute | solution.py:36
  133.5 13.7 %collective-permute-start.60 = (bf16[8,2048]{1,0:T(8,128)(2,1)S(1)}, bf16[8,2048]{1,0:T(8,128)(2,1)S(1)}, u32[]{:S(2)}, u32[]{:S(2)}) collective-permute-start(bf16[8,2048]{1,0:T(8,128)(2,1)S(1)} %get-tuple-element.54), channel_id=1, source_target_pairs={{0,44},{1,45},{2,46},{3,47},{4,32},{5,33},{6,34},{7,35},{8,36},{9,... | collective-permute-start | bytes 98312 | tf_op jit(solution)/shard_map/ppermute | solution.py:36
  148.5 1.3 collective-permute-start.61
  (3 other events, 2.3 us)

commit v2 on v1

--- a/solution.py
+++ b/solution.py
@@ -17,6 +17,10 @@
 
 def near(value):
     return pltpu.with_memory_space_constraint(value, pltpu.VMEM)
+
+
+def far(value):
+    return pltpu.with_memory_space_constraint(value, pltpu.HBM)
 
 
 def bf16(*shape):
@@ -36,11 +40,9 @@
     return lax.ppermute(value, ("dom", "orb"), pairs)
 
 
-def ring(low, high, move):
-    low_before, high_after = move(low, 1), move(high, -1)
-    high_before, low_after = move(high, 1), move(low, -1)
-    low_far, high_far = move(low_before, 1), move(high_after, -1)
-    return [(low, high), (low_before, high_before), (low_after, high_after), (low_far, high_far)]
+def ring(value, move):
+    opposite = move(value, 2)
+    return [value, move(value, 1), move(value, -1), opposite]
 
 
 def mask_kernel(info, coupling, pattern, *refs):
@@ -71,102 +73,71 @@
         out_specs=[WHOLE] * SIDE,
         scratch_shapes=[pltpu.VMEM((rows, order), jnp.bfloat16), pltpu.SemaphoreType.DMA],
         compiler_params=pltpu.CompilerParams(vmem_limit_bytes=4 << 20),
-    )(info, coupling, pattern)
-
-
-def halves_kernel(green, after, low, high, done):
-    half = low.shape[0]
-    copies = [
-        pltpu.make_async_copy(green.at[pl.ds(at * half, half)], out, done.at[at]) for at, out in enumerate((low, high))
-    ]
-    for copy in copies:
-        copy.start()
-    for copy in copies:
-        copy.wait()
-
-
-def halves(green, after):
-    rows, order = green.shape
-    return pl.pallas_call(
-        halves_kernel,
-        out_shape=[pltpu.VMEM((rows // 2, order), jnp.bfloat16)] * 2,
-        in_specs=[pl.BlockSpec(memory_space=pltpu.HBM), pl.BlockSpec(memory_space=pl.ANY)],
-        out_specs=[WHOLE] * 2,
-        scratch_shapes=[pltpu.SemaphoreType.DMA((2,))],
-        compiler_params=pltpu.CompilerParams(vmem_limit_bytes=2 << 20),
-    )(green, after)
+    )(info, far(coupling), pattern)
 
 
 def tile_kernel(info, *refs):
-    count = 2 * SIDE
-    columns, greens = refs[:count], refs[count : 2 * count]
-    out_low, out_high, all_columns, all_greens = refs[2 * count :]
+    columns, greens = refs[:SIDE], refs[SIDE : 2 * SIDE]
+    out, all_columns, all_greens = refs[2 * SIDE + 1 :]
     core, a, b = info[0], info[1], info[2]
-    rows = columns[0].shape[0] // 2
+    rows = greens[0].shape[0]
     for at, offset in enumerate(OFFSETS):
         row_turn = lax.rem(a + (offset + SIDE), SIDE)
+        for inner in range(SIDE):
+            turn = lax.rem(b + (SIDE - inner), SIDE)
+            block = jnp.where(core == 0, SIDE * row_turn + turn, SIDE * turn + row_turn)
+            place = pl.ds(pl.multiple_of(block * rows, rows), rows)
+            all_columns[place, :] = columns[at][inner * rows : (inner + 1) * rows, :]
         green_turn = lax.rem(b + (offset + SIDE), SIDE)
-        for half in range(2):
-            for inner in range(2):
-                turn = lax.rem(b + (SIDE - 2 * half - inner), SIDE)
-                block = jnp.where(core == 0, SIDE * row_turn + turn, SIDE * turn + row_turn)
-                place = pl.ds(pl.multiple_of(block * rows, rows), rows)
-                all_columns[place, :] = columns[2 * at + half][inner * rows : (inner + 1) * rows, :]
-            part = greens[2 * at + half]
-            size = part.shape[0]
-            start = pl.multiple_of((2 * green_turn + half) * size, size)
-            all_greens[pl.ds(start, size), :] = part[...]
+        all_greens[pl.ds(pl.multiple_of(green_turn * rows, rows), rows), :] = greens[at][...]
     tile = jnp.dot(all_greens[...], all_columns[...], preferred_element_type=jnp.float32)
-    middle = tile.shape[1] // 2
-    out_low[...] = tile[:, :middle].T.astype(jnp.bfloat16)
-    out_high[...] = tile[:, middle:].T.astype(jnp.bfloat16)
-
-
-def tiled(info, columns, greens):
-    columns = [half for pair in columns for half in pair]
-    greens = [half for pair in greens for half in pair]
+    out[...] = tile.T.astype(jnp.bfloat16)
+
+
+def tiled(info, columns, greens, after):
     wide = columns[0].shape[1]
     order = greens[0].shape[1]
     return pl.pallas_call(
         tile_kernel,
-        out_shape=[bf16(wide // 2, wide)] * 2,
-        in_specs=[SCALARS] + [WHOLE] * 16,
-        out_specs=[WHOLE] * 2,
+        out_shape=pltpu.VMEM((wide, wide), jnp.bfloat16),
+        in_specs=[SCALARS] + [WHOLE] * 8 + [pl.BlockSpec(memory_space=pl.ANY)],
+        out_specs=WHOLE,
         scratch_shapes=[pltpu.VMEM((order, wide), jnp.bfloat16), pltpu.VMEM((wide, order), jnp.bfloat16)],
         compiler_params=pltpu.CompilerParams(vmem_limit_bytes=12 << 20),
-    )(info, *map(near, columns + greens))
-
-
-def arrange_kernel(info, *refs):
-    own, other, (even, odd) = refs[:8], refs[8:16], refs[16:]
+    )(info, *map(near, columns + greens), after)
+
+
+def arrange_kernel(offsets, info, *refs):
+    count = len(offsets)
+    own, other, (even, odd) = refs[:count], refs[count : 2 * count], refs[-2:]
     core, x = info[0], info[3]
-    half, wide = own[0].shape
+    wide = own[0].shape[0]
     block = wide // SIDE
 
     def arrange(from_even, from_odd):
-        for at, offset in enumerate(OFFSETS):
+        for at, offset in enumerate(offsets):
             turn = lax.rem(x + (offset + SIDE), SIDE)
-            for side in range(2):
-                even[pl.ds(pl.multiple_of(turn * wide + side * half, half), half), :] = from_even[2 * at + side][...]
-                for row in range(SIDE):
-                    place = pl.ds(pl.multiple_of((SIDE * row + turn) * block, block), block)
-                    piece = from_odd[2 * at + side][:, row * block : (row + 1) * block]
-                    odd[side * half : (side + 1) * half, place] = piece
+            even[pl.ds(pl.multiple_of(turn * wide, wide), wide), :] = from_even[at][...]
+            for row in range(SIDE):
+                place = pl.ds(pl.multiple_of((SIDE * row + turn) * block, block), block)
+                odd[:, place] = from_odd[at][:, row * block : (row + 1) * block]
 
     pl.when(core == 0)(lambda: arrange(own, other))
     pl.when(core != 0)(lambda: arrange(other, own))
 
 
-def arranged(info, own, other):
-    wide = own[0].shape[1]
+def arranged(offsets, info, own, other, so_far=()):
+    wide = own[0].shape[0]
     order = SIDE * wide
-    return pl.pallas_call(
-        arrange_kernel,
+    count = 1 + 2 * len(offsets)
+    return pl.pallas_call(
+        functools.partial(arrange_kernel, offsets),
         out_shape=[pltpu.VMEM((order, wide), jnp.bfloat16), pltpu.VMEM((wide, order), jnp.bfloat16)],
-        in_specs=[SCALARS] + [WHOLE] * 16,
+        in_specs=[SCALARS] + [WHOLE] * (count - 1 + len(so_far)),
         out_specs=[WHOLE] * 2,
+        input_output_aliases={count + at: at for at in range(len(so_far))},
         compiler_params=pltpu.CompilerParams(vmem_limit_bytes=4 << 20),
-    )(info, *map(near, own), *map(near, other))
+    )(info, *map(near, (*own, *other, *so_far)))
 
 
 def plane_kernel(at, info, state, *refs):
@@ -213,28 +184,31 @@
     along_a = lambda value, step: send(value, target=lambda z, k, y, x: (z, k, y + (1 - k) * step, x + k * step))
     to_other_core = lambda value: send(value, target=lambda z, k, y, x: (z, 1 - k, y, x))
 
-    pieces = masked_pieces(info, couplings[0], pattern[0])
-    green_low, green_high = halves(green_blocks[0], pieces[0])
-    pieces = [pieces[0]] + [along_b(pieces[offset], offset) for offset in range(1, SIDE)]
-    greens = ring(green_low, green_high, along_b)
-    columns = ring(jnp.concatenate(pieces[:2]), jnp.concatenate(pieces[2:]), along_a)
-    tile_low, tile_high = tiled(info, columns, greens)
-    own = [half for pair in ring(tile_low, tile_high, along_x) for half in pair]
-    other = [to_other_core(half) for half in own]
-    even, odd = arranged(info, own, other)
-
     order = injected.shape[1]
     wide = order // SIDE
     modes = injected.shape[0] // (SIDE * CORES)
-    by_x = sources[0].reshape(SIDE, CORES * modes, -1)
+    mine, theirs = sources[0], to_other_core(sources[0])
+    pieces = masked_pieces(info, couplings[0], pattern[0])
+    pieces = [pieces[0]] + [along_b(pieces[offset], offset) for offset in range(1, SIDE)]
+    green, *_ = lax.optimization_barrier((green_blocks[0], pieces[1]))
+    greens = ring(green, along_b)
+    columns = ring(jnp.concatenate(pieces), along_a)
+    mine, theirs, *_ = lax.optimization_barrier((mine, theirs, columns[1], columns[2]))
+    both = jnp.stack([jnp.where(first, mine, theirs), jnp.where(first, theirs, mine)])
+    both = both.reshape(CORES, SIDE, CORES, modes, -1)
+    by_x = lax.dynamic_index_in_dim(both, core, 2, keepdims=False)
     source = jnp.zeros((CORES * modes, wide), jnp.bfloat16)
     for step in range(SIDE):
-        piece = lax.dynamic_index_in_dim(by_x, (x + step) % SIDE, 0, keepdims=False)
+        piece = lax.dynamic_index_in_dim(by_x, (x + step) % SIDE, 1, keepdims=False).reshape(CORES * modes, -1)
         piece = along_x(piece, step) if step else piece
         source = lax.dynamic_update_slice(source, piece, (0, (x - step) % SIDE * (wide // SIDE)))
-    mine = jnp.where(first, source[:modes], source[modes:])
-    theirs = to_other_core(jnp.where(first, source[modes:], source[:modes]))
-    even_source, odd_source = jnp.where(first, mine, theirs), jnp.where(first, theirs, mine)
+    even_source, odd_source = source[:modes], source[modes:]
+    tile = tiled(info, columns, greens, source)
+    own = ring(tile, along_x)
+    other = [to_other_core(piece) for piece in own]
+    even, odd = arranged(OFFSETS[:3], info, own[:3], other[:3])
+    even, odd = arranged(OFFSETS[3:], info, own[3:], other[3:], (even, odd))
+
     odd_source = lax.dynamic_update_slice(jnp.zeros((modes, order), jnp.bfloat16), odd_source, (0, y * wide))
 
     start = lax.dynamic_slice_in_dim(injected, (CORES * x + core) * modes, modes, 0)
@@ -248,7 +222,7 @@
         if at + 1 < planes:
             arrived = [
                 send(odd_part, target=lambda z, k, y, x: (z + 1, k, y + turn, x) if onward(z, at) else None)
-                for turn in range(SIDE)
+                for turn in (2, 1, 3, 0)
             ]
 
     even_part = lax.dynamic_update_slice(jnp.zeros_like(odd_part), even_state, (0, y * wide))

time: 164 us -> 160 us (0.976)
  local copies, waits for them, and re-layouts: 6.01 us -> 0.9 us
  starting transfers between devices: 60.2 us -> 55.9 us
  waiting for transfers between devices: 64.1 us -> 68.2 us
    ppermute x62 -> x49, starting transfers between devices: 60.2 us -> 55.9 us  [sent(): return lax.ppermute(value, ('dom', 'orb'), pairs)]
    ppermute x62 -> x49, waiting for transfers between devices: 64.1 us -> 68.2 us  [sent(): return lax.ppermute(value, ('dom', 'orb'), pairs)]
    unnamed x12 -> x7, local copies, waits for them, and re-layouts: 4.44 us -> 0.76 us
  transfers between devices with their start and end apart: 62 -> 49, of which waited for: 26 -> 22; matrix products, arithmetic and copies ran while one was open for 1% -> 1% of each run, Pallas kernels for 2% -> 1%
where the time goes in v2:
time: 160 us; the launch traced here: 159 us
  waiting for transfers between devices  68.2 us (43%)
  starting transfers between devices  55.9 us (35%)
  Pallas kernels  18.2 us (11%)
  blocking collectives  13.1 us (8%)
  other arithmetic  2.16 us (1%)
    ppermute x49, waiting for transfers between devices, sent(): return lax.ppermute(value, ('dom', 'orb'), pairs)  68.2 us
    ppermute x49, starting transfers between devices, sent(): return lax.ppermute(value, ('dom', 'orb'), pairs)  55.9 us
    all_to_all x1, blocking collectives, on_device(): parts = lax.all_to_all(both, 'orb', 0, 0, tiled=True)  13.1 us
    pallas_call x8, Pallas kernels, through_plane(): pl.pallas_call(functools.partial(plane_kernel, at), out_shape=[pltpu.VMEM...  12 us
  transfers between devices with their start and end apart: 49, of which 22 were waited for; matrix products, arithmetic and copies ran while one was open for 1% of the time, Pallas kernels for 1%

profile of v2, /device:TPU:224, one launch (start us, length us, event | category | flops | bytes accessed | tf_op | source)
XLA Modules:
  0.0 159.0 jit_solution(16963474218046978376)
XLA Ops:
  0.1 0.7 copy-done.1
  0.8 1.7 %shard_map.55 = (bf16[128,512]{1,0:T(8,128)(2,1)S(1)}, bf16[128,512]{1,0:T(8,128)(2,1)S(1)}, bf16[128,512]{1,0:T(8,128)(2,1)S(1)}, bf16[128,512]{1,0:T(8,128)(2,1)S(1)}) custom-call(s32[6]{0:T(128)S(1)} %stack.36.info, bf16[128,2048]{1,0:T(8,128)(2,1)} %bitcast.38, s32[2,32]{1,0:T(2,128)S(1)} %bitcast.37), custom_call_target="tpu_custom_call" | custom-call | tf_op jit(solution)/shard_map/pallas_call | solution.py:69
  2.5 1.6 collective-permute-start.1
  4.1 2.7 %collective-permute-start.2 = (bf16[128,512]{1,0:T(8,128)(2,1)S(1)}, bf16[128,512]{1,0:T(8,128)(2,1)S(1)}, u32[]{:S(2)}, u32[]{:S(2)}) collective-permute-start(bf16[128,512]{1,0:T(8,128)(2,1)S(1)} %get-tuple-element.34), channel_id=1, source_target_pairs={{0,2},{1,3},{2,0},{3,1},{4,6},{5,7},{6,4},{7,5},{8,10},{9,11},{10,... | collective-permute-start | bytes 393224 | tf_op jit(solution)/shard_map/ppermute | solution.py:40
  6.8 1.4 collective-permute-start.3
  8.8 2.4 %collective-permute-done.2 = bf16[128,512]{1,0:T(8,128)(2,1)S(1)} collective-permute-done((bf16[128,512]{1,0:T(8,128)(2,1)S(1)}, bf16[128,512]{1,0:T(8,128)(2,1)S(1)}, u32[]{:S(2)}, u32[]{:S(2)}) %collective-permute-start.2) | collective-permute-done | bytes 131104 | tf_op jit(solution)/shard_map/ppermute | solution.py:40
  11.8 1.7 %collective-permute-start.4 = (bf16[512,512]{1,0:T(8,128)(2,1)S(1)}, bf16[512,512]{1,0:T(8,128)(2,1)S(1)}, u32[]{:S(2)}, u32[]{:S(2)}) collective-permute-start(bf16[512,512]{1,0:T(8,128)(2,1)S(1)} %constant_dynamic-update-slice_fusion.refs_0_), channel_id=1, source_target_pairs={{0,4},{1,5},{2,6},{3,7},{4,8},{5,9},{6,10},{7,11},{8,12},{9,13},{1... | collective-permute-start | bytes 1572872 | tf_op jit(solution)/shard_map/ppermute | solution.py:40
  13.4 1.7 %collective-permute-start.5 = (bf16[512,512]{1,0:T(8,128)(2,1)S(1)}, bf16[512,512]{1,0:T(8,128)(2,1)S(1)}, u32[]{:S(2)}, u32[]{:S(2)}) collective-permute-start(bf16[512,512]{1,0:T(8,128)(2,1)S(1)} %constant_dynamic-update-slice_fusion.refs_0_), channel_id=1, source_target_pairs={{0,12},{1,13},{2,14},{3,15},{4,0},{5,1},{6,2},{7,3},{8,4},{9,5},{1... | collective-permute-start | bytes 1572872 | tf_op jit(solution)/shard_map/ppermute | solution.py:40
  15.1 2.0 %collective-permute-start.9 = (bf16[512,512]{1,0:T(8,128)(2,1)S(1)}, bf16[512,512]{1,0:T(8,128)(2,1)S(1)}, u32[]{:S(2)}, u32[]{:S(2)}) collective-permute-start(bf16[512,512]{1,0:T(8,128)(2,1)S(1)} %constant_dynamic-update-slice_fusion.refs_0_), channel_id=1, source_target_pairs={{0,8},{1,9},{2,10},{3,11},{4,12},{5,13},{6,14},{7,15},{8,0},{9,1},... | collective-permute-start | bytes 1572872 | tf_op jit(solution)/shard_map/ppermute | solution.py:40
  17.1 1.3 collective-permute-start.10
  18.4 2.0 %collective-permute-start.11 = (bf16[128,2048]{1,0:T(8,128)(2,1)}, bf16[128,2048]{1,0:T(8,128)(2,1)S(1)}, u32[]{:S(2)}, u32[]{:S(2)}) collective-permute-start(bf16[128,2048]{1,0:T(8,128)(2,1)} %bitcast.34), channel_id=1, source_target_pairs={{0,3},{1,0},{2,1},{3,2},{4,7},{5,4},{6,5},{7,6},{8,11},{9,8},{10,9... | collective-permute-start | bytes 1572872 | tf_op jit(solution)/shard_map/ppermute | solution.py:40
  20.3 2.4 %collective-permute-done.4.refs_1_ = bf16[512,512]{1,0:T(8,128)(2,1)S(1)} collective-permute-done((bf16[512,512]{1,0:T(8,128)(2,1)S(1)}, bf16[512,512]{1,0:T(8,128)(2,1)S(1)}, u32[]{:S(2)}, u32[]{:S(2)}) %collective-permute-start.4) | collective-permute-done | bytes 524320 | tf_op jit(solution)/shard_map/ppermute | solution.py:40
  22.8 3.4 %collective-permute-start.12 = (bf16[128,2048]{1,0:T(8,128)(2,1)}, bf16[128,2048]{1,0:T(8,128)(2,1)S(1)}, u32[]{:S(2)}, u32[]{:S(2)}) collective-permute-start(bf16[128,2048]{1,0:T(8,128)(2,1)} %bitcast.35), channel_id=1, source_target_pairs={{0,2},{1,3},{2,0},{3,1},{4,6},{5,7},{6,4},{7,5},{8,10},{9,11},{10,... | collective-permute-start | bytes 1572872 | tf_op jit(solution)/shard_map/ppermute | solution.py:40
  26.2 0.7 broadcast_select_fusion.5
  26.9 1.2 collective-permute-start.6
  28.1 7.0 %collective-permute-done.6 = bf16[16,128]{1,0:T(8,128)(2,1)S(1)} collective-permute-done((bf16[16,128]{1,0:T(8,128)(2,1)S(1)}, bf16[16,128]{1,0:T(8,128)(2,1)S(1)}, u32[]{:S(2)}, u32[]{:S(2)}) %collective-permute-start.6) | collective-permute-done | bytes 4128 | tf_op jit(solution)/shard_map/ppermute | solution.py:40
  35.1 2.4 %collective-permute-start.7 = (bf16[16,128]{1,0:T(8,128)(2,1)S(1)}, bf16[16,128]{1,0:T(8,128)(2,1)S(1)}, u32[]{:S(2)}, u32[]{:S(2)}) collective-permute-start(bf16[16,128]{1,0:T(8,128)(2,1)S(1)} %get-tuple-element.63), channel_id=1, source_target_pairs={{0,2},{1,3},{2,0},{3,1},{4,6},{5,7},{6,4},{7,5},{8,10},{9,11},{10,... | collective-permute-start | bytes 12296 | tf_op jit(solution)/shard_map/ppermute | solution.py:40
  37.5 2.7 %collective-permute-done.7 = bf16[16,128]{1,0:T(8,128)(2,1)S(1)} collective-permute-done((bf16[16,128]{1,0:T(8,128)(2,1)S(1)}, bf16[16,128]{1,0:T(8,128)(2,1)S(1)}, u32[]{:S(2)}, u32[]{:S(2)}) %collective-permute-start.7) | collective-permute-done | bytes 4128 | tf_op jit(solution)/shard_map/ppermute | solution.py:40
  40.2 3.4 %collective-permute-start.8 = (bf16[16,128]{1,0:T(8,128)(2,1)S(1)}, bf16[16,128]{1,0:T(8,128)(2,1)S(1)}, u32[]{:S(2)}, u32[]{:S(2)}) collective-permute-start(bf16[16,128]{1,0:T(8,128)(2,1)S(1)} %get-tuple-element.61), channel_id=1, source_target_pairs={{0,3},{1,0},{2,1},{3,2},{4,7},{5,4},{6,5},{7,6},{8,11},{9,8},{10,9... | collective-permute-start | bytes 12296 | tf_op jit(solution)/shard_map/ppermute | solution.py:40
  43.6 1.3 collective-permute-done.8
  45.0 2.0 %shard_map.56.refs_0_ = bf16[512,512]{1,0:T(8,128)(2,1)S(1)} custom-call(s32[6]{0:T(128)S(1)} %stack.36.info, bf16[512,512]{1,0:T(8,128)(2,1)S(1)} %constant_dynamic-update-slice_fusion.refs_0_, bf16[512,512]{1,0:T(8,128)(2,1)S(1)} %collective-permute-done.4.refs_1_, bf16[512,512]{1,0:T(8,128)(2,1)S(1)} %collective-permute-done.5.refs_2_, ...), custom_call_target="tpu_custom_call" | custom-call | tf_op jit(solution)/shard_map/pallas_call | solution.py:100
  47.0 1.4 collective-permute-start.15
  48.4 2.3 %collective-permute-start.16 = (bf16[512,512]{1,0:T(8,128)(2,1)S(1)}, bf16[512,512]{1,0:T(8,128)(2,1)S(1)}, u32[]{:S(2)}, u32[]{:S(2)}) collective-permute-start(bf16[512,512]{1,0:T(8,128)(2,1)S(1)} %shard_map.56.refs_0_), channel_id=1, source_target_pairs={{0,3},{1,0},{2,1},{3,2},{4,7},{5,4},{6,5},{7,6},{8,11},{9,8},{10,9... | collective-permute-start | bytes 1572872 | tf_op jit(solution)/shard_map/ppermute | solution.py:40
  50.7 1.4 collective-permute-start.13
  52.0 11.3 %collective-permute-done.15.refs_1_ = bf16[512,512]{1,0:T(8,128)(2,1)S(1)} collective-permute-done((bf16[512,512]{1,0:T(8,128)(2,1)S(1)}, bf16[512,512]{1,0:T(8,128)(2,1)S(1)}, u32[]{:S(2)}, u32[]{:S(2)}) %collective-permute-start.15) | collective-permute-done | bytes 524320 | tf_op jit(solution)/shard_map/ppermute | solution.py:40
  63.4 4.6 %collective-permute-done.16.refs_2_ = bf16[512,512]{1,0:T(8,128)(2,1)S(1)} collective-permute-done((bf16[512,512]{1,0:T(8,128)(2,1)S(1)}, bf16[512,512]{1,0:T(8,128)(2,1)S(1)}, u32[]{:S(2)}, u32[]{:S(2)}) %collective-permute-start.16) | collective-permute-done | bytes 524320 | tf_op jit(solution)/shard_map/ppermute | solution.py:40
  68.0 1.6 collective-permute-done.13.refs_0_
  69.6 0.8 dynamic-slice_select_fusion.state
  70.4 1.1 shard_map.57
  71.8 1.4 shard_map.58
  73.2 1.5 shard_map.59
  74.8 1.3 collective-permute-start.20
  76.1 1.3 collective-permute-start.21
  77.4 1.3 collective-permute-start.22
  78.7 1.3 collective-permute-start.23
  80.0 3.0 %collective-permute-done.20.refs_0_ = bf16[8,2048]{1,0:T(8,128)(2,1)S(1)} collective-permute-done((bf16[8,2048]{1,0:T(8,128)(2,1)S(1)}, bf16[8,2048]{1,0:T(8,128)(2,1)S(1)}, u32[]{:S(2)}, u32[]{:S(2)}) %collective-permute-start.20) | collective-permute-done | bytes 32800 | tf_op jit(solution)/shard_map/ppermute | solution.py:40
  83.0 2.1 %collective-permute-done.21.refs_1_ = bf16[8,2048]{1,0:T(8,128)(2,1)S(1)} collective-permute-done((bf16[8,2048]{1,0:T(8,128)(2,1)S(1)}, bf16[8,2048]{1,0:T(8,128)(2,1)S(1)}, u32[]{:S(2)}, u32[]{:S(2)}) %collective-permute-start.21) | collective-permute-done | bytes 32800 | tf_op jit(solution)/shard_map/ppermute | solution.py:40
  85.1 0.8 collective-permute-done.23.refs_3_
  85.9 1.5 shard_map.60
  88.1 0.7 collective-permute-start.25
  88.8 0.7 collective-permute-start.26
  90.1 1.5 shard_map.61
  92.3 0.7 collective-permute-start.29
  94.4 1.5 shard_map.62
  95.9 1.3 collective-permute-start.32
  97.2 1.3 collective-permute-start.33
  98.5 1.3 collective-permute-start.34
  99.8 1.3 collective-permute-start.35
  101.1 12.5 %collective-permute-done.32.refs_0_ = bf16[8,2048]{1,0:T(8,128)(2,1)S(1)} collective-permute-done((bf16[8,2048]{1,0:T(8,128)(2,1)S(1)}, bf16[8,2048]{1,0:T(8,128)(2,1)S(1)}, u32[]{:S(2)}, u32[]{:S(2)}) %collective-permute-start.32) | collective-permute-done | bytes 32800 | tf_op jit(solution)/shard_map/ppermute | solution.py:40
  113.6 1.8 %collective-permute-done.33.refs_1_ = bf16[8,2048]{1,0:T(8,128)(2,1)S(1)} collective-permute-done((bf16[8,2048]{1,0:T(8,128)(2,1)S(1)}, bf16[8,2048]{1,0:T(8,128)(2,1)S(1)}, u32[]{:S(2)}, u32[]{:S(2)}) %collective-permute-start.33) | collective-permute-done | bytes 32800 | tf_op jit(solution)/shard_map/ppermute | solution.py:40
  115.9 1.5 shard_map.63
  120.1 1.5 shard_map.64
  124.4 1.5 shard_map.65
  125.9 1.3 collective-permute-start.44
  127.2 1.3 collective-permute-start.45
  128.5 1.3 collective-permute-start.46
  129.8 1.3 collective-permute-start.47
  131.1 8.5 %collective-permute-done.44.refs_0_ = bf16[8,2048]{1,0:T(8,128)(2,1)S(1)} collective-permute-done((bf16[8,2048]{1,0:T(8,128)(2,1)S(1)}, bf16[8,2048]{1,0:T(8,128)(2,1)S(1)}, u32[]{:S(2)}, u32[]{:S(2)}) %collective-permute-start.44) | collective-permute-done | bytes 32800 | tf_op jit(solution)/shard_map/ppermute | solution.py:40
  139.6 1.2 collective-permute-done.45.refs_1_
  140.8 0.8 collective-permute-done.46.refs_2_
  141.6 1.0 collective-permute-done.47.refs_3_
  142.6 1.3 shard_map.66
  144.1 1.2 collective-permute-done.48
  145.3 13.1 %all_to_all.5 = bf16[16,16,128]{2,1,0:T(8,128)(2,1)S(1)} all-to-all(bf16[16,16,128]{2,1,0:T(8,128)(2,1)S(1)} %bitcast_bitcast_fusion), channel_id=1, replica_groups=mesh['dom'=16,'orb'=16] {'orb'}, dimensions={0} | all-to-all | bytes 131072 | tf_op jit(solution)/shard_map/all_to_all | solution.py:233
  (72 shorter events, 11.5 us)
Async XLA Ops:
  0.0 45.0 %copy-start = (bf16[1,128,2048]{2,1,0:T(8,128)(2,1)S(1)}, bf16[1,128,2048]{2,1,0:T(8,128)(2,1)}, u32[]{:S(2)}) copy-start(bf16[1,128,2048]{2,1,0:T(8,128)(2,1)} %param.5) | copy-start | bytes 1572868
  0.1 0.7 copy-start.1
  2.5 6.3 %collective-permute-start.1 = (bf16[128,512]{1,0:T(8,128)(2,1)S(1)}, bf16[128,512]{1,0:T(8,128)(2,1)S(1)}, u32[]{:S(2)}, u32[]{:S(2)}) collective-permute-start(bf16[128,512]{1,0:T(8,128)(2,1)S(1)} %get-tuple-element.33), channel_id=1, source_target_pairs={{0,1},{1,2},{2,3},{3,0},{4,5},{5,6},{6,7},{7,4},{8,9},{9,10},{10,1... | collective-permute-start | bytes 393224 | tf_op jit(solution)/shard_map/ppermute | solution.py:40
  4.1 7.1 %collective-permute-start.2 = (bf16[128,512]{1,0:T(8,128)(2,1)S(1)}, bf16[128,512]{1,0:T(8,128)(2,1)S(1)}, u32[]{:S(2)}, u32[]{:S(2)}) collective-permute-start(bf16[128,512]{1,0:T(8,128)(2,1)S(1)} %get-tuple-element.34), channel_id=1, source_target_pairs={{0,2},{1,3},{2,0},{3,1},{4,6},{5,7},{6,4},{7,5},{8,10},{9,11},{10,... | collective-permute-start | bytes 393224 | tf_op jit(solution)/shard_map/ppermute | solution.py:40
  6.8 5.0 %collective-permute-start.3 = (bf16[128,512]{1,0:T(8,128)(2,1)S(1)}, bf16[128,512]{1,0:T(8,128)(2,1)S(1)}, u32[]{:S(2)}, u32[]{:S(2)}) collective-permute-start(bf16[128,512]{1,0:T(8,128)(2,1)S(1)} %get-tuple-element.35), channel_id=1, source_target_pairs={{0,3},{1,0},{2,1},{3,2},{4,7},{5,4},{6,5},{7,6},{8,11},{9,8},{10,9... | collective-permute-start | bytes 393224 | tf_op jit(solution)/shard_map/ppermute | solution.py:40
  11.8 11.0 %collective-permute-start.4 = (bf16[512,512]{1,0:T(8,128)(2,1)S(1)}, bf16[512,512]{1,0:T(8,128)(2,1)S(1)}, u32[]{:S(2)}, u32[]{:S(2)}) collective-permute-start(bf16[512,512]{1,0:T(8,128)(2,1)S(1)} %constant_dynamic-update-slice_fusion.refs_0_), channel_id=1, source_target_pairs={{0,4},{1,5},{2,6},{3,7},{4,8},{5,9},{6,10},{7,11},{8,12},{9,13},{1... | collective-permute-start | bytes 1572872 | tf_op jit(solution)/shard_map/ppermute | solution.py:40
  13.4 12.8 %collective-permute-start.5 = (bf16[512,512]{1,0:T(8,128)(2,1)S(1)}, bf16[512,512]{1,0:T(8,128)(2,1)S(1)}, u32[]{:S(2)}, u32[]{:S(2)}) collective-permute-start(bf16[512,512]{1,0:T(8,128)(2,1)S(1)} %constant_dynamic-update-slice_fusion.refs_0_), channel_id=1, source_target_pairs={{0,12},{1,13},{2,14},{3,15},{4,0},{5,1},{6,2},{7,3},{8,4},{9,5},{1... | collective-permute-start | bytes 1572872 | tf_op jit(solution)/shard_map/ppermute | solution.py:40
  15.1 3.3 %collective-permute-start = (bf16[64,128]{1,0:T(8,128)(2,1)}, bf16[64,128]{1,0:T(8,128)(2,1)S(1)}, u32[]{:S(2)}, u32[]{:S(2)}) collective-permute-start(bf16[64,128]{1,0:T(8,128)(2,1)} %bitcast.44), channel_id=1, source_target_pairs={{0,16},{1,17},{2,18},{3,19},{4,20},{5,21},{6,22},{7,23},{8,24},{9,... | collective-permute-start | bytes 49160 | tf_op jit(solution)/shard_map/ppermute | solution.py:40
  15.1 29.8 %collective-permute-start.9 = (bf16[512,512]{1,0:T(8,128)(2,1)S(1)}, bf16[512,512]{1,0:T(8,128)(2,1)S(1)}, u32[]{:S(2)}, u32[]{:S(2)}) collective-permute-start(bf16[512,512]{1,0:T(8,128)(2,1)S(1)} %constant_dynamic-update-slice_fusion.refs_0_), channel_id=1, source_target_pairs={{0,8},{1,9},{2,10},{3,11},{4,12},{5,13},{6,14},{7,15},{8,0},{9,1},... | collective-permute-start | bytes 1572872 | tf_op jit(solution)/shard_map/ppermute | solution.py:40
  17.1 27.9 %collective-permute-start.10 = (bf16[128,2048]{1,0:T(8,128)(2,1)}, bf16[128,2048]{1,0:T(8,128)(2,1)S(1)}, u32[]{:S(2)}, u32[]{:S(2)}) collective-permute-start(bf16[128,2048]{1,0:T(8,128)(2,1)} %bitcast.33), channel_id=1, source_target_pairs={{0,1},{1,2},{2,3},{3,0},{4,5},{5,6},{6,7},{7,4},{8,9},{9,10},{10,1... | collective-permute-start | bytes 1572872 | tf_op jit(solution)/shard_map/ppermute | solution.py:40
  18.4 26.6 %collective-permute-start.11 = (bf16[128,2048]{1,0:T(8,128)(2,1)}, bf16[128,2048]{1,0:T(8,128)(2,1)S(1)}, u32[]{:S(2)}, u32[]{:S(2)}) collective-permute-start(bf16[128,2048]{1,0:T(8,128)(2,1)} %bitcast.34), channel_id=1, source_target_pairs={{0,3},{1,0},{2,1},{3,2},{4,7},{5,4},{6,5},{7,6},{8,11},{9,8},{10,9... | collective-permute-start | bytes 1572872 | tf_op jit(solution)/shard_map/ppermute | solution.py:40
  22.8 22.2 %collective-permute-start.12 = (bf16[128,2048]{1,0:T(8,128)(2,1)}, bf16[128,2048]{1,0:T(8,128)(2,1)S(1)}, u32[]{:S(2)}, u32[]{:S(2)}) collective-permute-start(bf16[128,2048]{1,0:T(8,128)(2,1)} %bitcast.35), channel_id=1, source_target_pairs={{0,2},{1,3},{2,0},{3,1},{4,6},{5,7},{6,4},{7,5},{8,10},{9,11},{10,... | collective-permute-start | bytes 1572872 | tf_op jit(solution)/shard_map/ppermute | solution.py:40
  26.9 8.1 %collective-permute-start.6 = (bf16[16,128]{1,0:T(8,128)(2,1)S(1)}, bf16[16,128]{1,0:T(8,128)(2,1)S(1)}, u32[]{:S(2)}, u32[]{:S(2)}) collective-permute-start(bf16[16,128]{1,0:T(8,128)(2,1)S(1)} %get-tuple-element.62), channel_id=1, source_target_pairs={{0,1},{1,2},{2,3},{3,0},{4,5},{5,6},{6,7},{7,4},{8,9},{9,10},{10,1... | collective-permute-start | bytes 12296 | tf_op jit(solution)/shard_map/ppermute | solution.py:40
  35.1 5.1 %collective-permute-start.7 = (bf16[16,128]{1,0:T(8,128)(2,1)S(1)}, bf16[16,128]{1,0:T(8,128)(2,1)S(1)}, u32[]{:S(2)}, u32[]{:S(2)}) collective-permute-start(bf16[16,128]{1,0:T(8,128)(2,1)S(1)} %get-tuple-element.63), channel_id=1, source_target_pairs={{0,2},{1,3},{2,0},{3,1},{4,6},{5,7},{6,4},{7,5},{8,10},{9,11},{10,... | collective-permute-start | bytes 12296 | tf_op jit(solution)/shard_map/ppermute | solution.py:40
  40.2 4.7 %collective-permute-start.8 = (bf16[16,128]{1,0:T(8,128)(2,1)S(1)}, bf16[16,128]{1,0:T(8,128)(2,1)S(1)}, u32[]{:S(2)}, u32[]{:S(2)}) collective-permute-start(bf16[16,128]{1,0:T(8,128)(2,1)S(1)} %get-tuple-element.61), channel_id=1, source_target_pairs={{0,3},{1,0},{2,1},{3,2},{4,7},{5,4},{6,5},{7,6},{8,11},{9,8},{10,9... | collective-permute-start | bytes 12296 | tf_op jit(solution)/shard_map/ppermute | solution.py:40
  47.0 16.3 %collective-permute-start.15 = (bf16[512,512]{1,0:T(8,128)(2,1)S(1)}, bf16[512,512]{1,0:T(8,128)(2,1)S(1)}, u32[]{:S(2)}, u32[]{:S(2)}) collective-permute-start(bf16[512,512]{1,0:T(8,128)(2,1)S(1)} %shard_map.56.refs_0_), channel_id=1, source_target_pairs={{0,1},{1,2},{2,3},{3,0},{4,5},{5,6},{6,7},{7,4},{8,9},{9,10},{10,1... | collective-permute-start | bytes 1572872 | tf_op jit(solution)/shard_map/ppermute | solution.py:40
  48.4 19.6 %collective-permute-start.16 = (bf16[512,512]{1,0:T(8,128)(2,1)S(1)}, bf16[512,512]{1,0:T(8,128)(2,1)S(1)}, u32[]{:S(2)}, u32[]{:S(2)}) collective-permute-start(bf16[512,512]{1,0:T(8,128)(2,1)S(1)} %shard_map.56.refs_0_), channel_id=1, source_target_pairs={{0,3},{1,0},{2,1},{3,2},{4,7},{5,4},{6,5},{7,6},{8,11},{9,8},{10,9... | collective-permute-start | bytes 1572872 | tf_op jit(solution)/shard_map/ppermute | solution.py:40
  50.7 18.9 %collective-permute-start.13 = (bf16[512,512]{1,0:T(8,128)(2,1)S(1)}, bf16[512,512]{1,0:T(8,128)(2,1)}, u32[]{:S(2)}, u32[]{:S(2)}) collective-permute-start(bf16[512,512]{1,0:T(8,128)(2,1)S(1)} %shard_map.56.refs_0_), channel_id=1, source_target_pairs={{0,2},{1,3},{2,0},{3,1},{4,6},{5,7},{6,4},{7,5},{8,10},{9,11},{10,... | collective-permute-start | bytes 1572872 | tf_op jit(solution)/shard_map/ppermute | solution.py:40
  52.0 18.3 %collective-permute-start.17 = (bf16[512,512]{1,0:T(8,128)(2,1)S(1)}, bf16[512,512]{1,0:T(8,128)(2,1)S(1)}, u32[]{:S(2)}, u32[]{:S(2)}) collective-permute-start(bf16[512,512]{1,0:T(8,128)(2,1)S(1)} %shard_map.56.refs_0_), channel_id=1, source_target_pairs={{0,16},{1,17},{2,18},{3,19},{4,20},{5,21},{6,22},{7,23},{8,24},{9,... | collective-permute-start | bytes 1572872 | tf_op jit(solution)/shard_map/ppermute | solution.py:40
  63.4 7.0 %collective-permute-start.18 = (bf16[512,512]{1,0:T(8,128)(2,1)S(1)}, bf16[512,512]{1,0:T(8,128)(2,1)S(1)}, u32[]{:S(2)}, u32[]{:S(2)}) collective-permute-start(bf16[512,512]{1,0:T(8,128)(2,1)S(1)} %collective-permute-done.15.refs_1_), channel_id=1, source_target_pairs={{0,16},{1,17},{2,18},{3,19},{4,20},{5,21},{6,22},{7,23},{8,24},{9,... | collective-permute-start | bytes 1572872 | tf_op jit(solution)/shard_map/ppermute | solution.py:40
  68.0 2.4 %collective-permute-start.19 = (bf16[512,512]{1,0:T(8,128)(2,1)S(1)}, bf16[512,512]{1,0:T(8,128)(2,1)S(1)}, u32[]{:S(2)}, u32[]{:S(2)}) collective-permute-start(bf16[512,512]{1,0:T(8,128)(2,1)S(1)} %collective-permute-done.16.refs_2_), channel_id=1, source_target_pairs={{0,16},{1,17},{2,18},{3,19},{4,20},{5,21},{6,22},{7,23},{8,24},{9,... | collective-permute-start | bytes 1572872 | tf_op jit(solution)/shard_map/ppermute | solution.py:40
  69.6 2.3 %collective-permute-start.14 = (bf16[512,512]{1,0:T(8,128)(2,1)}, bf16[512,512]{1,0:T(8,128)(2,1)}, u32[]{:S(2)}, u32[]{:S(2)}) collective-permute-start(bf16[512,512]{1,0:T(8,128)(2,1)} %collective-permute-done.13.refs_0_), channel_id=1, source_target_pairs={{0,16},{1,17},{2,18},{3,19},{4,20},{5,21},{6,22},{7,23},{8,24},{9,... | collective-permute-start | bytes 1572872 | tf_op jit(solution)/shard_map/ppermute | solution.py:40
  74.8 8.2 %collective-permute-start.20 = (bf16[8,2048]{1,0:T(8,128)(2,1)S(1)}, bf16[8,2048]{1,0:T(8,128)(2,1)S(1)}, u32[]{:S(2)}, u32[]{:S(2)}) collective-permute-start(bf16[8,2048]{1,0:T(8,128)(2,1)S(1)} %get-tuple-element.44), channel_id=1, source_target_pairs={{0,40},{1,41},{2,42},{3,43},{4,44},{5,45},{6,46},{7,47},{8,32},{9,... | collective-permute-start | bytes 98312 | tf_op jit(solution)/shard_map/ppermute | solution.py:40
  76.1 9.0 %collective-permute-start.21 = (bf16[8,2048]{1,0:T(8,128)(2,1)S(1)}, bf16[8,2048]{1,0:T(8,128)(2,1)S(1)}, u32[]{:S(2)}, u32[]{:S(2)}) collective-permute-start(bf16[8,2048]{1,0:T(8,128)(2,1)S(1)} %get-tuple-element.44), channel_id=1, source_target_pairs={{0,36},{1,37},{2,38},{3,39},{4,40},{5,41},{6,42},{7,43},{8,44},{9,... | collective-permute-start | bytes 98312 | tf_op jit(solution)/shard_map/ppermute | solution.py:40
  77.4 7.7 %collective-permute-start.22 = (bf16[8,2048]{1,0:T(8,128)(2,1)S(1)}, bf16[8,2048]{1,0:T(8,128)(2,1)S(1)}, u32[]{:S(2)}, u32[]{:S(2)}) collective-permute-start(bf16[8,2048]{1,0:T(8,128)(2,1)S(1)} %get-tuple-element.44), channel_id=1, source_target_pairs={{0,44},{1,45},{2,46},{3,47},{4,32},{5,33},{6,34},{7,35},{8,36},{9,... | collective-permute-start | bytes 98312 | tf_op jit(solution)/shard_map/ppermute | solution.py:40
  78.7 7.2 %collective-permute-start.23 = (bf16[8,2048]{1,0:T(8,128)(2,1)S(1)}, bf16[8,2048]{1,0:T(8,128)(2,1)S(1)}, u32[]{:S(2)}, u32[]{:S(2)}) collective-permute-start(bf16[8,2048]{1,0:T(8,128)(2,1)S(1)} %get-tuple-element.44), channel_id=1, source_target_pairs={{0,32},{1,33},{2,34},{3,35},{4,36},{5,37},{6,38},{7,39},{8,40},{9,... | collective-permute-start | bytes 98312 | tf_op jit(solution)/shard_map/ppermute | solution.py:40
  87.4 2.7 %collective-permute-start.24 = (bf16[8,2048]{1,0:T(8,128)(2,1)S(1)}, bf16[8,2048]{1,0:T(8,128)(2,1)S(1)}, u32[]{:S(2)}, u32[]{:S(2)}) collective-permute-start(bf16[8,2048]{1,0:T(8,128)(2,1)S(1)} %get-tuple-element.46), channel_id=1, source_target_pairs={{32,72},{33,73},{34,74},{35,75},{36,76},{37,77},{38,78},{39,79},{4... | collective-permute-start | bytes 98312 | tf_op jit(solution)/shard_map/ppermute | solution.py:40
  88.1 2.0 %collective-permute-start.25 = (bf16[8,2048]{1,0:T(8,128)(2,1)S(1)}, bf16[8,2048]{1,0:T(8,128)(2,1)S(1)}, u32[]{:S(2)}, u32[]{:S(2)}) collective-permute-start(bf16[8,2048]{1,0:T(8,128)(2,1)S(1)} %get-tuple-element.46), channel_id=1, source_target_pairs={{32,68},{33,69},{34,70},{35,71},{36,72},{37,73},{38,74},{39,75},{4... | collective-permute-start | bytes 98312 | tf_op jit(solution)/shard_map/ppermute | solution.py:40
  88.8 1.4 collective-permute-start.26
  89.4 0.7 collective-permute-start.27
  91.7 2.7 %collective-permute-start.28 = (bf16[8,2048]{1,0:T(8,128)(2,1)S(1)}, bf16[8,2048]{1,0:T(8,128)(2,1)S(1)}, u32[]{:S(2)}, u32[]{:S(2)}) collective-permute-start(bf16[8,2048]{1,0:T(8,128)(2,1)S(1)} %get-tuple-element.48), channel_id=1, source_target_pairs={{64,104},{65,105},{66,106},{67,107},{68,108},{69,109},{70,110},{71... | collective-permute-start | bytes 98312 | tf_op jit(solution)/shard_map/ppermute | solution.py:40
  92.3 2.0 %collective-permute-start.29 = (bf16[8,2048]{1,0:T(8,128)(2,1)S(1)}, bf16[8,2048]{1,0:T(8,128)(2,1)S(1)}, u32[]{:S(2)}, u32[]{:S(2)}) collective-permute-start(bf16[8,2048]{1,0:T(8,128)(2,1)S(1)} %get-tuple-element.48), channel_id=1, source_target_pairs={{64,100},{65,101},{66,102},{67,103},{68,104},{69,105},{70,106},{71... | collective-permute-start | bytes 98312 | tf_op jit(solution)/shard_map/ppermute | solution.py:40
  93.0 1.4 collective-permute-start.30
  93.7 0.7 collective-permute-start.31
  95.9 17.7 %collective-permute-start.32 = (bf16[8,2048]{1,0:T(8,128)(2,1)S(1)}, bf16[8,2048]{1,0:T(8,128)(2,1)S(1)}, u32[]{:S(2)}, u32[]{:S(2)}) collective-permute-start(bf16[8,2048]{1,0:T(8,128)(2,1)S(1)} %get-tuple-element.50), channel_id=1, source_target_pairs={{0,40},{1,41},{2,42},{3,43},{4,44},{5,45},{6,46},{7,47},{8,32},{9,... | collective-permute-start | bytes 98312 | tf_op jit(solution)/shard_map/ppermute | solution.py:40
  97.2 18.2 %collective-permute-start.33 = (bf16[8,2048]{1,0:T(8,128)(2,1)S(1)}, bf16[8,2048]{1,0:T(8,128)(2,1)S(1)}, u32[]{:S(2)}, u32[]{:S(2)}) collective-permute-start(bf16[8,2048]{1,0:T(8,128)(2,1)S(1)} %get-tuple-element.50), channel_id=1, source_target_pairs={{0,36},{1,37},{2,38},{3,39},{4,40},{5,41},{6,42},{7,43},{8,44},{9,... | collective-permute-start | bytes 98312 | tf_op jit(solution)/shard_map/ppermute | solution.py:40
  98.5 16.9 %collective-permute-start.34 = (bf16[8,2048]{1,0:T(8,128)(2,1)S(1)}, bf16[8,2048]{1,0:T(8,128)(2,1)S(1)}, u32[]{:S(2)}, u32[]{:S(2)}) collective-permute-start(bf16[8,2048]{1,0:T(8,128)(2,1)S(1)} %get-tuple-element.50), channel_id=1, source_target_pairs={{0,44},{1,45},{2,46},{3,47},{4,32},{5,33},{6,34},{7,35},{8,36},{9,... | collective-permute-start | bytes 98312 | tf_op jit(solution)/shard_map/ppermute | solution.py:40
  99.8 16.1 %collective-permute-start.35 = (bf16[8,2048]{1,0:T(8,128)(2,1)S(1)}, bf16[8,2048]{1,0:T(8,128)(2,1)S(1)}, u32[]{:S(2)}, u32[]{:S(2)}) collective-permute-start(bf16[8,2048]{1,0:T(8,128)(2,1)S(1)} %get-tuple-element.50), channel_id=1, source_target_pairs={{0,32},{1,33},{2,34},{3,35},{4,36},{5,37},{6,38},{7,39},{8,40},{9,... | collective-permute-start | bytes 98312 | tf_op jit(solution)/shard_map/ppermute | solution.py:40
  117.4 2.7 %collective-permute-start.36 = (bf16[8,2048]{1,0:T(8,128)(2,1)S(1)}, bf16[8,2048]{1,0:T(8,128)(2,1)S(1)}, u32[]{:S(2)}, u32[]{:S(2)}) collective-permute-start(bf16[8,2048]{1,0:T(8,128)(2,1)S(1)} %get-tuple-element.52), channel_id=1, source_target_pairs={{32,72},{33,73},{34,74},{35,75},{36,76},{37,77},{38,78},{39,79},{4... | collective-permute-start | bytes 98312 | tf_op jit(solution)/shard_map/ppermute | solution.py:40
  118.1 2.0 %collective-permute-start.37 = (bf16[8,2048]{1,0:T(8,128)(2,1)S(1)}, bf16[8,2048]{1,0:T(8,128)(2,1)S(1)}, u32[]{:S(2)}, u32[]{:S(2)}) collective-permute-start(bf16[8,2048]{1,0:T(8,128)(2,1)S(1)} %get-tuple-element.52), channel_id=1, source_target_pairs={{32,68},{33,69},{34,70},{35,71},{36,72},{37,73},{38,74},{39,75},{4... | collective-permute-start | bytes 98312 | tf_op jit(solution)/shard_map/ppermute | solution.py:40
  118.7 1.4 collective-permute-start.38
  119.4 0.7 collective-permute-start.39
  121.6 2.7 %collective-permute-start.40 = (bf16[8,2048]{1,0:T(8,128)(2,1)S(1)}, bf16[8,2048]{1,0:T(8,128)(2,1)S(1)}, u32[]{:S(2)}, u32[]{:S(2)}) collective-permute-start(bf16[8,2048]{1,0:T(8,128)(2,1)S(1)} %get-tuple-element.54), channel_id=1, source_target_pairs={{64,104},{65,105},{66,106},{67,107},{68,108},{69,109},{70,110},{71... | collective-permute-start | bytes 98312 | tf_op jit(solution)/shard_map/ppermute | solution.py:40
  122.3 2.0 %collective-permute-start.41 = (bf16[8,2048]{1,0:T(8,128)(2,1)S(1)}, bf16[8,2048]{1,0:T(8,128)(2,1)S(1)}, u32[]{:S(2)}, u32[]{:S(2)}) collective-permute-start(bf16[8,2048]{1,0:T(8,128)(2,1)S(1)} %get-tuple-element.54), channel_id=1, source_target_pairs={{64,100},{65,101},{66,102},{67,103},{68,104},{69,105},{70,106},{71... | collective-permute-start | bytes 98312 | tf_op jit(solution)/shard_map/ppermute | solution.py:40
  123.0 1.4 collective-permute-start.42
  123.6 0.7 collective-permute-start.43
  125.9 13.7 %collective-permute-start.44 = (bf16[8,2048]{1,0:T(8,128)(2,1)S(1)}, bf16[8,2048]{1,0:T(8,128)(2,1)S(1)}, u32[]{:S(2)}, u32[]{:S(2)}) collective-permute-start(bf16[8,2048]{1,0:T(8,128)(2,1)S(1)} %get-tuple-element.56), channel_id=1, source_target_pairs={{0,40},{1,41},{2,42},{3,43},{4,44},{5,45},{6,46},{7,47},{8,32},{9,... | collective-permute-start | bytes 98312 | tf_op jit(solution)/shard_map/ppermute | solution.py:40
  127.2 13.7 %collective-permute-start.45 = (bf16[8,2048]{1,0:T(8,128)(2,1)S(1)}, bf16[8,2048]{1,0:T(8,128)(2,1)S(1)}, u32[]{:S(2)}, u32[]{:S(2)}) collective-permute-start(bf16[8,2048]{1,0:T(8,128)(2,1)S(1)} %get-tuple-element.56), channel_id=1, source_target_pairs={{0,36},{1,37},{2,38},{3,39},{4,40},{5,41},{6,42},{7,43},{8,44},{9,... | collective-permute-start | bytes 98312 | tf_op jit(solution)/shard_map/ppermute | solution.py:40
  128.5 13.1 %collective-permute-start.46 = (bf16[8,2048]{1,0:T(8,128)(2,1)S(1)}, bf16[8,2048]{1,0:T(8,128)(2,1)S(1)}, u32[]{:S(2)}, u32[]{:S(2)}) collective-permute-start(bf16[8,2048]{1,0:T(8,128)(2,1)S(1)} %get-tuple-element.56), channel_id=1, source_target_pairs={{0,44},{1,45},{2,46},{3,47},{4,32},{5,33},{6,34},{7,35},{8,36},{9,... | collective-permute-start | bytes 98312 | tf_op jit(solution)/shard_map/ppermute | solution.py:40
  129.8 12.8 %collective-permute-start.47 = (bf16[8,2048]{1,0:T(8,128)(2,1)S(1)}, bf16[8,2048]{1,0:T(8,128)(2,1)S(1)}, u32[]{:S(2)}, u32[]{:S(2)}) collective-permute-start(bf16[8,2048]{1,0:T(8,128)(2,1)S(1)} %get-tuple-element.56), channel_id=1, source_target_pairs={{0,32},{1,33},{2,34},{3,35},{4,36},{5,37},{6,38},{7,39},{8,40},{9,... | collective-permute-start | bytes 98312 | tf_op jit(solution)/shard_map/ppermute | solution.py:40
  144.0 1.3 collective-permute-start.48

commit v3 on v2

--- a/solution.py
+++ b/solution.py
@@ -12,7 +12,6 @@
 CORES = 2
 OFFSETS = (0, -1, 1, 2)
 WHOLE = pl.BlockSpec(memory_space=pltpu.VMEM)
-SCALARS = pl.BlockSpec(memory_space=pltpu.SMEM)
 
 
 def near(value):
@@ -25,6 +24,12 @@
 
 def bf16(*shape):
     return jax.ShapeDtypeStruct(shape, jnp.bfloat16)
+
+
+def position():
+    core, orb = lax.rem(lax.axis_index("dom"), CORES), lax.axis_index("orb")
+    y, x = lax.div(orb, SIDE), lax.rem(orb, SIDE)
+    return core, jnp.where(core == 0, y, x), jnp.where(core == 0, x, y), x, y
 
 
 def sent(value, planes, target):
@@ -45,7 +50,7 @@
     return [value, move(value, 1), move(value, -1), opposite]
 
 
-def mask_kernel(info, coupling, pattern, *refs):
+def mask_kernel(coupling, pattern, *refs):
     pieces, (masked, done) = refs[:SIDE], refs[SIDE:]
     rows, order = coupling.shape
     fetch = pltpu.make_async_copy(coupling, masked, done)
@@ -60,26 +65,26 @@
         masked[part, :] = masked[part, :] * present[at : at + 1, :].astype(jnp.bfloat16)
     wide = order // SIDE
     for offset in range(SIDE):
-        turn = lax.rem(info[2] + offset, SIDE)
+        turn = lax.rem(position()[2] + offset, SIDE)
         pieces[offset][...] = masked[:, pl.ds(pl.multiple_of(turn * wide, wide), wide)]
 
 
-def masked_pieces(info, coupling, pattern):
+def masked_pieces(coupling, pattern):
     rows, order = coupling.shape
     return pl.pallas_call(
         mask_kernel,
         out_shape=[pltpu.VMEM((rows, order // SIDE), jnp.bfloat16)] * SIDE,
-        in_specs=[SCALARS, pl.BlockSpec(memory_space=pltpu.HBM), WHOLE],
+        in_specs=[pl.BlockSpec(memory_space=pltpu.HBM), WHOLE],
         out_specs=[WHOLE] * SIDE,
         scratch_shapes=[pltpu.VMEM((rows, order), jnp.bfloat16), pltpu.SemaphoreType.DMA],
         compiler_params=pltpu.CompilerParams(vmem_limit_bytes=4 << 20),
-    )(info, far(coupling), pattern)
-
-
-def tile_kernel(info, *refs):
+    )(far(coupling), pattern)
+
+
+def tile_kernel(*refs):
     columns, greens = refs[:SIDE], refs[SIDE : 2 * SIDE]
-    out, all_columns, all_greens = refs[2 * SIDE + 1 :]
-    core, a, b = info[0], info[1], info[2]
+    out, all_columns, all_greens = refs[-3:]
+    core, a, b, _, _ = position()
     rows = greens[0].shape[0]
     for at, offset in enumerate(OFFSETS):
         row_turn = lax.rem(a + (offset + SIDE), SIDE)
@@ -94,23 +99,23 @@
     out[...] = tile.T.astype(jnp.bfloat16)
 
 
-def tiled(info, columns, greens, after):
+def tiled(columns, greens, after):
     wide = columns[0].shape[1]
     order = greens[0].shape[1]
     return pl.pallas_call(
         tile_kernel,
         out_shape=pltpu.VMEM((wide, wide), jnp.bfloat16),
-        in_specs=[SCALARS] + [WHOLE] * 8 + [pl.BlockSpec(memory_space=pl.ANY)],
+        in_specs=[WHOLE] * 8 + [pl.BlockSpec(memory_space=pl.ANY)] * len(after),
         out_specs=WHOLE,
         scratch_shapes=[pltpu.VMEM((order, wide), jnp.bfloat16), pltpu.VMEM((wide, order), jnp.bfloat16)],
         compiler_params=pltpu.CompilerParams(vmem_limit_bytes=12 << 20),
-    )(info, *map(near, columns + greens), after)
-
-
-def arrange_kernel(offsets, info, *refs):
+    )(*map(near, columns + greens), *after)
+
+
+def arrange_kernel(offsets, *refs):
     count = len(offsets)
     own, other, (even, odd) = refs[:count], refs[count : 2 * count], refs[-2:]
-    core, x = info[0], info[3]
+    core, _, _, x, _ = position()
     wide = own[0].shape[0]
     block = wide // SIDE
 
@@ -126,29 +131,27 @@
     pl.when(core != 0)(lambda: arrange(other, own))
 
 
-def arranged(offsets, info, own, other, so_far=()):
+def arranged(offsets, own, other, so_far=()):
     wide = own[0].shape[0]
     order = SIDE * wide
-    count = 1 + 2 * len(offsets)
+    count = 2 * len(offsets)
     return pl.pallas_call(
         functools.partial(arrange_kernel, offsets),
         out_shape=[pltpu.VMEM((order, wide), jnp.bfloat16), pltpu.VMEM((wide, order), jnp.bfloat16)],
-        in_specs=[SCALARS] + [WHOLE] * (count - 1 + len(so_far)),
+        in_specs=[WHOLE] * (count + len(so_far)),
         out_specs=[WHOLE] * 2,
         input_output_aliases={count + at: at for at in range(len(so_far))},
         compiler_params=pltpu.CompilerParams(vmem_limit_bytes=4 << 20),
-    )(info, *map(near, (*own, *other, *so_far)))
-
-
-def plane_kernel(at, info, state, *refs):
+    )(*map(near, (*own, *other, *so_far)))
+
+
+def plane_kernel(at, due, state, *refs):
     arrived, refs = refs[:SIDE], refs[SIDE:]
     even_source, odd_source, even, odd, odd_part, even_state, kept = refs
-    plane, y = info[5], info[4]
-    wide = even_state.shape[1]
     total = arrived[0][...].astype(jnp.float32)
     for piece in arrived[1:]:
         total += piece[...].astype(jnp.float32)
-    total = jnp.where(plane == at, total, 0.0) + state[...].astype(jnp.float32)
+    total = jnp.where(due[at : at + 1, :1] > 0, total, 0.0) + state[...].astype(jnp.float32)
     total = total.astype(jnp.bfloat16)
     kept[...] = total
     product = jnp.dot(total, even[...], preferred_element_type=jnp.float32)
@@ -158,16 +161,16 @@
     odd_part[...] = (odd_source[...].astype(jnp.float32) - product).astype(jnp.bfloat16)
 
 
-def through_plane(at, info, state, arrived, sources, even, odd):
+def through_plane(at, due, state, arrived, sources, even, odd):
     modes, order = state.shape
     wide = even.shape[1]
     return pl.pallas_call(
         functools.partial(plane_kernel, at),
         out_shape=[pltpu.VMEM((modes, columns), jnp.bfloat16) for columns in (order, wide, order)],
-        in_specs=[SCALARS] + [WHOLE] * 9,
+        in_specs=[WHOLE] * 10,
         out_specs=[WHOLE] * 3,
         compiler_params=pltpu.CompilerParams(vmem_limit_bytes=4 << 20),
-    )(info, *map(near, (state, *arrived, *sources, even, odd)))
+    )(*map(near, (due, state, *arrived, *sources, even, odd)))
 
 
 def on_device(green_blocks, couplings, pattern, sources, injected):
@@ -176,8 +179,6 @@
     y, x = orb // SIDE, orb % SIDE
     plane, core = dom // CORES, dom % CORES
     first = core == 0
-    a, b = jnp.where(first, y, x), jnp.where(first, x, y)
-    info = jnp.stack([core, a, b, x, y, plane]).astype(jnp.int32)
     send = functools.partial(sent, planes=planes)
     along_x = lambda value, step: send(value, target=lambda z, k, y, x: (z, k, y, x + step))
     along_b = lambda value, step: send(value, target=lambda z, k, y, x: (z, k, y + k * step, x + (1 - k) * step))
@@ -188,7 +189,7 @@
     wide = order // SIDE
     modes = injected.shape[0] // (SIDE * CORES)
     mine, theirs = sources[0], to_other_core(sources[0])
-    pieces = masked_pieces(info, couplings[0], pattern[0])
+    pieces = masked_pieces(couplings[0], pattern[0])
     pieces = [pieces[0]] + [along_b(pieces[offset], offset) for offset in range(1, SIDE)]
     green, *_ = lax.optimization_barrier((green_blocks[0], pieces[1]))
     greens = ring(green, along_b)
@@ -203,21 +204,22 @@
         piece = along_x(piece, step) if step else piece
         source = lax.dynamic_update_slice(source, piece, (0, (x - step) % SIDE * (wide // SIDE)))
     even_source, odd_source = source[:modes], source[modes:]
-    tile = tiled(info, columns, greens, source)
+    start = lax.dynamic_slice_in_dim(injected, (CORES * x + core) * modes, modes, 0)
+    state = jnp.where(plane == 0, start, jnp.zeros_like(start))
+    due = jnp.where(jnp.arange(planes)[:, None] == plane, jnp.ones((planes, 128), jnp.float32), 0.0)
+    tile = tiled(columns, greens, (source, state, due))
     own = ring(tile, along_x)
     other = [to_other_core(piece) for piece in own]
-    even, odd = arranged(OFFSETS[:3], info, own[:3], other[:3])
-    even, odd = arranged(OFFSETS[3:], info, own[3:], other[3:], (even, odd))
+    even, odd = arranged(OFFSETS[:3], own[:3], other[:3])
+    even, odd = arranged(OFFSETS[3:], own[3:], other[3:], (even, odd))
 
     odd_source = lax.dynamic_update_slice(jnp.zeros((modes, order), jnp.bfloat16), odd_source, (0, y * wide))
 
-    start = lax.dynamic_slice_in_dim(injected, (CORES * x + core) * modes, modes, 0)
-    state = jnp.where(plane == 0, start, jnp.zeros_like(start))
     arrived = [jnp.zeros_like(start)] * SIDE
     onward = lambda z, at: z % 3 == at % 3 and z + 1 < planes
     for at in range(planes):
         odd_part, even_state, state = through_plane(
-            at, info, state, arrived, (even_source, odd_source), even, odd
+            at, due, state, arrived, (even_source, odd_source), even, odd
         )
         if at + 1 < planes:
             arrived = [

time: 160 us -> 154 us (0.963)
  Pallas kernels: 18.2 us -> 12.4 us
  starting transfers between devices: 55.9 us -> 53.1 us
  waiting for transfers between devices: 68.2 us -> 69.9 us
    pallas_call x8, Pallas kernels: 12 us -> 7.82 us  [through_plane(): pl.pallas_call(functools.partial(plane_kernel, at), out_shape=[pltpu.VMEM...]
    ppermute x49, starting transfers between devices: 55.9 us -> 53.1 us  [sent(): return lax.ppermute(value, ('dom', 'orb'), pairs)]
    ppermute x49, waiting for transfers between devices: 68.2 us -> 69.9 us  [sent(): return lax.ppermute(value, ('dom', 'orb'), pairs)]
  transfers between devices with their start and end apart: 49 -> 49, of which waited for: 22 -> 24; matrix products, arithmetic and copies ran while one was open for 1% -> 1% of each run, Pallas kernels for 1% -> 1%
where the time goes in v3:
time: 154 us; the launch traced here: 153 us
  waiting for transfers between devices  69.9 us (45%)
  starting transfers between devices  53.1 us (34%)
  blocking collectives  14.1 us (9%)
  Pallas kernels  12.4 us (8%)
  other arithmetic  2.16 us (1%)
    ppermute x49, waiting for transfers between devices, sent(): return lax.ppermute(value, ('dom', 'orb'), pairs)  69.9 us
    ppermute x49, starting transfers between devices, sent(): return lax.ppermute(value, ('dom', 'orb'), pairs)  53.1 us
    all_to_all x1, blocking collectives, on_device(): parts = lax.all_to_all(both, 'orb', 0, 0, tiled=True)  14.1 us
    pallas_call x8, Pallas kernels, through_plane(): pl.pallas_call(functools.partial(plane_kernel, at), out_shape=[pltpu.VMEM...  7.82 us
  transfers between devices with their start and end apart: 49, of which 24 were waited for; matrix products, arithmetic and copies ran while one was open for 1% of the time, Pallas kernels for 1%

profile of v3, /device:TPU:224, one launch (start us, length us, event | category | flops | bytes accessed | tf_op | source)
XLA Modules:
  0.0 153.2 jit_solution(16360203082121943265)
XLA Ops:
  0.0 0.7 copy-done.1
  0.7 1.1 shard_map.55
  1.9 1.6 %collective-permute-start.1 = (bf16[128,512]{1,0:T(8,128)(2,1)S(1)}, bf16[128,512]{1,0:T(8,128)(2,1)S(1)}, u32[]{:S(2)}, u32[]{:S(2)}) collective-permute-start(bf16[128,512]{1,0:T(8,128)(2,1)S(1)} %get-tuple-element.33), channel_id=1, source_target_pairs={{0,1},{1,2},{2,3},{3,0},{4,5},{5,6},{6,7},{7,4},{8,9},{9,10},{10,1... | collective-permute-start | bytes 393224 | tf_op jit(solution)/shard_map/ppermute | solution.py:45
  3.5 2.7 %collective-permute-start.2 = (bf16[128,512]{1,0:T(8,128)(2,1)S(1)}, bf16[128,512]{1,0:T(8,128)(2,1)S(1)}, u32[]{:S(2)}, u32[]{:S(2)}) collective-permute-start(bf16[128,512]{1,0:T(8,128)(2,1)S(1)} %get-tuple-element.34), channel_id=1, source_target_pairs={{0,2},{1,3},{2,0},{3,1},{4,6},{5,7},{6,4},{7,5},{8,10},{9,11},{10,... | collective-permute-start | bytes 393224 | tf_op jit(solution)/shard_map/ppermute | solution.py:45
  6.2 1.4 collective-permute-start.3
  8.2 2.4 %collective-permute-done.2 = bf16[128,512]{1,0:T(8,128)(2,1)S(1)} collective-permute-done((bf16[128,512]{1,0:T(8,128)(2,1)S(1)}, bf16[128,512]{1,0:T(8,128)(2,1)S(1)}, u32[]{:S(2)}, u32[]{:S(2)}) %collective-permute-start.2) | collective-permute-done | bytes 131104 | tf_op jit(solution)/shard_map/ppermute | solution.py:45
  11.2 1.7 %collective-permute-start.4 = (bf16[512,512]{1,0:T(8,128)(2,1)S(1)}, bf16[512,512]{1,0:T(8,128)(2,1)S(1)}, u32[]{:S(2)}, u32[]{:S(2)}) collective-permute-start(bf16[512,512]{1,0:T(8,128)(2,1)S(1)} %constant_dynamic-update-slice_fusion.refs_0_), channel_id=1, source_target_pairs={{0,4},{1,5},{2,6},{3,7},{4,8},{5,9},{6,10},{7,11},{8,12},{9,13},{1... | collective-permute-start | bytes 1572872 | tf_op jit(solution)/shard_map/ppermute | solution.py:45
  12.8 1.7 %collective-permute-start.5 = (bf16[512,512]{1,0:T(8,128)(2,1)S(1)}, bf16[512,512]{1,0:T(8,128)(2,1)S(1)}, u32[]{:S(2)}, u32[]{:S(2)}) collective-permute-start(bf16[512,512]{1,0:T(8,128)(2,1)S(1)} %constant_dynamic-update-slice_fusion.refs_0_), channel_id=1, source_target_pairs={{0,12},{1,13},{2,14},{3,15},{4,0},{5,1},{6,2},{7,3},{8,4},{9,5},{1... | collective-permute-start | bytes 1572872 | tf_op jit(solution)/shard_map/ppermute | solution.py:45
  14.5 0.8 dynamic-slice_select_fusion.refs_9_.state
  15.4 2.1 %collective-permute-start.9 = (bf16[512,512]{1,0:T(8,128)(2,1)S(1)}, bf16[512,512]{1,0:T(8,128)(2,1)S(1)}, u32[]{:S(2)}, u32[]{:S(2)}) collective-permute-start(bf16[512,512]{1,0:T(8,128)(2,1)S(1)} %constant_dynamic-update-slice_fusion.refs_0_), channel_id=1, source_target_pairs={{0,8},{1,9},{2,10},{3,11},{4,12},{5,13},{6,14},{7,15},{8,0},{9,1},... | collective-permute-start | bytes 1572872 | tf_op jit(solution)/shard_map/ppermute | solution.py:45
  17.5 1.3 collective-permute-start.10
  18.8 2.0 %collective-permute-start.11 = (bf16[128,2048]{1,0:T(8,128)(2,1)}, bf16[128,2048]{1,0:T(8,128)(2,1)S(1)}, u32[]{:S(2)}, u32[]{:S(2)}) collective-permute-start(bf16[128,2048]{1,0:T(8,128)(2,1)} %bitcast.28), channel_id=1, source_target_pairs={{0,3},{1,0},{2,1},{3,2},{4,7},{5,4},{6,5},{7,6},{8,11},{9,8},{10,9... | collective-permute-start | bytes 1572872 | tf_op jit(solution)/shard_map/ppermute | solution.py:45
  20.7 0.9 collective-permute-done.4.refs_1_
  21.6 2.9 %collective-permute-start.12 = (bf16[128,2048]{1,0:T(8,128)(2,1)}, bf16[128,2048]{1,0:T(8,128)(2,1)S(1)}, u32[]{:S(2)}, u32[]{:S(2)}) collective-permute-start(bf16[128,2048]{1,0:T(8,128)(2,1)} %bitcast.29), channel_id=1, source_target_pairs={{0,2},{1,3},{2,0},{3,1},{4,6},{5,7},{6,4},{7,5},{8,10},{9,11},{10,... | collective-permute-start | bytes 1572872 | tf_op jit(solution)/shard_map/ppermute | solution.py:45
  24.6 0.7 broadcast_select_fusion.5
  25.3 1.2 collective-permute-start.6
  26.5 9.0 %collective-permute-done.6 = bf16[16,128]{1,0:T(8,128)(2,1)S(1)} collective-permute-done((bf16[16,128]{1,0:T(8,128)(2,1)S(1)}, bf16[16,128]{1,0:T(8,128)(2,1)S(1)}, u32[]{:S(2)}, u32[]{:S(2)}) %collective-permute-start.6) | collective-permute-done | bytes 4128 | tf_op jit(solution)/shard_map/ppermute | solution.py:45
  35.5 1.4 collective-permute-start.7
  36.9 3.7 %collective-permute-done.7 = bf16[16,128]{1,0:T(8,128)(2,1)S(1)} collective-permute-done((bf16[16,128]{1,0:T(8,128)(2,1)S(1)}, bf16[16,128]{1,0:T(8,128)(2,1)S(1)}, u32[]{:S(2)}, u32[]{:S(2)}) %collective-permute-start.7) | collective-permute-done | bytes 4128 | tf_op jit(solution)/shard_map/ppermute | solution.py:45
  40.6 2.4 %collective-permute-start.8 = (bf16[16,128]{1,0:T(8,128)(2,1)S(1)}, bf16[16,128]{1,0:T(8,128)(2,1)S(1)}, u32[]{:S(2)}, u32[]{:S(2)}) collective-permute-start(bf16[16,128]{1,0:T(8,128)(2,1)S(1)} %get-tuple-element.61), channel_id=1, source_target_pairs={{0,3},{1,0},{2,1},{3,2},{4,7},{5,4},{6,5},{7,6},{8,11},{9,8},{10,9... | collective-permute-start | bytes 12296 | tf_op jit(solution)/shard_map/ppermute | solution.py:45
  43.0 1.6 %collective-permute-done.8 = bf16[16,128]{1,0:T(8,128)(2,1)S(1)} collective-permute-done((bf16[16,128]{1,0:T(8,128)(2,1)S(1)}, bf16[16,128]{1,0:T(8,128)(2,1)S(1)}, u32[]{:S(2)}, u32[]{:S(2)}) %collective-permute-start.8) | collective-permute-done | bytes 4128 | tf_op jit(solution)/shard_map/ppermute | solution.py:45
  44.7 1.5 shard_map.56.refs_0_
  46.2 2.1 %collective-permute-start.15 = (bf16[512,512]{1,0:T(8,128)(2,1)S(1)}, bf16[512,512]{1,0:T(8,128)(2,1)S(1)}, u32[]{:S(2)}, u32[]{:S(2)}) collective-permute-start(bf16[512,512]{1,0:T(8,128)(2,1)S(1)} %shard_map.56.refs_0_), channel_id=1, source_target_pairs={{0,1},{1,2},{2,3},{3,0},{4,5},{5,6},{6,7},{7,4},{8,9},{9,10},{10,1... | collective-permute-start | bytes 1572872 | tf_op jit(solution)/shard_map/ppermute | solution.py:45
  48.3 1.3 collective-permute-start.16
  49.6 1.4 collective-permute-start.13
  51.0 11.3 %collective-permute-done.15.refs_1_ = bf16[512,512]{1,0:T(8,128)(2,1)S(1)} collective-permute-done((bf16[512,512]{1,0:T(8,128)(2,1)S(1)}, bf16[512,512]{1,0:T(8,128)(2,1)S(1)}, u32[]{:S(2)}, u32[]{:S(2)}) %collective-permute-start.15) | collective-permute-done | bytes 524320 | tf_op jit(solution)/shard_map/ppermute | solution.py:45
  62.3 4.5 %collective-permute-done.16.refs_2_ = bf16[512,512]{1,0:T(8,128)(2,1)S(1)} collective-permute-done((bf16[512,512]{1,0:T(8,128)(2,1)S(1)}, bf16[512,512]{1,0:T(8,128)(2,1)S(1)}, u32[]{:S(2)}, u32[]{:S(2)}) %collective-permute-start.16) | collective-permute-done | bytes 524320 | tf_op jit(solution)/shard_map/ppermute | solution.py:45
  66.8 1.6 %collective-permute-done.13.refs_0_ = bf16[512,512]{1,0:T(8,128)(2,1)S(1)} collective-permute-done((bf16[512,512]{1,0:T(8,128)(2,1)S(1)}, bf16[512,512]{1,0:T(8,128)(2,1)S(1)}, u32[]{:S(2)}, u32[]{:S(2)}) %collective-permute-start.13) | collective-permute-done | bytes 524320 | tf_op jit(solution)/shard_map/ppermute | solution.py:45
  68.8 1.8 %shard_map.57 = (bf16[2048,512]{1,0:T(8,128)(2,1)S(1)}, bf16[512,2048]{1,0:T(8,128)(2,1)S(1)}) custom-call(bf16[512,512]{1,0:T(8,128)(2,1)S(1)} %shard_map.56.refs_0_, bf16[512,512]{1,0:T(8,128)(2,1)S(1)} %collective-permute-done.15.refs_1_, bf16[512,512]{1,0:T(8,128)(2,1)S(1)} %collective-permute-done.16.refs_2_, ...), custom_call_target="tpu_custom_call" | custom-call | tf_op jit(solution)/shard_map/pallas_call | solution.py:138
  70.8 1.0 shard_map.59
  71.8 1.3 collective-permute-start.20
  73.1 1.3 collective-permute-start.21
  74.4 1.3 collective-permute-start.22
  75.7 1.3 collective-permute-start.23
  77.0 3.0 %collective-permute-done.20.refs_0_ = bf16[8,2048]{1,0:T(8,128)(2,1)S(1)} collective-permute-done((bf16[8,2048]{1,0:T(8,128)(2,1)S(1)}, bf16[8,2048]{1,0:T(8,128)(2,1)S(1)}, u32[]{:S(2)}, u32[]{:S(2)}) %collective-permute-start.20) | collective-permute-done | bytes 32800 | tf_op jit(solution)/shard_map/ppermute | solution.py:45
  80.0 2.0 %collective-permute-done.21.refs_1_ = bf16[8,2048]{1,0:T(8,128)(2,1)S(1)} collective-permute-done((bf16[8,2048]{1,0:T(8,128)(2,1)S(1)}, bf16[8,2048]{1,0:T(8,128)(2,1)S(1)}, u32[]{:S(2)}, u32[]{:S(2)}) %collective-permute-start.21) | collective-permute-done | bytes 32800 | tf_op jit(solution)/shard_map/ppermute | solution.py:45
  82.1 1.0 collective-permute-done.23.refs_3_
  83.1 1.0 shard_map.60
  84.8 0.7 collective-permute-start.25
  85.4 0.7 collective-permute-start.26
  86.1 0.7 collective-permute-start.27
  86.8 1.0 shard_map.61
  90.5 1.0 shard_map.62
  91.5 1.3 collective-permute-start.32
  92.8 1.3 collective-permute-start.33
  94.1 1.3 collective-permute-start.34
  95.4 1.3 collective-permute-start.35
  96.7 12.6 %collective-permute-done.32.refs_0_ = bf16[8,2048]{1,0:T(8,128)(2,1)S(1)} collective-permute-done((bf16[8,2048]{1,0:T(8,128)(2,1)S(1)}, bf16[8,2048]{1,0:T(8,128)(2,1)S(1)}, u32[]{:S(2)}, u32[]{:S(2)}) %collective-permute-start.32) | collective-permute-done | bytes 32800 | tf_op jit(solution)/shard_map/ppermute | solution.py:45
  109.4 1.0 collective-permute-done.33.refs_1_
  110.5 1.0 collective-permute-done.35.refs_3_
  111.5 1.0 shard_map.63
  115.2 1.0 shard_map.64
  118.9 1.0 shard_map.65
  119.9 1.3 collective-permute-start.44
  121.2 1.3 collective-permute-start.45
  122.5 1.3 collective-permute-start.46
  123.8 1.3 collective-permute-start.47
  125.1 8.3 %collective-permute-done.44.refs_0_ = bf16[8,2048]{1,0:T(8,128)(2,1)S(1)} collective-permute-done((bf16[8,2048]{1,0:T(8,128)(2,1)S(1)}, bf16[8,2048]{1,0:T(8,128)(2,1)S(1)}, u32[]{:S(2)}, u32[]{:S(2)}) %collective-permute-start.44) | collective-permute-done | bytes 32800 | tf_op jit(solution)/shard_map/ppermute | solution.py:45
  133.4 1.3 collective-permute-done.45.refs_1_
  134.7 0.7 collective-permute-done.46.refs_2_
  135.4 1.0 collective-permute-done.47.refs_3_
  136.4 0.8 shard_map.66
  137.3 1.2 collective-permute-done.48
  138.5 14.1 %all_to_all.5 = bf16[16,16,128]{2,1,0:T(8,128)(2,1)S(1)} all-to-all(bf16[16,16,128]{2,1,0:T(8,128)(2,1)S(1)} %bitcast_bitcast_fusion), channel_id=1, replica_groups=mesh['dom'=16,'orb'=16] {'orb'}, dimensions={0} | all-to-all | bytes 131072 | tf_op jit(solution)/shard_map/all_to_all | solution.py:235
  (73 shorter events, 11.5 us)
Async XLA Ops:
  0.0 44.7 %copy-start = (bf16[1,128,2048]{2,1,0:T(8,128)(2,1)S(1)}, bf16[1,128,2048]{2,1,0:T(8,128)(2,1)}, u32[]{:S(2)}) copy-start(bf16[1,128,2048]{2,1,0:T(8,128)(2,1)} %param.5) | copy-start | bytes 1572868
  0.0 0.7 copy-start.1
  1.9 6.3 %collective-permute-start.1 = (bf16[128,512]{1,0:T(8,128)(2,1)S(1)}, bf16[128,512]{1,0:T(8,128)(2,1)S(1)}, u32[]{:S(2)}, u32[]{:S(2)}) collective-permute-start(bf16[128,512]{1,0:T(8,128)(2,1)S(1)} %get-tuple-element.33), channel_id=1, source_target_pairs={{0,1},{1,2},{2,3},{3,0},{4,5},{5,6},{6,7},{7,4},{8,9},{9,10},{10,1... | collective-permute-start | bytes 393224 | tf_op jit(solution)/shard_map/ppermute | solution.py:45
  3.5 7.1 %collective-permute-start.2 = (bf16[128,512]{1,0:T(8,128)(2,1)S(1)}, bf16[128,512]{1,0:T(8,128)(2,1)S(1)}, u32[]{:S(2)}, u32[]{:S(2)}) collective-permute-start(bf16[128,512]{1,0:T(8,128)(2,1)S(1)} %get-tuple-element.34), channel_id=1, source_target_pairs={{0,2},{1,3},{2,0},{3,1},{4,6},{5,7},{6,4},{7,5},{8,10},{9,11},{10,... | collective-permute-start | bytes 393224 | tf_op jit(solution)/shard_map/ppermute | solution.py:45
  6.2 5.0 %collective-permute-start.3 = (bf16[128,512]{1,0:T(8,128)(2,1)S(1)}, bf16[128,512]{1,0:T(8,128)(2,1)S(1)}, u32[]{:S(2)}, u32[]{:S(2)}) collective-permute-start(bf16[128,512]{1,0:T(8,128)(2,1)S(1)} %get-tuple-element.35), channel_id=1, source_target_pairs={{0,3},{1,0},{2,1},{3,2},{4,7},{5,4},{6,5},{7,6},{8,11},{9,8},{10,9... | collective-permute-start | bytes 393224 | tf_op jit(solution)/shard_map/ppermute | solution.py:45
  11.2 10.5 %collective-permute-start.4 = (bf16[512,512]{1,0:T(8,128)(2,1)S(1)}, bf16[512,512]{1,0:T(8,128)(2,1)S(1)}, u32[]{:S(2)}, u32[]{:S(2)}) collective-permute-start(bf16[512,512]{1,0:T(8,128)(2,1)S(1)} %constant_dynamic-update-slice_fusion.refs_0_), channel_id=1, source_target_pairs={{0,4},{1,5},{2,6},{3,7},{4,8},{5,9},{6,10},{7,11},{8,12},{9,13},{1... | collective-permute-start | bytes 1572872 | tf_op jit(solution)/shard_map/ppermute | solution.py:45
  12.8 11.7 %collective-permute-start.5 = (bf16[512,512]{1,0:T(8,128)(2,1)S(1)}, bf16[512,512]{1,0:T(8,128)(2,1)S(1)}, u32[]{:S(2)}, u32[]{:S(2)}) collective-permute-start(bf16[512,512]{1,0:T(8,128)(2,1)S(1)} %constant_dynamic-update-slice_fusion.refs_0_), channel_id=1, source_target_pairs={{0,12},{1,13},{2,14},{3,15},{4,0},{5,1},{6,2},{7,3},{8,4},{9,5},{1... | collective-permute-start | bytes 1572872 | tf_op jit(solution)/shard_map/ppermute | solution.py:45
  14.5 4.3 %collective-permute-start = (bf16[64,128]{1,0:T(8,128)(2,1)}, bf16[64,128]{1,0:T(8,128)(2,1)S(1)}, u32[]{:S(2)}, u32[]{:S(2)}) collective-permute-start(bf16[64,128]{1,0:T(8,128)(2,1)} %bitcast.38), channel_id=1, source_target_pairs={{0,16},{1,17},{2,18},{3,19},{4,20},{5,21},{6,22},{7,23},{8,24},{9,... | collective-permute-start | bytes 49160 | tf_op jit(solution)/shard_map/ppermute | solution.py:45
  15.4 29.2 %collective-permute-start.9 = (bf16[512,512]{1,0:T(8,128)(2,1)S(1)}, bf16[512,512]{1,0:T(8,128)(2,1)S(1)}, u32[]{:S(2)}, u32[]{:S(2)}) collective-permute-start(bf16[512,512]{1,0:T(8,128)(2,1)S(1)} %constant_dynamic-update-slice_fusion.refs_0_), channel_id=1, source_target_pairs={{0,8},{1,9},{2,10},{3,11},{4,12},{5,13},{6,14},{7,15},{8,0},{9,1},... | collective-permute-start | bytes 1572872 | tf_op jit(solution)/shard_map/ppermute | solution.py:45
  17.5 27.1 %collective-permute-start.10 = (bf16[128,2048]{1,0:T(8,128)(2,1)}, bf16[128,2048]{1,0:T(8,128)(2,1)S(1)}, u32[]{:S(2)}, u32[]{:S(2)}) collective-permute-start(bf16[128,2048]{1,0:T(8,128)(2,1)} %bitcast.27), channel_id=1, source_target_pairs={{0,1},{1,2},{2,3},{3,0},{4,5},{5,6},{6,7},{7,4},{8,9},{9,10},{10,1... | collective-permute-start | bytes 1572872 | tf_op jit(solution)/shard_map/ppermute | solution.py:45
  18.8 25.9 %collective-permute-start.11 = (bf16[128,2048]{1,0:T(8,128)(2,1)}, bf16[128,2048]{1,0:T(8,128)(2,1)S(1)}, u32[]{:S(2)}, u32[]{:S(2)}) collective-permute-start(bf16[128,2048]{1,0:T(8,128)(2,1)} %bitcast.28), channel_id=1, source_target_pairs={{0,3},{1,0},{2,1},{3,2},{4,7},{5,4},{6,5},{7,6},{8,11},{9,8},{10,9... | collective-permute-start | bytes 1572872 | tf_op jit(solution)/shard_map/ppermute | solution.py:45
  21.6 23.0 %collective-permute-start.12 = (bf16[128,2048]{1,0:T(8,128)(2,1)}, bf16[128,2048]{1,0:T(8,128)(2,1)S(1)}, u32[]{:S(2)}, u32[]{:S(2)}) collective-permute-start(bf16[128,2048]{1,0:T(8,128)(2,1)} %bitcast.29), channel_id=1, source_target_pairs={{0,2},{1,3},{2,0},{3,1},{4,6},{5,7},{6,4},{7,5},{8,10},{9,11},{10,... | collective-permute-start | bytes 1572872 | tf_op jit(solution)/shard_map/ppermute | solution.py:45
  25.3 10.2 %collective-permute-start.6 = (bf16[16,128]{1,0:T(8,128)(2,1)S(1)}, bf16[16,128]{1,0:T(8,128)(2,1)S(1)}, u32[]{:S(2)}, u32[]{:S(2)}) collective-permute-start(bf16[16,128]{1,0:T(8,128)(2,1)S(1)} %get-tuple-element.62), channel_id=1, source_target_pairs={{0,1},{1,2},{2,3},{3,0},{4,5},{5,6},{6,7},{7,4},{8,9},{9,10},{10,1... | collective-permute-start | bytes 12296 | tf_op jit(solution)/shard_map/ppermute | solution.py:45
  35.5 5.1 %collective-permute-start.7 = (bf16[16,128]{1,0:T(8,128)(2,1)S(1)}, bf16[16,128]{1,0:T(8,128)(2,1)S(1)}, u32[]{:S(2)}, u32[]{:S(2)}) collective-permute-start(bf16[16,128]{1,0:T(8,128)(2,1)S(1)} %get-tuple-element.63), channel_id=1, source_target_pairs={{0,2},{1,3},{2,0},{3,1},{4,6},{5,7},{6,4},{7,5},{8,10},{9,11},{10,... | collective-permute-start | bytes 12296 | tf_op jit(solution)/shard_map/ppermute | solution.py:45
  40.6 4.0 %collective-permute-start.8 = (bf16[16,128]{1,0:T(8,128)(2,1)S(1)}, bf16[16,128]{1,0:T(8,128)(2,1)S(1)}, u32[]{:S(2)}, u32[]{:S(2)}) collective-permute-start(bf16[16,128]{1,0:T(8,128)(2,1)S(1)} %get-tuple-element.61), channel_id=1, source_target_pairs={{0,3},{1,0},{2,1},{3,2},{4,7},{5,4},{6,5},{7,6},{8,11},{9,8},{10,9... | collective-permute-start | bytes 12296 | tf_op jit(solution)/shard_map/ppermute | solution.py:45
  46.2 16.1 %collective-permute-start.15 = (bf16[512,512]{1,0:T(8,128)(2,1)S(1)}, bf16[512,512]{1,0:T(8,128)(2,1)S(1)}, u32[]{:S(2)}, u32[]{:S(2)}) collective-permute-start(bf16[512,512]{1,0:T(8,128)(2,1)S(1)} %shard_map.56.refs_0_), channel_id=1, source_target_pairs={{0,1},{1,2},{2,3},{3,0},{4,5},{5,6},{6,7},{7,4},{8,9},{9,10},{10,1... | collective-permute-start | bytes 1572872 | tf_op jit(solution)/shard_map/ppermute | solution.py:45
  48.3 18.5 %collective-permute-start.16 = (bf16[512,512]{1,0:T(8,128)(2,1)S(1)}, bf16[512,512]{1,0:T(8,128)(2,1)S(1)}, u32[]{:S(2)}, u32[]{:S(2)}) collective-permute-start(bf16[512,512]{1,0:T(8,128)(2,1)S(1)} %shard_map.56.refs_0_), channel_id=1, source_target_pairs={{0,3},{1,0},{2,1},{3,2},{4,7},{5,4},{6,5},{7,6},{8,11},{9,8},{10,9... | collective-permute-start | bytes 1572872 | tf_op jit(solution)/shard_map/ppermute | solution.py:45
  49.6 18.8 %collective-permute-start.13 = (bf16[512,512]{1,0:T(8,128)(2,1)S(1)}, bf16[512,512]{1,0:T(8,128)(2,1)S(1)}, u32[]{:S(2)}, u32[]{:S(2)}) collective-permute-start(bf16[512,512]{1,0:T(8,128)(2,1)S(1)} %shard_map.56.refs_0_), channel_id=1, source_target_pairs={{0,2},{1,3},{2,0},{3,1},{4,6},{5,7},{6,4},{7,5},{8,10},{9,11},{10,... | collective-permute-start | bytes 1572872 | tf_op jit(solution)/shard_map/ppermute | solution.py:45
  51.0 17.5 %collective-permute-start.17 = (bf16[512,512]{1,0:T(8,128)(2,1)S(1)}, bf16[512,512]{1,0:T(8,128)(2,1)S(1)}, u32[]{:S(2)}, u32[]{:S(2)}) collective-permute-start(bf16[512,512]{1,0:T(8,128)(2,1)S(1)} %shard_map.56.refs_0_), channel_id=1, source_target_pairs={{0,16},{1,17},{2,18},{3,19},{4,20},{5,21},{6,22},{7,23},{8,24},{9,... | collective-permute-start | bytes 1572872 | tf_op jit(solution)/shard_map/ppermute | solution.py:45
  62.3 6.1 %collective-permute-start.18 = (bf16[512,512]{1,0:T(8,128)(2,1)S(1)}, bf16[512,512]{1,0:T(8,128)(2,1)}, u32[]{:S(2)}, u32[]{:S(2)}) collective-permute-start(bf16[512,512]{1,0:T(8,128)(2,1)S(1)} %collective-permute-done.15.refs_1_), channel_id=1, source_target_pairs={{0,16},{1,17},{2,18},{3,19},{4,20},{5,21},{6,22},{7,23},{8,24},{9,... | collective-permute-start | bytes 1572872 | tf_op jit(solution)/shard_map/ppermute | solution.py:45
  66.8 2.0 %collective-permute-start.19 = (bf16[512,512]{1,0:T(8,128)(2,1)S(1)}, bf16[512,512]{1,0:T(8,128)(2,1)}, u32[]{:S(2)}, u32[]{:S(2)}) collective-permute-start(bf16[512,512]{1,0:T(8,128)(2,1)S(1)} %collective-permute-done.16.refs_2_), channel_id=1, source_target_pairs={{0,16},{1,17},{2,18},{3,19},{4,20},{5,21},{6,22},{7,23},{8,24},{9,... | collective-permute-start | bytes 1572872 | tf_op jit(solution)/shard_map/ppermute | solution.py:45
  68.4 2.2 %collective-permute-start.14 = (bf16[512,512]{1,0:T(8,128)(2,1)S(1)}, bf16[512,512]{1,0:T(8,128)(2,1)S(1)}, u32[]{:S(2)}, u32[]{:S(2)}) collective-permute-start(bf16[512,512]{1,0:T(8,128)(2,1)S(1)} %collective-permute-done.13.refs_0_), channel_id=1, source_target_pairs={{0,16},{1,17},{2,18},{3,19},{4,20},{5,21},{6,22},{7,23},{8,24},{9,... | collective-permute-start | bytes 1572872 | tf_op jit(solution)/shard_map/ppermute | solution.py:45
  71.8 8.2 %collective-permute-start.20 = (bf16[8,2048]{1,0:T(8,128)(2,1)S(1)}, bf16[8,2048]{1,0:T(8,128)(2,1)S(1)}, u32[]{:S(2)}, u32[]{:S(2)}) collective-permute-start(bf16[8,2048]{1,0:T(8,128)(2,1)S(1)} %get-tuple-element.44), channel_id=1, source_target_pairs={{0,40},{1,41},{2,42},{3,43},{4,44},{5,45},{6,46},{7,47},{8,32},{9,... | collective-permute-start | bytes 98312 | tf_op jit(solution)/shard_map/ppermute | solution.py:45
  73.1 8.9 %collective-permute-start.21 = (bf16[8,2048]{1,0:T(8,128)(2,1)S(1)}, bf16[8,2048]{1,0:T(8,128)(2,1)S(1)}, u32[]{:S(2)}, u32[]{:S(2)}) collective-permute-start(bf16[8,2048]{1,0:T(8,128)(2,1)S(1)} %get-tuple-element.44), channel_id=1, source_target_pairs={{0,36},{1,37},{2,38},{3,39},{4,40},{5,41},{6,42},{7,43},{8,44},{9,... | collective-permute-start | bytes 98312 | tf_op jit(solution)/shard_map/ppermute | solution.py:45
  74.4 7.7 %collective-permute-start.22 = (bf16[8,2048]{1,0:T(8,128)(2,1)S(1)}, bf16[8,2048]{1,0:T(8,128)(2,1)S(1)}, u32[]{:S(2)}, u32[]{:S(2)}) collective-permute-start(bf16[8,2048]{1,0:T(8,128)(2,1)S(1)} %get-tuple-element.44), channel_id=1, source_target_pairs={{0,44},{1,45},{2,46},{3,47},{4,32},{5,33},{6,34},{7,35},{8,36},{9,... | collective-permute-start | bytes 98312 | tf_op jit(solution)/shard_map/ppermute | solution.py:45
  75.7 7.4 %collective-permute-start.23 = (bf16[8,2048]{1,0:T(8,128)(2,1)S(1)}, bf16[8,2048]{1,0:T(8,128)(2,1)S(1)}, u32[]{:S(2)}, u32[]{:S(2)}) collective-permute-start(bf16[8,2048]{1,0:T(8,128)(2,1)S(1)} %get-tuple-element.44), channel_id=1, source_target_pairs={{0,32},{1,33},{2,34},{3,35},{4,36},{5,37},{6,38},{7,39},{8,40},{9,... | collective-permute-start | bytes 98312 | tf_op jit(solution)/shard_map/ppermute | solution.py:45
  84.1 2.7 %collective-permute-start.24 = (bf16[8,2048]{1,0:T(8,128)(2,1)S(1)}, bf16[8,2048]{1,0:T(8,128)(2,1)S(1)}, u32[]{:S(2)}, u32[]{:S(2)}) collective-permute-start(bf16[8,2048]{1,0:T(8,128)(2,1)S(1)} %get-tuple-element.46), channel_id=1, source_target_pairs={{32,72},{33,73},{34,74},{35,75},{36,76},{37,77},{38,78},{39,79},{4... | collective-permute-start | bytes 98312 | tf_op jit(solution)/shard_map/ppermute | solution.py:45
  84.8 2.0 %collective-permute-start.25 = (bf16[8,2048]{1,0:T(8,128)(2,1)S(1)}, bf16[8,2048]{1,0:T(8,128)(2,1)S(1)}, u32[]{:S(2)}, u32[]{:S(2)}) collective-permute-start(bf16[8,2048]{1,0:T(8,128)(2,1)S(1)} %get-tuple-element.46), channel_id=1, source_target_pairs={{32,68},{33,69},{34,70},{35,71},{36,72},{37,73},{38,74},{39,75},{4... | collective-permute-start | bytes 98312 | tf_op jit(solution)/shard_map/ppermute | solution.py:45
  85.4 1.4 collective-permute-start.26
  86.1 0.7 collective-permute-start.27
  87.8 2.7 %collective-permute-start.28 = (bf16[8,2048]{1,0:T(8,128)(2,1)S(1)}, bf16[8,2048]{1,0:T(8,128)(2,1)S(1)}, u32[]{:S(2)}, u32[]{:S(2)}) collective-permute-start(bf16[8,2048]{1,0:T(8,128)(2,1)S(1)} %get-tuple-element.48), channel_id=1, source_target_pairs={{64,104},{65,105},{66,106},{67,107},{68,108},{69,109},{70,110},{71... | collective-permute-start | bytes 98312 | tf_op jit(solution)/shard_map/ppermute | solution.py:45
  88.5 2.0 %collective-permute-start.29 = (bf16[8,2048]{1,0:T(8,128)(2,1)S(1)}, bf16[8,2048]{1,0:T(8,128)(2,1)S(1)}, u32[]{:S(2)}, u32[]{:S(2)}) collective-permute-start(bf16[8,2048]{1,0:T(8,128)(2,1)S(1)} %get-tuple-element.48), channel_id=1, source_target_pairs={{64,100},{65,101},{66,102},{67,103},{68,104},{69,105},{70,106},{71... | collective-permute-start | bytes 98312 | tf_op jit(solution)/shard_map/ppermute | solution.py:45
  89.2 1.4 collective-permute-start.30
  89.8 0.7 collective-permute-start.31
  91.5 17.8 %collective-permute-start.32 = (bf16[8,2048]{1,0:T(8,128)(2,1)S(1)}, bf16[8,2048]{1,0:T(8,128)(2,1)S(1)}, u32[]{:S(2)}, u32[]{:S(2)}) collective-permute-start(bf16[8,2048]{1,0:T(8,128)(2,1)S(1)} %get-tuple-element.50), channel_id=1, source_target_pairs={{0,40},{1,41},{2,42},{3,43},{4,44},{5,45},{6,46},{7,47},{8,32},{9,... | collective-permute-start | bytes 98312 | tf_op jit(solution)/shard_map/ppermute | solution.py:45
  92.8 17.6 %collective-permute-start.33 = (bf16[8,2048]{1,0:T(8,128)(2,1)S(1)}, bf16[8,2048]{1,0:T(8,128)(2,1)S(1)}, u32[]{:S(2)}, u32[]{:S(2)}) collective-permute-start(bf16[8,2048]{1,0:T(8,128)(2,1)S(1)} %get-tuple-element.50), channel_id=1, source_target_pairs={{0,36},{1,37},{2,38},{3,39},{4,40},{5,41},{6,42},{7,43},{8,44},{9,... | collective-permute-start | bytes 98312 | tf_op jit(solution)/shard_map/ppermute | solution.py:45
  94.1 16.4 %collective-permute-start.34 = (bf16[8,2048]{1,0:T(8,128)(2,1)S(1)}, bf16[8,2048]{1,0:T(8,128)(2,1)S(1)}, u32[]{:S(2)}, u32[]{:S(2)}) collective-permute-start(bf16[8,2048]{1,0:T(8,128)(2,1)S(1)} %get-tuple-element.50), channel_id=1, source_target_pairs={{0,44},{1,45},{2,46},{3,47},{4,32},{5,33},{6,34},{7,35},{8,36},{9,... | collective-permute-start | bytes 98312 | tf_op jit(solution)/shard_map/ppermute | solution.py:45
  95.4 16.1 %collective-permute-start.35 = (bf16[8,2048]{1,0:T(8,128)(2,1)S(1)}, bf16[8,2048]{1,0:T(8,128)(2,1)S(1)}, u32[]{:S(2)}, u32[]{:S(2)}) collective-permute-start(bf16[8,2048]{1,0:T(8,128)(2,1)S(1)} %get-tuple-element.50), channel_id=1, source_target_pairs={{0,32},{1,33},{2,34},{3,35},{4,36},{5,37},{6,38},{7,39},{8,40},{9,... | collective-permute-start | bytes 98312 | tf_op jit(solution)/shard_map/ppermute | solution.py:45
  112.5 2.7 %collective-permute-start.36 = (bf16[8,2048]{1,0:T(8,128)(2,1)S(1)}, bf16[8,2048]{1,0:T(8,128)(2,1)S(1)}, u32[]{:S(2)}, u32[]{:S(2)}) collective-permute-start(bf16[8,2048]{1,0:T(8,128)(2,1)S(1)} %get-tuple-element.52), channel_id=1, source_target_pairs={{32,72},{33,73},{34,74},{35,75},{36,76},{37,77},{38,78},{39,79},{4... | collective-permute-start | bytes 98312 | tf_op jit(solution)/shard_map/ppermute | solution.py:45
  113.2 2.0 %collective-permute-start.37 = (bf16[8,2048]{1,0:T(8,128)(2,1)S(1)}, bf16[8,2048]{1,0:T(8,128)(2,1)S(1)}, u32[]{:S(2)}, u32[]{:S(2)}) collective-permute-start(bf16[8,2048]{1,0:T(8,128)(2,1)S(1)} %get-tuple-element.52), channel_id=1, source_target_pairs={{32,68},{33,69},{34,70},{35,71},{36,72},{37,73},{38,74},{39,75},{4... | collective-permute-start | bytes 98312 | tf_op jit(solution)/shard_map/ppermute | solution.py:45
  113.8 1.4 collective-permute-start.38
  114.5 0.7 collective-permute-start.39
  116.2 2.7 %collective-permute-start.40 = (bf16[8,2048]{1,0:T(8,128)(2,1)S(1)}, bf16[8,2048]{1,0:T(8,128)(2,1)S(1)}, u32[]{:S(2)}, u32[]{:S(2)}) collective-permute-start(bf16[8,2048]{1,0:T(8,128)(2,1)S(1)} %get-tuple-element.54), channel_id=1, source_target_pairs={{64,104},{65,105},{66,106},{67,107},{68,108},{69,109},{70,110},{71... | collective-permute-start | bytes 98312 | tf_op jit(solution)/shard_map/ppermute | solution.py:45
  116.9 2.0 %collective-permute-start.41 = (bf16[8,2048]{1,0:T(8,128)(2,1)S(1)}, bf16[8,2048]{1,0:T(8,128)(2,1)S(1)}, u32[]{:S(2)}, u32[]{:S(2)}) collective-permute-start(bf16[8,2048]{1,0:T(8,128)(2,1)S(1)} %get-tuple-element.54), channel_id=1, source_target_pairs={{64,100},{65,101},{66,102},{67,103},{68,104},{69,105},{70,106},{71... | collective-permute-start | bytes 98312 | tf_op jit(solution)/shard_map/ppermute | solution.py:45
  117.6 1.4 collective-permute-start.42
  118.2 0.7 collective-permute-start.43
  119.9 13.5 %collective-permute-start.44 = (bf16[8,2048]{1,0:T(8,128)(2,1)S(1)}, bf16[8,2048]{1,0:T(8,128)(2,1)S(1)}, u32[]{:S(2)}, u32[]{:S(2)}) collective-permute-start(bf16[8,2048]{1,0:T(8,128)(2,1)S(1)} %get-tuple-element.56), channel_id=1, source_target_pairs={{0,40},{1,41},{2,42},{3,43},{4,44},{5,45},{6,46},{7,47},{8,32},{9,... | collective-permute-start | bytes 98312 | tf_op jit(solution)/shard_map/ppermute | solution.py:45
  121.2 13.5 %collective-permute-start.45 = (bf16[8,2048]{1,0:T(8,128)(2,1)S(1)}, bf16[8,2048]{1,0:T(8,128)(2,1)S(1)}, u32[]{:S(2)}, u32[]{:S(2)}) collective-permute-start(bf16[8,2048]{1,0:T(8,128)(2,1)S(1)} %get-tuple-element.56), channel_id=1, source_target_pairs={{0,36},{1,37},{2,38},{3,39},{4,40},{5,41},{6,42},{7,43},{8,44},{9,... | collective-permute-start | bytes 98312 | tf_op jit(solution)/shard_map/ppermute | solution.py:45
  122.5 12.8 %collective-permute-start.46 = (bf16[8,2048]{1,0:T(8,128)(2,1)S(1)}, bf16[8,2048]{1,0:T(8,128)(2,1)S(1)}, u32[]{:S(2)}, u32[]{:S(2)}) collective-permute-start(bf16[8,2048]{1,0:T(8,128)(2,1)S(1)} %get-tuple-element.56), channel_id=1, source_target_pairs={{0,44},{1,45},{2,46},{3,47},{4,32},{5,33},{6,34},{7,35},{8,36},{9,... | collective-permute-start | bytes 98312 | tf_op jit(solution)/shard_map/ppermute | solution.py:45
  123.8 12.6 %collective-permute-start.47 = (bf16[8,2048]{1,0:T(8,128)(2,1)S(1)}, bf16[8,2048]{1,0:T(8,128)(2,1)S(1)}, u32[]{:S(2)}, u32[]{:S(2)}) collective-permute-start(bf16[8,2048]{1,0:T(8,128)(2,1)S(1)} %get-tuple-element.56), channel_id=1, source_target_pairs={{0,32},{1,33},{2,34},{3,35},{4,36},{5,37},{6,38},{7,39},{8,40},{9,... | collective-permute-start | bytes 98312 | tf_op jit(solution)/shard_map/ppermute | solution.py:45
  137.2 1.3 collective-permute-start.48

commit v4 on v3

--- a/solution.py
+++ b/solution.py
@@ -51,14 +51,17 @@
 
 
 def mask_kernel(coupling, pattern, *refs):
-    pieces, (masked, done) = refs[:SIDE], refs[SIDE:]
+    pieces, (masked, present_blocks, done) = refs[:SIDE], refs[SIDE:]
     rows, order = coupling.shape
-    fetch = pltpu.make_async_copy(coupling, masked, done)
+    fetch_blocks = pltpu.make_async_copy(pattern, present_blocks, done.at[1])
+    fetch_blocks.start()
+    fetch = pltpu.make_async_copy(coupling, masked, done.at[0])
     fetch.start()
     blocks = order // BLOCK
     column_block = lax.broadcasted_iota(jnp.int32, (blocks, order), 1) // BLOCK
     spread = (column_block == lax.broadcasted_iota(jnp.int32, (blocks, order), 0)).astype(jnp.bfloat16)
-    present = jnp.dot(pattern[...].astype(jnp.bfloat16), spread, preferred_element_type=jnp.float32)
+    fetch_blocks.wait()
+    present = jnp.dot(present_blocks[...].astype(jnp.bfloat16), spread, preferred_element_type=jnp.float32)
     fetch.wait()
     for at in range(rows // BLOCK):
         part = slice(at * BLOCK, (at + 1) * BLOCK)
@@ -74,11 +77,15 @@
     return pl.pallas_call(
         mask_kernel,
         out_shape=[pltpu.VMEM((rows, order // SIDE), jnp.bfloat16)] * SIDE,
-        in_specs=[pl.BlockSpec(memory_space=pltpu.HBM), WHOLE],
+        in_specs=[pl.BlockSpec(memory_space=pltpu.HBM)] * 2,
         out_specs=[WHOLE] * SIDE,
-        scratch_shapes=[pltpu.VMEM((rows, order), jnp.bfloat16), pltpu.SemaphoreType.DMA],
+        scratch_shapes=[
+            pltpu.VMEM((rows, order), jnp.bfloat16),
+            pltpu.VMEM(pattern.shape, jnp.int32),
+            pltpu.SemaphoreType.DMA((2,)),
+        ],
         compiler_params=pltpu.CompilerParams(vmem_limit_bytes=4 << 20),
-    )(far(coupling), pattern)
+    )(far(coupling), far(pattern))
 
 
 def tile_kernel(*refs):

time: 154 us -> 153 us (level)
  no operation moved by 1% of the time
where the time goes in v4:
time: 153 us
  waiting for transfers between devices  69.9 us (46%)
  starting transfers between devices  53.1 us (35%)
  blocking collectives  14.1 us (9%)
  Pallas kernels  12.5 us (8%)
  other arithmetic  2.16 us (1%)
    ppermute x49, waiting for transfers between devices, sent(): return lax.ppermute(value, ('dom', 'orb'), pairs)  69.9 us
    ppermute x49, starting transfers between devices, sent(): return lax.ppermute(value, ('dom', 'orb'), pairs)  53.1 us
    all_to_all x1, blocking collectives, on_device(): parts = lax.all_to_all(both, 'orb', 0, 0, tiled=True)  14.1 us
    pallas_call x8, Pallas kernels, through_plane(): pl.pallas_call(functools.partial(plane_kernel, at), out_shape=[pltpu.VMEM...  7.82 us
  transfers between devices with their start and end apart: 49, of which 24 were waited for; matrix products, arithmetic and copies ran while one was open for 1% of the time, Pallas kernels for 1%

profile of v4, /device:TPU:224, one launch (start us, length us, event | category | flops | bytes accessed | tf_op | source)
XLA Modules:
  0.0 152.6 jit_solution(10732838484974233534)
XLA Ops:
  0.0 1.2 shard_map.55
  1.2 1.6 %collective-permute-start.1 = (bf16[128,512]{1,0:T(8,128)(2,1)S(1)}, bf16[128,512]{1,0:T(8,128)(2,1)S(1)}, u32[]{:S(2)}, u32[]{:S(2)}) collective-permute-start(bf16[128,512]{1,0:T(8,128)(2,1)S(1)} %get-tuple-element.33), channel_id=1, source_target_pairs={{0,1},{1,2},{2,3},{3,0},{4,5},{5,6},{6,7},{7,4},{8,9},{9,10},{10,1... | collective-permute-start | bytes 393224 | tf_op jit(solution)/shard_map/ppermute | solution.py:45
  2.8 2.7 %collective-permute-start.2 = (bf16[128,512]{1,0:T(8,128)(2,1)S(1)}, bf16[128,512]{1,0:T(8,128)(2,1)S(1)}, u32[]{:S(2)}, u32[]{:S(2)}) collective-permute-start(bf16[128,512]{1,0:T(8,128)(2,1)S(1)} %get-tuple-element.34), channel_id=1, source_target_pairs={{0,2},{1,3},{2,0},{3,1},{4,6},{5,7},{6,4},{7,5},{8,10},{9,11},{10,... | collective-permute-start | bytes 393224 | tf_op jit(solution)/shard_map/ppermute | solution.py:45
  5.5 1.4 collective-permute-start.3
  7.5 2.4 %collective-permute-done.2 = bf16[128,512]{1,0:T(8,128)(2,1)S(1)} collective-permute-done((bf16[128,512]{1,0:T(8,128)(2,1)S(1)}, bf16[128,512]{1,0:T(8,128)(2,1)S(1)}, u32[]{:S(2)}, u32[]{:S(2)}) %collective-permute-start.2) | collective-permute-done | bytes 131104 | tf_op jit(solution)/shard_map/ppermute | solution.py:45
  10.5 1.7 %collective-permute-start.4 = (bf16[512,512]{1,0:T(8,128)(2,1)S(1)}, bf16[512,512]{1,0:T(8,128)(2,1)S(1)}, u32[]{:S(2)}, u32[]{:S(2)}) collective-permute-start(bf16[512,512]{1,0:T(8,128)(2,1)S(1)} %constant_dynamic-update-slice_fusion.refs_0_), channel_id=1, source_target_pairs={{0,4},{1,5},{2,6},{3,7},{4,8},{5,9},{6,10},{7,11},{8,12},{9,13},{1... | collective-permute-start | bytes 1572872 | tf_op jit(solution)/shard_map/ppermute | solution.py:45
  12.2 1.7 %collective-permute-start.5 = (bf16[512,512]{1,0:T(8,128)(2,1)S(1)}, bf16[512,512]{1,0:T(8,128)(2,1)S(1)}, u32[]{:S(2)}, u32[]{:S(2)}) collective-permute-start(bf16[512,512]{1,0:T(8,128)(2,1)S(1)} %constant_dynamic-update-slice_fusion.refs_0_), channel_id=1, source_target_pairs={{0,12},{1,13},{2,14},{3,15},{4,0},{5,1},{6,2},{7,3},{8,4},{9,5},{1... | collective-permute-start | bytes 1572872 | tf_op jit(solution)/shard_map/ppermute | solution.py:45
  13.8 0.8 dynamic-slice_select_fusion.refs_9_.state
  14.8 2.1 %collective-permute-start.9 = (bf16[512,512]{1,0:T(8,128)(2,1)S(1)}, bf16[512,512]{1,0:T(8,128)(2,1)S(1)}, u32[]{:S(2)}, u32[]{:S(2)}) collective-permute-start(bf16[512,512]{1,0:T(8,128)(2,1)S(1)} %constant_dynamic-update-slice_fusion.refs_0_), channel_id=1, source_target_pairs={{0,8},{1,9},{2,10},{3,11},{4,12},{5,13},{6,14},{7,15},{8,0},{9,1},... | collective-permute-start | bytes 1572872 | tf_op jit(solution)/shard_map/ppermute | solution.py:45
  16.8 1.3 collective-permute-start.10
  18.1 2.0 %collective-permute-start.11 = (bf16[128,2048]{1,0:T(8,128)(2,1)}, bf16[128,2048]{1,0:T(8,128)(2,1)S(1)}, u32[]{:S(2)}, u32[]{:S(2)}) collective-permute-start(bf16[128,2048]{1,0:T(8,128)(2,1)} %bitcast.28), channel_id=1, source_target_pairs={{0,3},{1,0},{2,1},{3,2},{4,7},{5,4},{6,5},{7,6},{8,11},{9,8},{10,9... | collective-permute-start | bytes 1572872 | tf_op jit(solution)/shard_map/ppermute | solution.py:45
  20.1 0.9 collective-permute-done.4.refs_1_
  21.0 2.9 %collective-permute-start.12 = (bf16[128,2048]{1,0:T(8,128)(2,1)}, bf16[128,2048]{1,0:T(8,128)(2,1)S(1)}, u32[]{:S(2)}, u32[]{:S(2)}) collective-permute-start(bf16[128,2048]{1,0:T(8,128)(2,1)} %bitcast.29), channel_id=1, source_target_pairs={{0,2},{1,3},{2,0},{3,1},{4,6},{5,7},{6,4},{7,5},{8,10},{9,11},{10,... | collective-permute-start | bytes 1572872 | tf_op jit(solution)/shard_map/ppermute | solution.py:45
  23.9 0.7 broadcast_select_fusion.5
  24.6 1.2 collective-permute-start.6
  25.8 9.0 %collective-permute-done.6 = bf16[16,128]{1,0:T(8,128)(2,1)S(1)} collective-permute-done((bf16[16,128]{1,0:T(8,128)(2,1)S(1)}, bf16[16,128]{1,0:T(8,128)(2,1)S(1)}, u32[]{:S(2)}, u32[]{:S(2)}) %collective-permute-start.6) | collective-permute-done | bytes 4128 | tf_op jit(solution)/shard_map/ppermute | solution.py:45
  34.8 1.4 collective-permute-start.7
  36.3 3.7 %collective-permute-done.7 = bf16[16,128]{1,0:T(8,128)(2,1)S(1)} collective-permute-done((bf16[16,128]{1,0:T(8,128)(2,1)S(1)}, bf16[16,128]{1,0:T(8,128)(2,1)S(1)}, u32[]{:S(2)}, u32[]{:S(2)}) %collective-permute-start.7) | collective-permute-done | bytes 4128 | tf_op jit(solution)/shard_map/ppermute | solution.py:45
  39.9 2.4 %collective-permute-start.8 = (bf16[16,128]{1,0:T(8,128)(2,1)S(1)}, bf16[16,128]{1,0:T(8,128)(2,1)S(1)}, u32[]{:S(2)}, u32[]{:S(2)}) collective-permute-start(bf16[16,128]{1,0:T(8,128)(2,1)S(1)} %get-tuple-element.61), channel_id=1, source_target_pairs={{0,3},{1,0},{2,1},{3,2},{4,7},{5,4},{6,5},{7,6},{8,11},{9,8},{10,9... | collective-permute-start | bytes 12296 | tf_op jit(solution)/shard_map/ppermute | solution.py:45
  42.3 1.6 %collective-permute-done.8 = bf16[16,128]{1,0:T(8,128)(2,1)S(1)} collective-permute-done((bf16[16,128]{1,0:T(8,128)(2,1)S(1)}, bf16[16,128]{1,0:T(8,128)(2,1)S(1)}, u32[]{:S(2)}, u32[]{:S(2)}) %collective-permute-start.8) | collective-permute-done | bytes 4128 | tf_op jit(solution)/shard_map/ppermute | solution.py:45
  44.1 1.5 shard_map.56.refs_0_
  45.6 2.1 %collective-permute-start.15 = (bf16[512,512]{1,0:T(8,128)(2,1)S(1)}, bf16[512,512]{1,0:T(8,128)(2,1)S(1)}, u32[]{:S(2)}, u32[]{:S(2)}) collective-permute-start(bf16[512,512]{1,0:T(8,128)(2,1)S(1)} %shard_map.56.refs_0_), channel_id=1, source_target_pairs={{0,1},{1,2},{2,3},{3,0},{4,5},{5,6},{6,7},{7,4},{8,9},{9,10},{10,1... | collective-permute-start | bytes 1572872 | tf_op jit(solution)/shard_map/ppermute | solution.py:45
  47.7 1.3 collective-permute-start.16
  48.9 1.4 collective-permute-start.13
  50.3 11.3 %collective-permute-done.15.refs_1_ = bf16[512,512]{1,0:T(8,128)(2,1)S(1)} collective-permute-done((bf16[512,512]{1,0:T(8,128)(2,1)S(1)}, bf16[512,512]{1,0:T(8,128)(2,1)S(1)}, u32[]{:S(2)}, u32[]{:S(2)}) %collective-permute-start.15) | collective-permute-done | bytes 524320 | tf_op jit(solution)/shard_map/ppermute | solution.py:45
  61.7 4.5 %collective-permute-done.16.refs_2_ = bf16[512,512]{1,0:T(8,128)(2,1)S(1)} collective-permute-done((bf16[512,512]{1,0:T(8,128)(2,1)S(1)}, bf16[512,512]{1,0:T(8,128)(2,1)S(1)}, u32[]{:S(2)}, u32[]{:S(2)}) %collective-permute-start.16) | collective-permute-done | bytes 524320 | tf_op jit(solution)/shard_map/ppermute | solution.py:45
  66.1 1.6 %collective-permute-done.13.refs_0_ = bf16[512,512]{1,0:T(8,128)(2,1)S(1)} collective-permute-done((bf16[512,512]{1,0:T(8,128)(2,1)S(1)}, bf16[512,512]{1,0:T(8,128)(2,1)S(1)}, u32[]{:S(2)}, u32[]{:S(2)}) %collective-permute-start.13) | collective-permute-done | bytes 524320 | tf_op jit(solution)/shard_map/ppermute | solution.py:45
  68.2 1.8 %shard_map.57 = (bf16[2048,512]{1,0:T(8,128)(2,1)S(1)}, bf16[512,2048]{1,0:T(8,128)(2,1)S(1)}) custom-call(bf16[512,512]{1,0:T(8,128)(2,1)S(1)} %shard_map.56.refs_0_, bf16[512,512]{1,0:T(8,128)(2,1)S(1)} %collective-permute-done.15.refs_1_, bf16[512,512]{1,0:T(8,128)(2,1)S(1)} %collective-permute-done.16.refs_2_, ...), custom_call_target="tpu_custom_call" | custom-call | tf_op jit(solution)/shard_map/pallas_call | solution.py:145
  70.2 1.0 shard_map.59
  71.2 1.3 collective-permute-start.20
  72.5 1.3 collective-permute-start.21
  73.8 1.3 collective-permute-start.22
  75.1 1.3 collective-permute-start.23
  76.4 3.0 %collective-permute-done.20.refs_0_ = bf16[8,2048]{1,0:T(8,128)(2,1)S(1)} collective-permute-done((bf16[8,2048]{1,0:T(8,128)(2,1)S(1)}, bf16[8,2048]{1,0:T(8,128)(2,1)S(1)}, u32[]{:S(2)}, u32[]{:S(2)}) %collective-permute-start.20) | collective-permute-done | bytes 32800 | tf_op jit(solution)/shard_map/ppermute | solution.py:45
  79.4 2.0 %collective-permute-done.21.refs_1_ = bf16[8,2048]{1,0:T(8,128)(2,1)S(1)} collective-permute-done((bf16[8,2048]{1,0:T(8,128)(2,1)S(1)}, bf16[8,2048]{1,0:T(8,128)(2,1)S(1)}, u32[]{:S(2)}, u32[]{:S(2)}) %collective-permute-start.21) | collective-permute-done | bytes 32800 | tf_op jit(solution)/shard_map/ppermute | solution.py:45
  81.4 1.0 collective-permute-done.23.refs_3_
  82.5 1.0 shard_map.60
  84.1 0.7 collective-permute-start.25
  84.8 0.7 collective-permute-start.26
  85.5 0.7 collective-permute-start.27
  86.2 1.0 shard_map.61
  87.8 0.7 collective-permute-start.29
  89.9 1.0 shard_map.62
  90.9 1.3 collective-permute-start.32
  92.2 1.3 collective-permute-start.33
  93.5 1.3 collective-permute-start.34
  94.8 1.3 collective-permute-start.35
  96.1 12.6 %collective-permute-done.32.refs_0_ = bf16[8,2048]{1,0:T(8,128)(2,1)S(1)} collective-permute-done((bf16[8,2048]{1,0:T(8,128)(2,1)S(1)}, bf16[8,2048]{1,0:T(8,128)(2,1)S(1)}, u32[]{:S(2)}, u32[]{:S(2)}) %collective-permute-start.32) | collective-permute-done | bytes 32800 | tf_op jit(solution)/shard_map/ppermute | solution.py:45
  108.7 1.0 collective-permute-done.33.refs_1_
  109.9 1.0 collective-permute-done.35.refs_3_
  110.9 1.0 shard_map.63
  114.6 1.0 shard_map.64
  118.3 1.0 shard_map.65
  119.3 1.3 collective-permute-start.44
  120.6 1.3 collective-permute-start.45
  121.9 1.3 collective-permute-start.46
  123.2 1.3 collective-permute-start.47
  124.5 8.3 %collective-permute-done.44.refs_0_ = bf16[8,2048]{1,0:T(8,128)(2,1)S(1)} collective-permute-done((bf16[8,2048]{1,0:T(8,128)(2,1)S(1)}, bf16[8,2048]{1,0:T(8,128)(2,1)S(1)}, u32[]{:S(2)}, u32[]{:S(2)}) %collective-permute-start.44) | collective-permute-done | bytes 32800 | tf_op jit(solution)/shard_map/ppermute | solution.py:45
  132.7 1.3 collective-permute-done.45.refs_1_
  134.0 0.7 collective-permute-done.46.refs_2_
  134.7 1.0 collective-permute-done.47.refs_3_
  135.7 0.8 shard_map.66
  136.7 1.2 collective-permute-done.48
  137.9 14.1 %all_to_all.5 = bf16[16,16,128]{2,1,0:T(8,128)(2,1)S(1)} all-to-all(bf16[16,16,128]{2,1,0:T(8,128)(2,1)S(1)} %bitcast_bitcast_fusion), channel_id=1, replica_groups=mesh['dom'=16,'orb'=16] {'orb'}, dimensions={0} | all-to-all | bytes 131072 | tf_op jit(solution)/shard_map/all_to_all | solution.py:242
  (71 shorter events, 10.8 us)
Async XLA Ops:
  0.0 44.1 %copy-start = (bf16[1,128,2048]{2,1,0:T(8,128)(2,1)S(1)}, bf16[1,128,2048]{2,1,0:T(8,128)(2,1)}, u32[]{:S(2)}) copy-start(bf16[1,128,2048]{2,1,0:T(8,128)(2,1)} %param.5) | copy-start | bytes 1572868
  1.2 6.3 %collective-permute-start.1 = (bf16[128,512]{1,0:T(8,128)(2,1)S(1)}, bf16[128,512]{1,0:T(8,128)(2,1)S(1)}, u32[]{:S(2)}, u32[]{:S(2)}) collective-permute-start(bf16[128,512]{1,0:T(8,128)(2,1)S(1)} %get-tuple-element.33), channel_id=1, source_target_pairs={{0,1},{1,2},{2,3},{3,0},{4,5},{5,6},{6,7},{7,4},{8,9},{9,10},{10,1... | collective-permute-start | bytes 393224 | tf_op jit(solution)/shard_map/ppermute | solution.py:45
  2.8 7.1 %collective-permute-start.2 = (bf16[128,512]{1,0:T(8,128)(2,1)S(1)}, bf16[128,512]{1,0:T(8,128)(2,1)S(1)}, u32[]{:S(2)}, u32[]{:S(2)}) collective-permute-start(bf16[128,512]{1,0:T(8,128)(2,1)S(1)} %get-tuple-element.34), channel_id=1, source_target_pairs={{0,2},{1,3},{2,0},{3,1},{4,6},{5,7},{6,4},{7,5},{8,10},{9,11},{10,... | collective-permute-start | bytes 393224 | tf_op jit(solution)/shard_map/ppermute | solution.py:45
  5.5 5.0 %collective-permute-start.3 = (bf16[128,512]{1,0:T(8,128)(2,1)S(1)}, bf16[128,512]{1,0:T(8,128)(2,1)S(1)}, u32[]{:S(2)}, u32[]{:S(2)}) collective-permute-start(bf16[128,512]{1,0:T(8,128)(2,1)S(1)} %get-tuple-element.35), channel_id=1, source_target_pairs={{0,3},{1,0},{2,1},{3,2},{4,7},{5,4},{6,5},{7,6},{8,11},{9,8},{10,9... | collective-permute-start | bytes 393224 | tf_op jit(solution)/shard_map/ppermute | solution.py:45
  10.5 10.5 %collective-permute-start.4 = (bf16[512,512]{1,0:T(8,128)(2,1)S(1)}, bf16[512,512]{1,0:T(8,128)(2,1)S(1)}, u32[]{:S(2)}, u32[]{:S(2)}) collective-permute-start(bf16[512,512]{1,0:T(8,128)(2,1)S(1)} %constant_dynamic-update-slice_fusion.refs_0_), channel_id=1, source_target_pairs={{0,4},{1,5},{2,6},{3,7},{4,8},{5,9},{6,10},{7,11},{8,12},{9,13},{1... | collective-permute-start | bytes 1572872 | tf_op jit(solution)/shard_map/ppermute | solution.py:45
  12.2 11.7 %collective-permute-start.5 = (bf16[512,512]{1,0:T(8,128)(2,1)S(1)}, bf16[512,512]{1,0:T(8,128)(2,1)S(1)}, u32[]{:S(2)}, u32[]{:S(2)}) collective-permute-start(bf16[512,512]{1,0:T(8,128)(2,1)S(1)} %constant_dynamic-update-slice_fusion.refs_0_), channel_id=1, source_target_pairs={{0,12},{1,13},{2,14},{3,15},{4,0},{5,1},{6,2},{7,3},{8,4},{9,5},{1... | collective-permute-start | bytes 1572872 | tf_op jit(solution)/shard_map/ppermute | solution.py:45
  13.8 4.3 %collective-permute-start = (bf16[64,128]{1,0:T(8,128)(2,1)}, bf16[64,128]{1,0:T(8,128)(2,1)S(1)}, u32[]{:S(2)}, u32[]{:S(2)}) collective-permute-start(bf16[64,128]{1,0:T(8,128)(2,1)} %bitcast.37), channel_id=1, source_target_pairs={{0,16},{1,17},{2,18},{3,19},{4,20},{5,21},{6,22},{7,23},{8,24},{9,... | collective-permute-start | bytes 49160 | tf_op jit(solution)/shard_map/ppermute | solution.py:45
  14.8 29.2 %collective-permute-start.9 = (bf16[512,512]{1,0:T(8,128)(2,1)S(1)}, bf16[512,512]{1,0:T(8,128)(2,1)S(1)}, u32[]{:S(2)}, u32[]{:S(2)}) collective-permute-start(bf16[512,512]{1,0:T(8,128)(2,1)S(1)} %constant_dynamic-update-slice_fusion.refs_0_), channel_id=1, source_target_pairs={{0,8},{1,9},{2,10},{3,11},{4,12},{5,13},{6,14},{7,15},{8,0},{9,1},... | collective-permute-start | bytes 1572872 | tf_op jit(solution)/shard_map/ppermute | solution.py:45
  16.8 27.1 %collective-permute-start.10 = (bf16[128,2048]{1,0:T(8,128)(2,1)}, bf16[128,2048]{1,0:T(8,128)(2,1)S(1)}, u32[]{:S(2)}, u32[]{:S(2)}) collective-permute-start(bf16[128,2048]{1,0:T(8,128)(2,1)} %bitcast.27), channel_id=1, source_target_pairs={{0,1},{1,2},{2,3},{3,0},{4,5},{5,6},{6,7},{7,4},{8,9},{9,10},{10,1... | collective-permute-start | bytes 1572872 | tf_op jit(solution)/shard_map/ppermute | solution.py:45
  18.1 25.9 %collective-permute-start.11 = (bf16[128,2048]{1,0:T(8,128)(2,1)}, bf16[128,2048]{1,0:T(8,128)(2,1)S(1)}, u32[]{:S(2)}, u32[]{:S(2)}) collective-permute-start(bf16[128,2048]{1,0:T(8,128)(2,1)} %bitcast.28), channel_id=1, source_target_pairs={{0,3},{1,0},{2,1},{3,2},{4,7},{5,4},{6,5},{7,6},{8,11},{9,8},{10,9... | collective-permute-start | bytes 1572872 | tf_op jit(solution)/shard_map/ppermute | solution.py:45
  21.0 23.0 %collective-permute-start.12 = (bf16[128,2048]{1,0:T(8,128)(2,1)}, bf16[128,2048]{1,0:T(8,128)(2,1)S(1)}, u32[]{:S(2)}, u32[]{:S(2)}) collective-permute-start(bf16[128,2048]{1,0:T(8,128)(2,1)} %bitcast.29), channel_id=1, source_target_pairs={{0,2},{1,3},{2,0},{3,1},{4,6},{5,7},{6,4},{7,5},{8,10},{9,11},{10,... | collective-permute-start | bytes 1572872 | tf_op jit(solution)/shard_map/ppermute | solution.py:45
  24.6 10.2 %collective-permute-start.6 = (bf16[16,128]{1,0:T(8,128)(2,1)S(1)}, bf16[16,128]{1,0:T(8,128)(2,1)S(1)}, u32[]{:S(2)}, u32[]{:S(2)}) collective-permute-start(bf16[16,128]{1,0:T(8,128)(2,1)S(1)} %get-tuple-element.62), channel_id=1, source_target_pairs={{0,1},{1,2},{2,3},{3,0},{4,5},{5,6},{6,7},{7,4},{8,9},{9,10},{10,1... | collective-permute-start | bytes 12296 | tf_op jit(solution)/shard_map/ppermute | solution.py:45
  34.8 5.1 %collective-permute-start.7 = (bf16[16,128]{1,0:T(8,128)(2,1)S(1)}, bf16[16,128]{1,0:T(8,128)(2,1)S(1)}, u32[]{:S(2)}, u32[]{:S(2)}) collective-permute-start(bf16[16,128]{1,0:T(8,128)(2,1)S(1)} %get-tuple-element.63), channel_id=1, source_target_pairs={{0,2},{1,3},{2,0},{3,1},{4,6},{5,7},{6,4},{7,5},{8,10},{9,11},{10,... | collective-permute-start | bytes 12296 | tf_op jit(solution)/shard_map/ppermute | solution.py:45
  39.9 4.0 %collective-permute-start.8 = (bf16[16,128]{1,0:T(8,128)(2,1)S(1)}, bf16[16,128]{1,0:T(8,128)(2,1)S(1)}, u32[]{:S(2)}, u32[]{:S(2)}) collective-permute-start(bf16[16,128]{1,0:T(8,128)(2,1)S(1)} %get-tuple-element.61), channel_id=1, source_target_pairs={{0,3},{1,0},{2,1},{3,2},{4,7},{5,4},{6,5},{7,6},{8,11},{9,8},{10,9... | collective-permute-start | bytes 12296 | tf_op jit(solution)/shard_map/ppermute | solution.py:45
  45.6 16.1 %collective-permute-start.15 = (bf16[512,512]{1,0:T(8,128)(2,1)S(1)}, bf16[512,512]{1,0:T(8,128)(2,1)S(1)}, u32[]{:S(2)}, u32[]{:S(2)}) collective-permute-start(bf16[512,512]{1,0:T(8,128)(2,1)S(1)} %shard_map.56.refs_0_), channel_id=1, source_target_pairs={{0,1},{1,2},{2,3},{3,0},{4,5},{5,6},{6,7},{7,4},{8,9},{9,10},{10,1... | collective-permute-start | bytes 1572872 | tf_op jit(solution)/shard_map/ppermute | solution.py:45
  47.7 18.5 %collective-permute-start.16 = (bf16[512,512]{1,0:T(8,128)(2,1)S(1)}, bf16[512,512]{1,0:T(8,128)(2,1)S(1)}, u32[]{:S(2)}, u32[]{:S(2)}) collective-permute-start(bf16[512,512]{1,0:T(8,128)(2,1)S(1)} %shard_map.56.refs_0_), channel_id=1, source_target_pairs={{0,3},{1,0},{2,1},{3,2},{4,7},{5,4},{6,5},{7,6},{8,11},{9,8},{10,9... | collective-permute-start | bytes 1572872 | tf_op jit(solution)/shard_map/ppermute | solution.py:45
  48.9 18.8 %collective-permute-start.13 = (bf16[512,512]{1,0:T(8,128)(2,1)S(1)}, bf16[512,512]{1,0:T(8,128)(2,1)S(1)}, u32[]{:S(2)}, u32[]{:S(2)}) collective-permute-start(bf16[512,512]{1,0:T(8,128)(2,1)S(1)} %shard_map.56.refs_0_), channel_id=1, source_target_pairs={{0,2},{1,3},{2,0},{3,1},{4,6},{5,7},{6,4},{7,5},{8,10},{9,11},{10,... | collective-permute-start | bytes 1572872 | tf_op jit(solution)/shard_map/ppermute | solution.py:45
  50.3 17.5 %collective-permute-start.17 = (bf16[512,512]{1,0:T(8,128)(2,1)S(1)}, bf16[512,512]{1,0:T(8,128)(2,1)S(1)}, u32[]{:S(2)}, u32[]{:S(2)}) collective-permute-start(bf16[512,512]{1,0:T(8,128)(2,1)S(1)} %shard_map.56.refs_0_), channel_id=1, source_target_pairs={{0,16},{1,17},{2,18},{3,19},{4,20},{5,21},{6,22},{7,23},{8,24},{9,... | collective-permute-start | bytes 1572872 | tf_op jit(solution)/shard_map/ppermute | solution.py:45
  61.7 6.1 %collective-permute-start.18 = (bf16[512,512]{1,0:T(8,128)(2,1)S(1)}, bf16[512,512]{1,0:T(8,128)(2,1)}, u32[]{:S(2)}, u32[]{:S(2)}) collective-permute-start(bf16[512,512]{1,0:T(8,128)(2,1)S(1)} %collective-permute-done.15.refs_1_), channel_id=1, source_target_pairs={{0,16},{1,17},{2,18},{3,19},{4,20},{5,21},{6,22},{7,23},{8,24},{9,... | collective-permute-start | bytes 1572872 | tf_op jit(solution)/shard_map/ppermute | solution.py:45
  66.1 2.0 %collective-permute-start.19 = (bf16[512,512]{1,0:T(8,128)(2,1)S(1)}, bf16[512,512]{1,0:T(8,128)(2,1)}, u32[]{:S(2)}, u32[]{:S(2)}) collective-permute-start(bf16[512,512]{1,0:T(8,128)(2,1)S(1)} %collective-permute-done.16.refs_2_), channel_id=1, source_target_pairs={{0,16},{1,17},{2,18},{3,19},{4,20},{5,21},{6,22},{7,23},{8,24},{9,... | collective-permute-start | bytes 1572872 | tf_op jit(solution)/shard_map/ppermute | solution.py:45
  67.8 2.2 %collective-permute-start.14 = (bf16[512,512]{1,0:T(8,128)(2,1)S(1)}, bf16[512,512]{1,0:T(8,128)(2,1)S(1)}, u32[]{:S(2)}, u32[]{:S(2)}) collective-permute-start(bf16[512,512]{1,0:T(8,128)(2,1)S(1)} %collective-permute-done.13.refs_0_), channel_id=1, source_target_pairs={{0,16},{1,17},{2,18},{3,19},{4,20},{5,21},{6,22},{7,23},{8,24},{9,... | collective-permute-start | bytes 1572872 | tf_op jit(solution)/shard_map/ppermute | solution.py:45
  71.2 8.2 %collective-permute-start.20 = (bf16[8,2048]{1,0:T(8,128)(2,1)S(1)}, bf16[8,2048]{1,0:T(8,128)(2,1)S(1)}, u32[]{:S(2)}, u32[]{:S(2)}) collective-permute-start(bf16[8,2048]{1,0:T(8,128)(2,1)S(1)} %get-tuple-element.44), channel_id=1, source_target_pairs={{0,40},{1,41},{2,42},{3,43},{4,44},{5,45},{6,46},{7,47},{8,32},{9,... | collective-permute-start | bytes 98312 | tf_op jit(solution)/shard_map/ppermute | solution.py:45
  72.5 8.9 %collective-permute-start.21 = (bf16[8,2048]{1,0:T(8,128)(2,1)S(1)}, bf16[8,2048]{1,0:T(8,128)(2,1)S(1)}, u32[]{:S(2)}, u32[]{:S(2)}) collective-permute-start(bf16[8,2048]{1,0:T(8,128)(2,1)S(1)} %get-tuple-element.44), channel_id=1, source_target_pairs={{0,36},{1,37},{2,38},{3,39},{4,40},{5,41},{6,42},{7,43},{8,44},{9,... | collective-permute-start | bytes 98312 | tf_op jit(solution)/shard_map/ppermute | solution.py:45
  73.8 7.7 %collective-permute-start.22 = (bf16[8,2048]{1,0:T(8,128)(2,1)S(1)}, bf16[8,2048]{1,0:T(8,128)(2,1)S(1)}, u32[]{:S(2)}, u32[]{:S(2)}) collective-permute-start(bf16[8,2048]{1,0:T(8,128)(2,1)S(1)} %get-tuple-element.44), channel_id=1, source_target_pairs={{0,44},{1,45},{2,46},{3,47},{4,32},{5,33},{6,34},{7,35},{8,36},{9,... | collective-permute-start | bytes 98312 | tf_op jit(solution)/shard_map/ppermute | solution.py:45
  75.1 7.4 %collective-permute-start.23 = (bf16[8,2048]{1,0:T(8,128)(2,1)S(1)}, bf16[8,2048]{1,0:T(8,128)(2,1)S(1)}, u32[]{:S(2)}, u32[]{:S(2)}) collective-permute-start(bf16[8,2048]{1,0:T(8,128)(2,1)S(1)} %get-tuple-element.44), channel_id=1, source_target_pairs={{0,32},{1,33},{2,34},{3,35},{4,36},{5,37},{6,38},{7,39},{8,40},{9,... | collective-permute-start | bytes 98312 | tf_op jit(solution)/shard_map/ppermute | solution.py:45
  83.5 2.7 %collective-permute-start.24 = (bf16[8,2048]{1,0:T(8,128)(2,1)S(1)}, bf16[8,2048]{1,0:T(8,128)(2,1)S(1)}, u32[]{:S(2)}, u32[]{:S(2)}) collective-permute-start(bf16[8,2048]{1,0:T(8,128)(2,1)S(1)} %get-tuple-element.46), channel_id=1, source_target_pairs={{32,72},{33,73},{34,74},{35,75},{36,76},{37,77},{38,78},{39,79},{4... | collective-permute-start | bytes 98312 | tf_op jit(solution)/shard_map/ppermute | solution.py:45
  84.1 2.0 %collective-permute-start.25 = (bf16[8,2048]{1,0:T(8,128)(2,1)S(1)}, bf16[8,2048]{1,0:T(8,128)(2,1)S(1)}, u32[]{:S(2)}, u32[]{:S(2)}) collective-permute-start(bf16[8,2048]{1,0:T(8,128)(2,1)S(1)} %get-tuple-element.46), channel_id=1, source_target_pairs={{32,68},{33,69},{34,70},{35,71},{36,72},{37,73},{38,74},{39,75},{4... | collective-permute-start | bytes 98312 | tf_op jit(solution)/shard_map/ppermute | solution.py:45
  84.8 1.4 collective-permute-start.26
  85.5 0.7 collective-permute-start.27
  87.2 2.7 %collective-permute-start.28 = (bf16[8,2048]{1,0:T(8,128)(2,1)S(1)}, bf16[8,2048]{1,0:T(8,128)(2,1)S(1)}, u32[]{:S(2)}, u32[]{:S(2)}) collective-permute-start(bf16[8,2048]{1,0:T(8,128)(2,1)S(1)} %get-tuple-element.48), channel_id=1, source_target_pairs={{64,104},{65,105},{66,106},{67,107},{68,108},{69,109},{70,110},{71... | collective-permute-start | bytes 98312 | tf_op jit(solution)/shard_map/ppermute | solution.py:45
  87.8 2.0 %collective-permute-start.29 = (bf16[8,2048]{1,0:T(8,128)(2,1)S(1)}, bf16[8,2048]{1,0:T(8,128)(2,1)S(1)}, u32[]{:S(2)}, u32[]{:S(2)}) collective-permute-start(bf16[8,2048]{1,0:T(8,128)(2,1)S(1)} %get-tuple-element.48), channel_id=1, source_target_pairs={{64,100},{65,101},{66,102},{67,103},{68,104},{69,105},{70,106},{71... | collective-permute-start | bytes 98312 | tf_op jit(solution)/shard_map/ppermute | solution.py:45
  88.5 1.4 collective-permute-start.30
  89.2 0.7 collective-permute-start.31
  90.9 17.8 %collective-permute-start.32 = (bf16[8,2048]{1,0:T(8,128)(2,1)S(1)}, bf16[8,2048]{1,0:T(8,128)(2,1)S(1)}, u32[]{:S(2)}, u32[]{:S(2)}) collective-permute-start(bf16[8,2048]{1,0:T(8,128)(2,1)S(1)} %get-tuple-element.50), channel_id=1, source_target_pairs={{0,40},{1,41},{2,42},{3,43},{4,44},{5,45},{6,46},{7,47},{8,32},{9,... | collective-permute-start | bytes 98312 | tf_op jit(solution)/shard_map/ppermute | solution.py:45
  92.2 17.6 %collective-permute-start.33 = (bf16[8,2048]{1,0:T(8,128)(2,1)S(1)}, bf16[8,2048]{1,0:T(8,128)(2,1)S(1)}, u32[]{:S(2)}, u32[]{:S(2)}) collective-permute-start(bf16[8,2048]{1,0:T(8,128)(2,1)S(1)} %get-tuple-element.50), channel_id=1, source_target_pairs={{0,36},{1,37},{2,38},{3,39},{4,40},{5,41},{6,42},{7,43},{8,44},{9,... | collective-permute-start | bytes 98312 | tf_op jit(solution)/shard_map/ppermute | solution.py:45
  93.5 16.4 %collective-permute-start.34 = (bf16[8,2048]{1,0:T(8,128)(2,1)S(1)}, bf16[8,2048]{1,0:T(8,128)(2,1)S(1)}, u32[]{:S(2)}, u32[]{:S(2)}) collective-permute-start(bf16[8,2048]{1,0:T(8,128)(2,1)S(1)} %get-tuple-element.50), channel_id=1, source_target_pairs={{0,44},{1,45},{2,46},{3,47},{4,32},{5,33},{6,34},{7,35},{8,36},{9,... | collective-permute-start | bytes 98312 | tf_op jit(solution)/shard_map/ppermute | solution.py:45
  94.8 16.1 %collective-permute-start.35 = (bf16[8,2048]{1,0:T(8,128)(2,1)S(1)}, bf16[8,2048]{1,0:T(8,128)(2,1)S(1)}, u32[]{:S(2)}, u32[]{:S(2)}) collective-permute-start(bf16[8,2048]{1,0:T(8,128)(2,1)S(1)} %get-tuple-element.50), channel_id=1, source_target_pairs={{0,32},{1,33},{2,34},{3,35},{4,36},{5,37},{6,38},{7,39},{8,40},{9,... | collective-permute-start | bytes 98312 | tf_op jit(solution)/shard_map/ppermute | solution.py:45
  111.9 2.7 %collective-permute-start.36 = (bf16[8,2048]{1,0:T(8,128)(2,1)S(1)}, bf16[8,2048]{1,0:T(8,128)(2,1)S(1)}, u32[]{:S(2)}, u32[]{:S(2)}) collective-permute-start(bf16[8,2048]{1,0:T(8,128)(2,1)S(1)} %get-tuple-element.52), channel_id=1, source_target_pairs={{32,72},{33,73},{34,74},{35,75},{36,76},{37,77},{38,78},{39,79},{4... | collective-permute-start | bytes 98312 | tf_op jit(solution)/shard_map/ppermute | solution.py:45
  112.5 2.0 %collective-permute-start.37 = (bf16[8,2048]{1,0:T(8,128)(2,1)S(1)}, bf16[8,2048]{1,0:T(8,128)(2,1)S(1)}, u32[]{:S(2)}, u32[]{:S(2)}) collective-permute-start(bf16[8,2048]{1,0:T(8,128)(2,1)S(1)} %get-tuple-element.52), channel_id=1, source_target_pairs={{32,68},{33,69},{34,70},{35,71},{36,72},{37,73},{38,74},{39,75},{4... | collective-permute-start | bytes 98312 | tf_op jit(solution)/shard_map/ppermute | solution.py:45
  113.2 1.4 collective-permute-start.38
  113.9 0.7 collective-permute-start.39
  115.6 2.7 %collective-permute-start.40 = (bf16[8,2048]{1,0:T(8,128)(2,1)S(1)}, bf16[8,2048]{1,0:T(8,128)(2,1)S(1)}, u32[]{:S(2)}, u32[]{:S(2)}) collective-permute-start(bf16[8,2048]{1,0:T(8,128)(2,1)S(1)} %get-tuple-element.54), channel_id=1, source_target_pairs={{64,104},{65,105},{66,106},{67,107},{68,108},{69,109},{70,110},{71... | collective-permute-start | bytes 98312 | tf_op jit(solution)/shard_map/ppermute | solution.py:45
  116.2 2.0 %collective-permute-start.41 = (bf16[8,2048]{1,0:T(8,128)(2,1)S(1)}, bf16[8,2048]{1,0:T(8,128)(2,1)S(1)}, u32[]{:S(2)}, u32[]{:S(2)}) collective-permute-start(bf16[8,2048]{1,0:T(8,128)(2,1)S(1)} %get-tuple-element.54), channel_id=1, source_target_pairs={{64,100},{65,101},{66,102},{67,103},{68,104},{69,105},{70,106},{71... | collective-permute-start | bytes 98312 | tf_op jit(solution)/shard_map/ppermute | solution.py:45
  116.9 1.4 collective-permute-start.42
  117.6 0.7 collective-permute-start.43
  119.3 13.5 %collective-permute-start.44 = (bf16[8,2048]{1,0:T(8,128)(2,1)S(1)}, bf16[8,2048]{1,0:T(8,128)(2,1)S(1)}, u32[]{:S(2)}, u32[]{:S(2)}) collective-permute-start(bf16[8,2048]{1,0:T(8,128)(2,1)S(1)} %get-tuple-element.56), channel_id=1, source_target_pairs={{0,40},{1,41},{2,42},{3,43},{4,44},{5,45},{6,46},{7,47},{8,32},{9,... | collective-permute-start | bytes 98312 | tf_op jit(solution)/shard_map/ppermute | solution.py:45
  120.6 13.5 %collective-permute-start.45 = (bf16[8,2048]{1,0:T(8,128)(2,1)S(1)}, bf16[8,2048]{1,0:T(8,128)(2,1)S(1)}, u32[]{:S(2)}, u32[]{:S(2)}) collective-permute-start(bf16[8,2048]{1,0:T(8,128)(2,1)S(1)} %get-tuple-element.56), channel_id=1, source_target_pairs={{0,36},{1,37},{2,38},{3,39},{4,40},{5,41},{6,42},{7,43},{8,44},{9,... | collective-permute-start | bytes 98312 | tf_op jit(solution)/shard_map/ppermute | solution.py:45
  121.9 12.8 %collective-permute-start.46 = (bf16[8,2048]{1,0:T(8,128)(2,1)S(1)}, bf16[8,2048]{1,0:T(8,128)(2,1)S(1)}, u32[]{:S(2)}, u32[]{:S(2)}) collective-permute-start(bf16[8,2048]{1,0:T(8,128)(2,1)S(1)} %get-tuple-element.56), channel_id=1, source_target_pairs={{0,44},{1,45},{2,46},{3,47},{4,32},{5,33},{6,34},{7,35},{8,36},{9,... | collective-permute-start | bytes 98312 | tf_op jit(solution)/shard_map/ppermute | solution.py:45
  123.2 12.6 %collective-permute-start.47 = (bf16[8,2048]{1,0:T(8,128)(2,1)S(1)}, bf16[8,2048]{1,0:T(8,128)(2,1)S(1)}, u32[]{:S(2)}, u32[]{:S(2)}) collective-permute-start(bf16[8,2048]{1,0:T(8,128)(2,1)S(1)} %get-tuple-element.56), channel_id=1, source_target_pairs={{0,32},{1,33},{2,34},{3,35},{4,36},{5,37},{6,38},{7,39},{8,40},{9,... | collective-permute-start | bytes 98312 | tf_op jit(solution)/shard_map/ppermute | solution.py:45
  136.6 1.3 collective-permute-start.48
